TPU v7x, 128 devices: a whole 4x4x4 slice. The times are simulated.
128 devices in a mesh: aa: 4 (over z_hi, core), ba: 32 (over y, z_lo, x).
Axes of the slice: x: 4, y: 4, z: 4 (z_hi: 2, z_lo: 2; z = z_hi * 2 + z_lo), core: 2. Of those that a mesh axis runs over, the one named last changes fastest.
Arguments:
- source_feats: bfloat16 [4, 10, 1024], P('aa'), may hold values from -4 to 4
- target_feats: bfloat16 [256, 512, 1024], P('ba'), may hold values from -4 to 4
- first_kernel: bfloat16 [16, 1, 3, 3, 3, 3], replicated, may hold values from -0.625 to 0.625
- first_bias: float32 [16], replicated, may hold values from -3 to 3
- second_kernel: bfloat16 [1, 16, 3, 3, 3, 3], replicated, may hold values from -0.15625 to 0.15625
- second_bias: float32 [1], replicated, may hold values from -1 to 1
Outputs:
- matches: float32 [4, 10, 256, 512], P('aa', None, 'ba')
All inputs are finite; a program needn't handle non-finite values.
Results may differ from a plain program's by a relative error of at most 0.0059.
Values may be sent and summed in bfloat16 or wider, within the bound.
No kernel may reach another device: no remote copies, remote signals or barrier semaphores. Data moves between devices by JAX's collectives and lax.ppermute only.
A program may use at most 192 MiB of HBM per device.

v0:
```python
import jax
import jax.numpy as jnp
from jax import lax
from jax.sharding import PartitionSpec as P

C = 1024


eps = 1e-05


def padded(shard, sides, width):
    for axis, dim in sides:
        size, length = (lax.axis_size(axis), shard.shape[dim])
        up = [(i, (i + 1) % size) for i in range(size - 1)]
        down = [(j, i) for i, j in up]
        last = lax.slice_in_dim(shard, length - width, length, axis=dim)
        leading = lax.slice_in_dim(shard, 0, width, axis=dim)
        before = lax.ppermute(last, axis, up)
        after = lax.ppermute(leading, axis, down)
        shard = jnp.concatenate([before, shard, after], axis=dim)
    return shard


def stencil(volume, kernel, offset):
    rows_a = volume.shape[0] - 2
    cols_a = volume.shape[1] - 2
    chan_in = volume.shape[2]
    rows_b = volume.shape[3] - 2
    cols_b = volume.shape[4] - 2
    chan_out = kernel.shape[0]
    running_sum = jnp.zeros((rows_a * cols_a, chan_out, rows_b, cols_b), jnp.float32)
    for shift_a in range(3):
        stacked = jnp.concatenate(
            [
                volume[shift_a : shift_a + rows_a, shift_c : shift_c + cols_a]
                for shift_c in range(3)
            ],
            axis=2,
        )
        stacked = stacked.reshape(rows_a * cols_a, 3 * chan_in, rows_b + 2, cols_b + 2)
        taps = jnp.transpose(kernel[:, :, shift_a], (0, 2, 1, 3, 4)).reshape(
            chan_out, 3 * chan_in, 3, 3
        )
        running_sum = running_sum + lax.conv_general_dilated(
            stacked,
            taps,
            (1, 1),
            "VALID",
            dimension_numbers=("NCHW", "OIHW", "NCHW"),
            preferred_element_type=jnp.float32,
        )
    return (
        running_sum.reshape(rows_a, cols_a, chan_out, rows_b, cols_b)
        + offset[None, None, :, None, None]
    )


def pad_sides(volume):
    return jnp.pad(volume, ((0, 0), (1, 1), (0, 0), (0, 0), (1, 1)))


def correlate(source_rows, target_rows):
    channels = source_rows.shape[-1]
    product = jnp.einsum(
        "ac,bc->ab",
        source_rows.reshape(-1, channels),
        target_rows.reshape(-1, channels),
        preferred_element_type=jnp.float32,
    )
    product = (product * C ** (-0.5)).astype(jnp.bfloat16)
    return product.reshape(
        source_rows.shape[0], source_rows.shape[1], 1, target_rows.shape[0], target_rows.shape[1]
    )


def per_device(source_feats, target_feats, first_kernel, first_bias, second_kernel, second_bias):
    own_rows = source_feats.shape[0]
    whole_slab = lax.all_gather(source_feats, "aa", axis=0, tiled=True)
    slab_count = whole_slab.shape[0]
    first_row = lax.axis_index("aa") * own_rows
    near_rows = lax.dynamic_slice_in_dim(
        jnp.pad(whole_slab, ((2, 2), (0, 0), (0, 0))), first_row, own_rows + 4, 0
    )
    row_ids = first_row - 1 + jnp.arange(own_rows + 2, dtype=jnp.int32)
    keep_rows = ((row_ids >= 0) & (row_ids < slab_count)).astype(jnp.float32)[
        :, None, None, None, None
    ]
    correlation = correlate(near_rows, target_feats)
    correlation = padded(correlation, (("ba", 3),), 1)
    pre = stencil(pad_sides(correlation), first_kernel, first_bias)
    hidden = (jnp.maximum(pre, 0.0) * keep_rows).astype(jnp.bfloat16)
    hidden = padded(hidden, (("ba", 3),), 1)
    logits = stencil(pad_sides(hidden), second_kernel, second_bias)
    scores = jax.nn.softplus(logits[:, :, 0])
    best_source = lax.pmax(jnp.max(scores, axis=(2, 3)), "ba")
    best_target = lax.pmax(jnp.max(scores, axis=(0, 1)), "aa")
    return (
        scores
        * (scores / (best_target[None, None] + eps))
        * (scores / (best_source[:, :, None, None] + eps))
    )


def solution(mesh):
    return jax.shard_map(
        per_device,
        mesh=mesh,
        in_specs=(P("aa", None, None), P("ba", None, None), P(), P(), P(), P()),
        out_specs=P("aa", None, "ba", None),
        check_vma=False,
    )
```

profile of v0, /device:TPU:0, one launch (start us, length us, event | category | flops | bytes accessed | tf_op | source)
XLA Modules:
  0.0 954.2 jit_solution(6438290869272222868)
XLA Ops:
  0.0 7.7 all_gather.3
  7.8 6.0 fusion.12
  31.5 6.1 copy.65
  38.4 6.2 copy.63
  47.2 6.1 copy.67
  53.3 17.6 %fusion.24 = f32[30,16,8,512]{0,1,3,2:T(8,128)} fusion(bf16[30,3,10,514]{0,1,3,2:T(4,128)(2,1)} %copy.65, bf16[16,1,1,3,3,3]{0,5,4,3,2,1:T(4,128)(2,1)S(1)} %get-tuple-element.34), kind=kOutput, calls=%fused_computation.52 | convolution fusion | flops 106168320 | bytes 8790384 | tf_op jit(solution)/shard_map/conv_general_dilated | solution.py:45
  70.8 15.3 %fusion.25 = f32[30,16,8,512]{0,1,3,2:T(8,128)} fusion(bf16[30,3,10,514]{0,1,3,2:T(4,128)(2,1)S(1)} %bitcast.80, bf16[16,1,1,3,3,3]{0,5,4,3,2,1:T(4,128)(2,1)S(1)} %get-tuple-element.35), kind=kOutput, calls=%fused_computation.54 | convolution fusion | flops 106168320 | bytes 8790384 | tf_op jit(solution)/shard_map/conv_general_dilated | solution.py:45
  86.1 36.4 %add_add_fusion = f32[30,16,8,512]{0,1,3,2:T(8,128)} fusion(f32[30,16,8,512]{0,1,3,2:T(8,128)} %fusion.25, f32[30,16,8,512]{0,1,3,2:T(8,128)} %fusion.24, bf16[30,3,10,514]{0,1,3,2:T(4,128)(2,1)} %copy.67, bf16[16,1,1,3,3,3]{0,5,4,3,2,1:T(4,128)(2,1)S(1)} %get-tuple-element.33), kind=kOutput, calls=%fused_computation | convolution fusion | flops 110100480 | bytes 24519024 | tf_op jit(solution)/shard_map/conv_general_dilated | solution.py:45
  122.5 18.9 %copy.68 = f32[30,16,8,512]{3,2,1,0:T(8,128)} copy(f32[30,16,8,512]{0,1,3,2:T(8,128)} %add_add_fusion) | data formatting | bytes 15728640 | tf_op jit(solution)/shard_map/add | solution.py:45
  141.4 4.5 multiply_convert_fusion
  162.9 4.3 collective-permute-done.3
  167.1 4.3 select_maximum_fusion
  171.5 4.8 fusion.27
  176.2 4.7 pad_maximum_fusion.1
  180.9 22.4 %copy.75 = bf16[1,10,48,10,514]{2,1,4,3,0:T(8,128)(2,1)} copy(bf16[1,10,48,10,514]{4,2,3,1,0:T(8,128)(2,1)} %pad_maximum_fusion.1) | data formatting | bytes 9868800 | tf_op jit(solution)/shard_map/concatenate | solution.py:34
  203.3 198.0 %fusion.2 = f32[10,1,8,512]{0,1,3,2:T(1,128)} fusion(bf16[1,48,3,3]{1,0,3,2:T(2,128)(2,1)S(1)} %reshape.163, bf16[1,10,48,10,514]{2,1,4,3,0:T(8,128)(2,1)} %copy.75), kind=kOutput, calls=%fused_computation.7 | convolution fusion | flops 35389440 | bytes 5099104 | tf_op jit(solution)/shard_map/conv_general_dilated | solution.py:45
  404.0 6.0 pad_maximum_fusion
  410.0 22.4 %copy.72 = bf16[1,10,48,10,514]{2,1,4,3,0:T(8,128)(2,1)} copy(bf16[1,10,48,10,514]{4,2,3,1,0:T(8,128)(2,1)} %pad_maximum_fusion) | data formatting | bytes 9868800 | tf_op jit(solution)/shard_map/concatenate | solution.py:34
  432.4 198.2 %fusion.4 = f32[10,1,8,512]{0,1,3,2:T(1,128)} fusion(bf16[1,48,3,3]{1,0,3,2:T(2,128)(2,1)S(1)} %reshape.162, bf16[1,10,48,10,514]{2,1,4,3,0:T(8,128)(2,1)} %copy.72), kind=kOutput, calls=%fused_computation.9 | convolution fusion | flops 35389440 | bytes 5099104 | tf_op jit(solution)/shard_map/conv_general_dilated | solution.py:45
  633.3 5.3 pad_maximum_fusion.2
  638.7 22.4 %copy.80 = bf16[1,10,48,10,514]{2,1,4,3,0:T(8,128)(2,1)} copy(bf16[1,10,48,10,514]{4,2,3,1,0:T(8,128)(2,1)} %pad_maximum_fusion.2) | data formatting | bytes 9868800 | tf_op jit(solution)/shard_map/concatenate | solution.py:34
  661.1 197.1 %fusion = f32[10,1,8,512]{0,1,3,2:T(1,128)S(1)} fusion(bf16[1,48,3,3]{1,0,3,2:T(2,128)(2,1)S(1)} %reshape.164, bf16[1,10,48,10,514]{2,1,4,3,0:T(8,128)(2,1)} %copy.80), kind=kOutput, calls=%fused_computation.5 | convolution fusion | flops 35389440 | bytes 5099104 | tf_op jit(solution)/shard_map/conv_general_dilated | solution.py:45
  859.4 13.7 %pmax.14 = f32[8,512]{1,0:T(8,128)S(1)} all-reduce(f32[8,512]{1,0:T(8,128)S(1)} %get-tuple-element.5), channel_id=1, replica_groups=mesh['aa'=4,'ba'=32] {'aa'}, use_global_device_ids=true, to_apply=%region_1.2 | all-reduce | flops 4096 | bytes 32768 | tf_op jit(solution)/shard_map/pmax | solution.py:97
  873.1 80.2 %pmax.15 = f32[1,10]{1,0:T(1,128)S(1)} all-reduce(f32[1,10]{1,0:T(1,128)S(1)} %bitcast.86), channel_id=1, replica_groups=mesh['aa'=4,'ba'=32] {'ba'}, use_global_device_ids=true, to_apply=%region_3.4 | all-reduce | flops 10 | bytes 80 | tf_op jit(solution)/shard_map/pmax | solution.py:96
  (53 shorter events, 44.6 us)
Async XLA Ops:
  7.8 11.1 %copy-start.1 = (bf16[16,1,3,3,3,3]{0,5,4,3,2,1:T(4,128)(2,1)S(1)}, bf16[16,1,3,3,3,3]{0,5,4,3,2,1:T(4,128)(2,1)}, u32[]{:S(2)}) copy-start(bf16[16,1,3,3,3,3]{0,5,4,3,2,1:T(4,128)(2,1)} %param.8) | copy-start | bytes 7780
  14.2 5.6 collective-permute-start
  17.6 6.3 collective-permute-start.1
  47.2 23.7 %slice-start = ((s8[5263360]{0:T(1024)(128)(4,1)}), s8[1069056]{0:T(1024)(128)(4,1)S(1)}, s32[]{:S(2)}) async-start(s8[5263360]{0:T(1024)(128)(4,1)} %bitcast.79), calls=%async_computation | async-start | bytes 2138112
  53.3 17.6 %slice-start.1 = ((s8[5263360]{0:T(1024)(128)(4,1)}), s8[4194304]{0:T(1024)(128)(4,1)S(1)}, s32[]{:S(2)}) async-start(s8[5263360]{0:T(1024)(128)(4,1)} %bitcast.79), calls=%async_computation.1 | async-start | bytes 8388608
  122.5 18.9 %copy-start.3 = (f32[16]{0:T(128)S(1)}, f32[16]{0:T(128)}, u32[]{:S(2)}) copy-start(f32[16]{0:T(128)} %param.9) | copy-start | bytes 196
  145.9 1.9 copy-start
  147.8 7.0 copy-start.2
  149.9 12.9 %collective-permute-start.2 = (bf16[3,10,16,1,512]{4,2,3,1,0:T(8,128)(2,1)S(1)}, bf16[3,10,16,1,512]{4,2,3,1,0:T(8,128)(2,1)S(1)}, u32[]{:S(2)}, u32[]{:S(2)}) collective-permute-start(bf16[3,10,16,1,512]{4,2,3,1,0:T(8,128)(2,1)S(1)} %copy.69), channel_id=1, source_target_pairs={{0,1},{1,2},{2,3},{3,4},{4,5},{5,6},{6,7},{7,8},{8,9},{9,10},{10,1... | collective-permute-start | bytes 1474568 | tf_op jit(solution)/shard_map/ppermute | solution.py:19
  153.5 13.7 %collective-permute-start.3 = (bf16[3,10,16,1,512]{4,2,3,1,0:T(8,128)(2,1)S(1)}, bf16[3,10,16,1,512]{4,2,3,1,0:T(8,128)(2,1)S(1)}, u32[]{:S(2)}, u32[]{:S(2)}) collective-permute-start(bf16[3,10,16,1,512]{4,2,3,1,0:T(8,128)(2,1)S(1)} %copy.70), channel_id=1, source_target_pairs={{1,0},{2,1},{3,2},{4,3},{5,4},{6,5},{7,6},{8,7},{9,8},{10,9},{11,1... | collective-permute-start | bytes 1474568 | tf_op jit(solution)/shard_map/ppermute | solution.py:20
where the time goes:
time: 960 us; the launch traced here: 954 us
  matrix products  669 us (70%)
  local copies, waits for them, and re-layouts  130 us (14%)
  blocking collectives  102 us (11%)
  other arithmetic  30.8 us (3%)
  waiting for transfers between devices  12.5 us (1%)
    conv_general_dilated x6, matrix products, stencil(): lax.conv_general_dilated(stacked, taps, (1, 1), 'VALID', dimension_number...  663 us
    pmax x1, blocking collectives, per_device(): best_source = lax.pmax(jnp.max(scores, axis=(2, 3)), 'ba')  80.2 us
    concatenate x3, local copies, waits for them, and re-layouts, stencil(): jnp.concatenate([volume[shift_a:shift_a + rows_a, shift_c:shift_c + cols_...  67.2 us
    reshape x6, local copies, waits for them, and re-layouts, stencil(): stacked.reshape(rows_a * cols_a, 3 * chan_in, rows_b + 2, cols_b + 2)  22.5 us
    concatenate x5, other arithmetic, stencil(): jnp.concatenate([volume[shift_a:shift_a + rows_a, shift_c:shift_c + cols_...  19.9 us
  transfers between devices with their start and end apart: 4, of which 4 were waited for; matrix products, arithmetic and copies ran while one was open for 0% of the time, Pallas kernels for 0%

commit v1 on v0

v1 whole, which is shorter than its diff:
```python
import functools

import jax
import jax.numpy as jnp
import numpy as np
from jax import lax
from jax.experimental import pallas as pl
from jax.experimental.pallas import tpu as pltpu
from jax.sharding import PartitionSpec as P

C = 1024
HID = 16
AW = 10
AR = 4
CELLS = AR * AW
PAD = 48
BW = 512
BR = 8
TAPS = 9
K1 = TAPS * PAD
M1 = CELLS * HID
M2 = TAPS * CELLS
M2P = 368
EPS = 1e-5
BF = jnp.bfloat16
F32 = jnp.float32
VMEM_LIMIT = 56 * 1024 * 1024


def softplus(v):
    return jnp.maximum(v, 0.0) + jnp.log1p(jnp.exp(-jnp.abs(v)))


def shifted(x, t):
    if t == 1:
        return x
    lane = lax.broadcasted_iota(jnp.int32, x.shape, 1)
    if t == 0:
        return jnp.where(lane == 0, 0.0, pltpu.roll(x, 1, 1))
    return jnp.where(lane == BW - 1, 0.0, pltpu.roll(x, BW - 1, 1))


def column_tables():
    table = np.full((8, 640), -1000, np.int32)
    col = np.arange(K1)
    cell = col % PAD
    table[0, :K1] = np.where(cell < CELLS, cell // AW, -1000)
    table[1, :K1] = np.where(cell < CELLS, cell % AW, 0)
    table[2, :K1] = col // PAD
    table[3, :K1] = np.where((col // PAD == 4) & (cell >= CELLS), cell - CELLS, -1000)
    col = np.arange(M1)
    table[4] = col // HID
    table[5] = col % HID
    return table


def prep_kernel(table_ref, k1_ref, b1_ref, k2_ref, w1_ref, w2_ref, w2f_ref):
    me = lax.axis_index("aa")
    rank = table_ref[0:1, :K1]
    real = rank >= 0
    rank = jnp.where(real, lax.bitwise_xor(jnp.where(real, rank, 0), me), -1000)
    cell = rank * AW + table_ref[1:2, :K1]
    tap = table_ref[2:3, :K1]
    slot = table_ref[3:4, :K1]
    weight = k1_ref[...]
    row_id = lax.broadcasted_iota(jnp.int32, (81, K1), 0)
    spread = []
    for uv in range(9):
        pick = jnp.where(row_id == uv * 9 + tap, 1.0, 0.0).astype(BF)
        spread.append(jnp.dot(weight, pick, preferred_element_type=F32))
    bias = b1_ref[...]
    hi = bias.astype(BF).astype(F32)
    mid = (bias - hi).astype(BF).astype(F32)
    low = bias - hi - mid
    slot16 = jnp.broadcast_to(slot, (HID, K1))
    base = jnp.where(
        slot16 == 0, hi, jnp.where(slot16 == 1, mid, jnp.where(slot16 == 2, low, 0.0))
    )
    cell16 = jnp.broadcast_to(cell, (HID, K1))
    for r in range(AR):
        for j in range(AW):
            block = base
            for u in range(3):
                for v in range(3):
                    if 0 <= r + u - 1 < AR and 0 <= j + v - 1 < AW:
                        where = (r + u - 1) * AW + j + v - 1
                        block = jnp.where(cell16 == where, spread[u * 3 + v], block)
            start = (r * AW + j) * HID
            w1_ref[start : start + HID, :] = block.astype(BF)
    chan = table_ref[5:6, :]
    pick = jnp.where(
        lax.broadcasted_iota(jnp.int32, (HID, M1), 0) == chan, 1.0, 0.0
    ).astype(BF)
    rows = jnp.dot(k2_ref[...], pick, preferred_element_type=F32)
    own = lax.broadcasted_iota(jnp.int32, (CELLS, M1), 0)
    own_row = jnp.where(own >= 10, 1, 0) + jnp.where(own >= 20, 1, 0) + jnp.where(own >= 30, 1, 0)
    own_col = own - own_row * AW
    own_cell = lax.bitwise_xor(own_row, me) * AW + own_col
    gap = table_ref[4:5, :] - own_cell
    gaps = [
        jnp.where(own_col >= 1, gap, 1000),
        gap,
        jnp.where(own_col <= AW - 2, gap, 1000),
    ]
    for st in range(9):
        block = jnp.zeros((CELLS, M1), F32)
        for u in range(3):
            for v in range(3):
                line = rows[(u * 3 + v) * 9 + st : (u * 3 + v) * 9 + st + 1, :]
                block = jnp.where(gaps[v] == (u - 1) * AW + v - 1, line, block)
        w2f_ref[st * CELLS : (st + 1) * CELLS, :] = block
    w2f_ref[M2:M2P, :] = jnp.zeros((M2P - M2, M1), F32)
    w2_ref[...] = w2f_ref[...].astype(BF)


def prep(k1, b1, k2):
    vm = pl.BlockSpec(memory_space=pltpu.VMEM)
    return pl.pallas_call(
        prep_kernel,
        out_shape=(
            jax.ShapeDtypeStruct((M1, K1), BF),
            jax.ShapeDtypeStruct((M2P, M1), BF),
        ),
        in_specs=[vm] * 4,
        out_specs=(vm, vm),
        scratch_shapes=[pltpu.VMEM((M2P, M1), F32)],
        compiler_params=pltpu.CompilerParams(vmem_limit_bytes=VMEM_LIMIT),
        cost_estimate=pl.CostEstimate(flops=10**9, bytes_accessed=10**6, transcendentals=0),
        name="prep",
    )(column_tables(), k1, b1, k2)


def corr_kernel(s0, s1, s2, s3, target_ref, out_ref, lo_ref, hi_ref, stage, feats):
    p = pl.program_id(0)

    @pl.when(p == 0)
    def _():
        for n, ref in enumerate((s0, s1, s2, s3)):
            stage[n * AW : (n + 1) * AW, :] = ref[0].astype(F32)
        feats[0:CELLS, :] = stage[...]
        feats[CELLS:PAD, :] = jnp.zeros((PAD - CELLS, C), F32)

    product = lax.dot_general(
        feats[...].astype(BF),
        target_ref[0],
        (((1,), (1,)), ((), ())),
        preferred_element_type=F32,
    )
    value = (product * C ** (-0.5)).astype(BF).astype(F32)
    row = lax.broadcasted_iota(jnp.int32, value.shape, 0)
    value = jnp.where(row >= CELLS, 1.0, value)
    center = value.astype(BF)
    out_ref[0:PAD, :] = shifted(value, 0).astype(BF)
    out_ref[PAD : 2 * PAD, :] = center
    out_ref[2 * PAD : 3 * PAD, :] = shifted(value, 2).astype(BF)
    for n in range(2):

        @pl.when(p == n)
        def _():
            lo_ref[:, n * BW : (n + 1) * BW] = center

        @pl.when(p == BR - 2 + n)
        def _():
            hi_ref[:, n * BW : (n + 1) * BW] = center


def correlate(sources, target):
    src = pl.BlockSpec((1, AW, C), lambda p: (0, 0, 0))
    edge = pl.BlockSpec((PAD, 2 * BW), lambda p: (0, 0))
    return pl.pallas_call(
        corr_kernel,
        grid=(BR,),
        out_shape=(
            jax.ShapeDtypeStruct((3 * PAD, BR * BW), BF),
            jax.ShapeDtypeStruct((PAD, 2 * BW), BF),
            jax.ShapeDtypeStruct((PAD, 2 * BW), BF),
        ),
        in_specs=[src] * 4 + [pl.BlockSpec((1, BW, C), lambda p: (p, 0, 0))],
        out_specs=(pl.BlockSpec((3 * PAD, BW), lambda p: (0, p)), edge, edge),
        scratch_shapes=[pltpu.VMEM((CELLS, C), F32), pltpu.VMEM((PAD, C), F32)],
        compiler_params=pltpu.CompilerParams(vmem_limit_bytes=VMEM_LIMIT),
        name="correlate",
    )(*sources, target)


def conv_kernel(
    blocks, x_ref, lo_ref, hi_ref, w1_ref, w2_ref, b2_ref, s_ref, bt_ref, mx_ref, edge, acc
):
    place = lax.axis_index("ba")
    for n, ref in enumerate((lo_ref, hi_ref)):
        for m in range(2):
            value = ref[:, m * BW : (m + 1) * BW].astype(F32)
            for t in range(3):
                edge[n * 2 + m, t * PAD : (t + 1) * PAD, :] = shifted(value, t).astype(BF)

    def ext(e):
        if e < 2:
            return edge[e]
        if e >= BR + 2:
            return edge[e - BR]
        return x_ref[:, (e - 2) * BW : (e - 1) * BW]

    for h in range(BR + 2):
        x = jnp.concatenate([ext(h), ext(h + 1), ext(h + 2)], axis=0)
        hidden = jnp.dot(w1_ref[...], x, preferred_element_type=F32)
        hidden = jnp.maximum(hidden, 0.0)
        if h == 0:
            hidden = jnp.where(place > 0, hidden, 0.0)
        if h == BR + 1:
            hidden = jnp.where(place < blocks - 1, hidden, 0.0)
        z = jnp.dot(w2_ref[...], hidden.astype(BF), preferred_element_type=F32)
        for s in range(3):
            p = h - s
            if 0 <= p < BR:
                part = z[s * 3 * CELLS : (s + 1) * 3 * CELLS, :]
                if s == 0:
                    acc[p] = part
                else:
                    acc[p] = acc[p] + part
    b2 = b2_ref[0]
    best = None
    for p in range(BR):
        logits = (
            acc[p, CELLS : 2 * CELLS, :]
            + shifted(acc[p, 0:CELLS, :], 0)
            + shifted(acc[p, 2 * CELLS : 3 * CELLS, :], 2)
            + b2
        )
        bt_ref[p : p + 1, :] = softplus(jnp.max(logits, axis=0, keepdims=True))
        mine = logits[0:AW, :]
        best = mine if best is None else jnp.maximum(best, mine)
        score = softplus(mine)
        for j in range(AW):
            s_ref[j, p : p + 1, :] = score[j : j + 1, :]
    top = jnp.max(best, axis=1, keepdims=True)
    row = lax.broadcasted_iota(jnp.int32, (AW, 128), 0)
    lane = lax.broadcasted_iota(jnp.int32, (AW, 128), 1)
    line = jnp.sum(jnp.where(row == lane, top, 0.0), axis=0, keepdims=True)
    mx_ref[...] = jnp.broadcast_to(line, mx_ref.shape)


def convolve(blocks, x, lo, hi, w1, w2, b2):
    vm = pl.BlockSpec(memory_space=pltpu.VMEM)
    return pl.pallas_call(
        functools.partial(conv_kernel, blocks),
        out_shape=(
            jax.ShapeDtypeStruct((AW, BR, BW), F32),
            jax.ShapeDtypeStruct((BR, BW), F32),
            jax.ShapeDtypeStruct((blocks, 128), F32),
        ),
        in_specs=[vm] * 5 + [pl.BlockSpec(memory_space=pltpu.SMEM)],
        out_specs=(vm, vm, vm),
        scratch_shapes=[
            pltpu.VMEM((4, 3 * PAD, BW), BF),
            pltpu.VMEM((BR, 3 * CELLS, BW), F32),
        ],
        compiler_params=pltpu.CompilerParams(vmem_limit_bytes=VMEM_LIMIT),
        name="convolve",
    )(x, lo, hi, w1, w2, b2)


def final_kernel(s_ref, bt_ref, mx_ref, out_ref):
    top = softplus(jnp.max(mx_ref[...], axis=0, keepdims=True))
    best = bt_ref[...] + EPS
    for j in range(AW):
        s = s_ref[j]
        out_ref[0, j] = s * (s / best) * (s / (top[:, j : j + 1] + EPS))


def finish(s, bt, mx):
    vm = pl.BlockSpec(memory_space=pltpu.VMEM)
    return pl.pallas_call(
        final_kernel,
        out_shape=jax.ShapeDtypeStruct((1, AW, BR, BW), F32),
        in_specs=[vm] * 3,
        out_specs=vm,
        name="finish",
    )(s, bt, mx)


def per_device(source, target, first_kernel, first_bias, second_kernel, second_bias):
    blocks = lax.axis_size("ba")
    size = lax.axis_size("aa")
    sources = [source] + [
        lax.ppermute(source, "aa", [(i, i ^ k) for i in range(size)]) for k in range(1, size)
    ]
    w1, w2 = prep(
        first_kernel.reshape(HID, 81), first_bias[:, None], second_kernel.reshape(HID, 81).T
    )
    x, lo, hi = correlate(sources, target)
    up = [(i, i + 1) for i in range(blocks - 1)]
    before = lax.ppermute(hi, "ba", up)
    after = lax.ppermute(lo, "ba", [(j, i) for i, j in up])
    s, bt, mx = convolve(blocks, x, before, after, w1, w2, second_bias)
    mx = lax.all_to_all(mx, "ba", 0, 0, tiled=True)
    return finish(s, bt, mx)


def solution(mesh):
    return jax.shard_map(
        per_device,
        mesh=mesh,
        in_specs=(P("aa", None, None), P("ba", None, None), P(), P(), P(), P()),
        out_specs=P("aa", None, "ba", None),
        check_vma=False,
    )
```

time: 960 us -> 60.2 us (0.06)
  matrix products: 669 us -> 0 us
  local copies, waits for them, and re-layouts: 130 us -> 3.27 us
  blocking collectives: 102 us -> 19.1 us
  other arithmetic: 30.8 us -> 0 us
  Pallas kernels: 0 us -> 22.7 us
    conv_general_dilated x6 -> x0, matrix products: 663 us -> none  [stencil(): lax.conv_general_dilated(stacked, taps, (1, 1), 'VALID', dimension_number...]
    pmax x2 -> x0, blocking collectives: 93.9 us -> none  [the longest x1 80.2 us: per_device(): best_source = lax.pmax(jnp.max(scores, axis=(2, 3)), 'ba')]
    concatenate x3 -> x0, local copies, waits for them, and re-layouts: 67.2 us -> none  [stencil(): jnp.concatenate([volume[shift_a:shift_a + rows_a, shift_c:shift_c + cols_...]
    concatenate x7 -> x0, other arithmetic: 25.3 us -> none  [the longest x5 19.9 us: stencil(): jnp.concatenate([volume[shift_a:shift_a + rows_a, shift_c:shift_c + cols_...]
    pallas_call x0 -> x4, Pallas kernels: none -> 22.7 us  [the longest x1 9.31 us: convolve(): pl.pallas_call(functools.partial(conv_kernel, blocks), out_shape=(jax.Sha...]
    reshape x11 -> x3, local copies, waits for them, and re-layouts: 22.9 us -> 1.33 us  [the longest x2 0.7 us: per_device(): first_kernel.reshape(HID, 81)]
    all_to_all x0 -> x1, blocking collectives: none -> 19.1 us  [per_device(): mx = lax.all_to_all(mx, 'ba', 0, 0, tiled=True)]
    add x1 -> x0, local copies, waits for them, and re-layouts: 18.9 us -> none  [stencil(): running_sum + lax.conv_general_dilated(stacked, taps, (1, 1), 'VALID', di...]
  transfers between devices with their start and end apart: 4 -> 5, of which waited for: 4 -> 3; matrix products, arithmetic and copies ran while one was open for 0% -> 3% of each run, Pallas kernels for 0% -> 5%
where the time goes in v1:
time: 60.2 us; the launch traced here: 59.7 us
  Pallas kernels  22.7 us (38%)
  blocking collectives  19.1 us (32%)
  starting transfers between devices  8.94 us (15%)
  waiting for transfers between devices  5.1 us (8%)
  local copies, waits for them, and re-layouts  3.27 us (5%)
  between operations  0.69 us (1%)
    all_to_all x1, blocking collectives, per_device(): mx = lax.all_to_all(mx, 'ba', 0, 0, tiled=True)  19.1 us
    pallas_call x1, Pallas kernels, convolve(): pl.pallas_call(functools.partial(conv_kernel, blocks), out_shape=(jax.Sha...  9.31 us
    pallas_call x1, Pallas kernels, correlate(): pl.pallas_call(corr_kernel, grid=(BR,), out_shape=(jax.ShapeDtypeStruct((...  8.84 us
    ppermute x3, waiting for transfers between devices, per_device(): lax.ppermute(source, 'aa', [(i, i ^ k) for i in range(size)])  4.83 us
    ppermute x3, starting transfers between devices, per_device(): lax.ppermute(source, 'aa', [(i, i ^ k) for i in range(size)])  4.26 us
    ppermute x1, starting transfers between devices, per_device(): before = lax.ppermute(hi, 'ba', up)  3.39 us
    pallas_call x1, Pallas kernels, prep(): pl.pallas_call(prep_kernel, out_shape=(jax.ShapeDtypeStruct((M1, K1), BF)...  2.79 us
    pallas_call x1, Pallas kernels, finish(): pl.pallas_call(final_kernel, out_shape=jax.ShapeDtypeStruct((1, AW, BR, B...  1.72 us
  transfers between devices with their start and end apart: 5, of which 3 were waited for; matrix products, arithmetic and copies ran while one was open for 3% of the time, Pallas kernels for 5%

profile of v1, /device:TPU:0, one launch (start us, length us, event | category | flops | bytes accessed | tf_op | source)
XLA Modules:
  0.0 59.7 jit_solution(11892424435833533060)
XLA Ops:
  0.0 4.0 %collective-permute-start.1 = (bf16[1,10,1024]{2,1,0:T(8,128)(2,1)}, bf16[1,10,1024]{2,1,0:T(8,128)(2,1)S(1)}, u32[]{:S(2)}, u32[]{:S(2)}) collective-permute-start(bf16[1,10,1024]{2,1,0:T(8,128)(2,1)} %s0.1), channel_id=1, source_target_pairs={{0,64},{32,96},{64,0},{96,32},{1,65},{33,97},{65,1},{97,33},{2,66}... | collective-permute-start | bytes 61448 | tf_op jit(solution)/shard_map/ppermute | solution.py:285
  4.0 0.0 collective-permute-start
  4.1 0.2 collective-permute-start.2
  4.3 1.9 %collective-permute-done.1.s2 = bf16[1,10,1024]{2,1,0:T(8,128)(2,1)S(1)} collective-permute-done((bf16[1,10,1024]{2,1,0:T(8,128)(2,1)}, bf16[1,10,1024]{2,1,0:T(8,128)(2,1)S(1)}, u32[]{:S(2)}, u32[]{:S(2)}) %collective-permute-start.1) | collective-permute-done | bytes 20512 | tf_op jit(solution)/shard_map/ppermute | solution.py:285
  6.2 0.0 collective-permute-done.s1
  6.2 2.9 %collective-permute-done.2.s3 = bf16[1,10,1024]{2,1,0:T(8,128)(2,1)S(1)} collective-permute-done((bf16[1,10,1024]{2,1,0:T(8,128)(2,1)}, bf16[1,10,1024]{2,1,0:T(8,128)(2,1)S(1)}, u32[]{:S(2)}, u32[]{:S(2)}) %collective-permute-start.2) | collective-permute-done | bytes 20512 | tf_op jit(solution)/shard_map/ppermute | solution.py:285
  9.1 0.0 copy-done.2
  9.1 0.6 %copy-done.4 = bf16[1,10,1024]{2,1,0:T(8,128)(2,1)} copy-done((bf16[1,10,1024]{2,1,0:T(8,128)(2,1)}, bf16[1,10,1024]{2,1,0:T(8,128)(2,1)S(1)}, u32[]{:S(2)}) %copy-start.4) | copy-done | bytes 20504
  9.7 8.8 %correlate.1 = (bf16[144,4096]{1,0:T(8,128)(2,1)}, bf16[48,1024]{1,0:T(8,128)(2,1)}, bf16[48,1024]{1,0:T(8,128)(2,1)}) custom-call(bf16[1,10,1024]{2,1,0:T(8,128)(2,1)} %s0.1, bf16[1,10,1024]{2,1,0:T(8,128)(2,1)} %copy-done.3, bf16[1,10,1024]{2,1,0:T(8,128)(2,1)} %copy-done.2, bf16[1,10,1024]{2,1,0:T(8,128)(2,1)} %copy-done.4, bf16[8,512,1024]{2,1,0:T(8,128)(2,1)} %target_ref.1), custom_call_target="tpu_custom_call" | custom-call | tf_op jit(solution)/shard_map/correlate/pallas_call | solution.py:170
  18.6 3.4 %collective-permute-start.3 = (bf16[48,1024]{1,0:T(8,128)(2,1)}, bf16[48,1024]{1,0:T(8,128)(2,1)S(1)}, u32[]{:S(2)}, u32[]{:S(2)}) collective-permute-start(bf16[48,1024]{1,0:T(8,128)(2,1)} %get-tuple-element.14), channel_id=1, source_target_pairs={{0,1},{1,2},{2,3},{3,4},{4,5},{5,6},{6,7},{7,8},{8,9},{9,10},{10,1... | collective-permute-start | bytes 294920 | tf_op jit(solution)/shard_map/ppermute | solution.py:292
  22.0 1.3 %collective-permute-start.4 = (bf16[48,1024]{1,0:T(8,128)(2,1)}, bf16[48,1024]{1,0:T(8,128)(2,1)S(1)}, u32[]{:S(2)}, u32[]{:S(2)}) collective-permute-start(bf16[48,1024]{1,0:T(8,128)(2,1)} %get-tuple-element.15), channel_id=1, source_target_pairs={{1,0},{2,1},{3,2},{4,3},{5,4},{6,5},{7,6},{8,7},{9,8},{10,9},{11,1... | collective-permute-start | bytes 294920 | tf_op jit(solution)/shard_map/ppermute | solution.py:293
  23.9 0.7 %copy.13.b1_ref = f32[16,1]{1,0:T(8,128)} copy(f32[16,1]{0,1:T(1,128)S(1)} %bitcast.13) | data formatting | bytes 128 | tf_op jit(solution)/shard_map/broadcast_in_dim | solution.py:288
  24.6 0.0 copy-done.5
  24.6 0.7 %copy.12.k1_ref = bf16[16,81]{1,0:T(8,128)(2,1)} copy(bf16[16,81]{0,1:T(8,128)(2,1)S(1)} %reshape.8) | data formatting | bytes 5184 | tf_op jit(solution)/shard_map/reshape | solution.py:288
  25.3 0.0 copy-done.6
  25.3 0.6 %reshape.9 = bf16[16,81]{0,1:T(8,128)(2,1)} reshape(bf16[1,16,3,3,3,3]{1,5,4,3,2,0:T(4,128)(2,1)S(1)} %copy-done.6) | data formatting | bytes 5184 | tf_op jit(solution)/shard_map/reshape | solution.py:288
  25.9 2.8 %prep.1 = (bf16[640,432]{1,0:T(8,128)(2,1)}, bf16[368,640]{1,0:T(8,128)(2,1)}) custom-call(s32[8,640]{1,0:T(8,128)} %constant.2.clone.table_ref, bf16[16,81]{1,0:T(8,128)(2,1)} %copy.12.k1_ref, f32[16,1]{1,0:T(8,128)} %copy.13.b1_ref, bf16[81,16]{1,0:T(8,128)(2,1)} %bitcast.11), custom_call_target="tpu_custom_call" | custom-call | flops 1000000000 | bytes 1000000 | tf_op jit(solution)/shard_map/prep/pallas_call | solution.py:118
  28.7 0.0 collective-permute-done.3.lo_ref
  28.7 0.3 collective-permute-done.4.hi_ref
  29.0 0.4 copy-done
  29.4 0.3 copy-done.1
  29.6 9.3 %convolve.1 = (f32[10,8,512]{2,1,0:T(8,128)}, f32[8,512]{1,0:T(8,128)}, f32[32,128]{1,0:T(8,128)}) custom-call(bf16[144,4096]{1,0:T(8,128)(2,1)} %get-tuple-element.13.x_ref, bf16[48,1024]{1,0:T(8,128)(2,1)} %copy-done, bf16[48,1024]{1,0:T(8,128)(2,1)} %copy-done.1, bf16[640,432]{1,0:T(8,128)(2,1)} %get-tuple-element.16.w1_ref, ...), custom_call_target="tpu_custom_call" | custom-call | tf_op jit(solution)/shard_map/convolve/pallas_call | solution.py:244
  38.9 19.1 %all_to_all.11 = f32[32,1,128]{2,1,0:T(1,128)} all-to-all(f32[32,1,128]{2,1,0:T(1,128)} %bitcast.12), channel_id=1, replica_groups=mesh['aa'=4,'ba'=32] {'ba'}, dimensions={0} | all-to-all | bytes 32768 | tf_op jit(solution)/shard_map/all_to_all | solution.py:295
  58.0 1.7 %finish.1 = f32[1,10,8,512]{3,2,1,0:T(8,128)} custom-call(f32[10,8,512]{2,1,0:T(8,128)} %get-tuple-element.18.s_ref, f32[8,512]{1,0:T(8,128)} %get-tuple-element.19.bt_ref, f32[32,128]{1,0:T(8,128)} %bitcast.10), custom_call_target="tpu_custom_call" | custom-call | tf_op jit(solution)/shard_map/finish/pallas_call | solution.py:272
  (11 shorter events, 0.0 us)
Async XLA Ops:
  0.0 23.9 %copy-start.7 = (f32[16]{0:T(128)S(1)}, f32[16]{0:T(128)}, u32[]{:S(2)}) copy-start(f32[16]{0:T(128)} %param.10) | copy-start | bytes 196
  0.0 24.6 %copy-start.5 = (bf16[16,1,3,3,3,3]{0,5,4,3,2,1:T(4,128)(2,1)S(1)}, bf16[16,1,3,3,3,3]{0,5,4,3,2,1:T(4,128)(2,1)}, u32[]{:S(2)}) copy-start(bf16[16,1,3,3,3,3]{0,5,4,3,2,1:T(4,128)(2,1)} %param.9) | copy-start | bytes 7780
  0.0 25.3 %copy-start.6 = (bf16[1,16,3,3,3,3]{1,5,4,3,2,0:T(4,128)(2,1)S(1)}, bf16[1,16,3,3,3,3]{1,5,4,3,2,0:T(4,128)(2,1)}, u32[]{:S(2)}) copy-start(bf16[1,16,3,3,3,3]{1,5,4,3,2,0:T(4,128)(2,1)} %param.11) | copy-start | bytes 7780
  0.0 6.1 %collective-permute-start.1 = (bf16[1,10,1024]{2,1,0:T(8,128)(2,1)}, bf16[1,10,1024]{2,1,0:T(8,128)(2,1)S(1)}, u32[]{:S(2)}, u32[]{:S(2)}) collective-permute-start(bf16[1,10,1024]{2,1,0:T(8,128)(2,1)} %s0.1), channel_id=1, source_target_pairs={{0,64},{32,96},{64,0},{96,32},{1,65},{33,97},{65,1},{97,33},{2,66}... | collective-permute-start | bytes 61448 | tf_op jit(solution)/shard_map/ppermute | solution.py:285
  4.0 2.1 %collective-permute-start = (bf16[1,10,1024]{2,1,0:T(8,128)(2,1)}, bf16[1,10,1024]{2,1,0:T(8,128)(2,1)S(1)}, u32[]{:S(2)}, u32[]{:S(2)}) collective-permute-start(bf16[1,10,1024]{2,1,0:T(8,128)(2,1)} %s0.1), channel_id=1, source_target_pairs={{0,32},{32,0},{64,96},{96,64},{1,33},{33,1},{65,97},{97,65},{2,34}... | collective-permute-start | bytes 61448 | tf_op jit(solution)/shard_map/ppermute | solution.py:285
  4.1 5.1 %collective-permute-start.2 = (bf16[1,10,1024]{2,1,0:T(8,128)(2,1)}, bf16[1,10,1024]{2,1,0:T(8,128)(2,1)S(1)}, u32[]{:S(2)}, u32[]{:S(2)}) collective-permute-start(bf16[1,10,1024]{2,1,0:T(8,128)(2,1)} %s0.1), channel_id=1, source_target_pairs={{0,96},{32,64},{64,32},{96,0},{1,97},{33,65},{65,33},{97,1},{2,98}... | collective-permute-start | bytes 61448 | tf_op jit(solution)/shard_map/ppermute | solution.py:285
  6.2 3.0 %copy-start.2 = (bf16[1,10,1024]{2,1,0:T(8,128)(2,1)}, bf16[1,10,1024]{2,1,0:T(8,128)(2,1)S(1)}, u32[]{:S(2)}) copy-start(bf16[1,10,1024]{2,1,0:T(8,128)(2,1)S(1)} %collective-permute-done.1.s2) | copy-start | bytes 61444
  6.2 3.0 %copy-start.3 = (bf16[1,10,1024]{2,1,0:T(8,128)(2,1)}, bf16[1,10,1024]{2,1,0:T(8,128)(2,1)S(1)}, u32[]{:S(2)}) copy-start(bf16[1,10,1024]{2,1,0:T(8,128)(2,1)S(1)} %collective-permute-done.s1) | copy-start | bytes 61444
  9.1 0.6 %copy-start.4 = (bf16[1,10,1024]{2,1,0:T(8,128)(2,1)}, bf16[1,10,1024]{2,1,0:T(8,128)(2,1)S(1)}, u32[]{:S(2)}) copy-start(bf16[1,10,1024]{2,1,0:T(8,128)(2,1)S(1)} %collective-permute-done.2.s3) | copy-start | bytes 61444
  18.6 10.2 %collective-permute-start.3 = (bf16[48,1024]{1,0:T(8,128)(2,1)}, bf16[48,1024]{1,0:T(8,128)(2,1)S(1)}, u32[]{:S(2)}, u32[]{:S(2)}) collective-permute-start(bf16[48,1024]{1,0:T(8,128)(2,1)} %get-tuple-element.14), channel_id=1, source_target_pairs={{0,1},{1,2},{2,3},{3,4},{4,5},{5,6},{6,7},{7,8},{8,9},{9,10},{10,1... | collective-permute-start | bytes 294920 | tf_op jit(solution)/shard_map/ppermute | solution.py:292
  22.0 7.0 %collective-permute-start.4 = (bf16[48,1024]{1,0:T(8,128)(2,1)}, bf16[48,1024]{1,0:T(8,128)(2,1)S(1)}, u32[]{:S(2)}, u32[]{:S(2)}) collective-permute-start(bf16[48,1024]{1,0:T(8,128)(2,1)} %get-tuple-element.15), channel_id=1, source_target_pairs={{1,0},{2,1},{3,2},{4,3},{5,4},{6,5},{7,6},{8,7},{9,8},{10,9},{11,1... | collective-permute-start | bytes 294920 | tf_op jit(solution)/shard_map/ppermute | solution.py:293
  28.7 0.6 %copy-start = (bf16[48,1024]{1,0:T(8,128)(2,1)}, bf16[48,1024]{1,0:T(8,128)(2,1)S(1)}, u32[]{:S(2)}) copy-start(bf16[48,1024]{1,0:T(8,128)(2,1)S(1)} %collective-permute-done.3.lo_ref) | copy-start | bytes 294916
  29.0 0.6 %copy-start.1 = (bf16[48,1024]{1,0:T(8,128)(2,1)}, bf16[48,1024]{1,0:T(8,128)(2,1)S(1)}, u32[]{:S(2)}) copy-start(bf16[48,1024]{1,0:T(8,128)(2,1)S(1)} %collective-permute-done.4.hi_ref) | copy-start | bytes 294916

commit v2 on v1

v2 whole, which is shorter than its diff:
```python
import functools

import jax
import jax.numpy as jnp
import numpy as np
from jax import lax
from jax.experimental import pallas as pl
from jax.experimental.pallas import tpu as pltpu
from jax.sharding import PartitionSpec as P

C = 1024
HID = 16
AW = 10
AR = 4
CELLS = AR * AW
PAD = 48
BW = 512
BR = 8
TAPS = 9
K1 = TAPS * PAD
M1 = CELLS * HID
M2 = TAPS * CELLS
M2P = 368
EPS = 1e-5
BF = jnp.bfloat16
F32 = jnp.float32
VMEM_LIMIT = 20 * 1024 * 1024


def cost(us):
    return pl.CostEstimate(flops=int(us * 1e9), bytes_accessed=int(us * 3e6), transcendentals=0)


def softplus(v):
    return jnp.maximum(v, 0.0) + jnp.log1p(jnp.exp(-jnp.abs(v)))


def shifted(x, t):
    if t == 1:
        return x
    lane = lax.broadcasted_iota(jnp.int32, x.shape, 1)
    if t == 0:
        return jnp.where(lane == 0, 0.0, pltpu.roll(x, 1, 1))
    return jnp.where(lane == BW - 1, 0.0, pltpu.roll(x, BW - 1, 1))


def column_tables():
    table = np.full((8, 640), -1000, np.int32)
    col = np.arange(K1)
    cell = col % PAD
    table[0, :K1] = np.where(cell < CELLS, cell // AW, -1000)
    table[1, :K1] = np.where(cell < CELLS, cell % AW, 0)
    table[2, :K1] = col // PAD
    table[3, :K1] = np.where((col // PAD == 4) & (cell >= CELLS), cell - CELLS, -1000)
    col = np.arange(M1)
    table[4] = col // HID
    table[5] = col % HID
    return table


def prep_kernel(table_ref, k1_ref, b1_ref, k2_ref, w1_ref, w2_ref, w2f_ref, flat_ref):
    me = lax.axis_index("aa")

    def lines(ref):
        for n in range(27):
            u, v, w = n // 9, n // 3 % 3, n % 3
            flat_ref[3 * n : 3 * n + 3, :] = ref[u, v, w].astype(F32)
        return flat_ref[...].astype(BF)

    rank = table_ref[0:1, :K1]
    real = rank >= 0
    rank = jnp.where(real, lax.bitwise_xor(jnp.where(real, rank, 0), me), -1000)
    cell = rank * AW + table_ref[1:2, :K1]
    tap = table_ref[2:3, :K1]
    slot = table_ref[3:4, :K1]
    weight = lines(k1_ref)
    row_id = lax.broadcasted_iota(jnp.int32, (81, K1), 0)
    spread = []
    for uv in range(9):
        pick = jnp.where(row_id == uv * 9 + tap, 1.0, 0.0).astype(BF)
        spread.append(
            lax.dot_general(
                weight, pick, (((0,), (0,)), ((), ())), preferred_element_type=F32
            )
        )
    square = (HID, HID)
    on = lax.broadcasted_iota(jnp.int32, square, 0) == lax.broadcasted_iota(jnp.int32, square, 1)
    bias = jnp.sum(jnp.where(on, b1_ref[...], 0.0), axis=1, keepdims=True)
    hi = bias.astype(BF).astype(F32)
    mid = (bias - hi).astype(BF).astype(F32)
    low = bias - hi - mid
    slot16 = jnp.broadcast_to(slot, (HID, K1))
    base = jnp.where(
        slot16 == 0, hi, jnp.where(slot16 == 1, mid, jnp.where(slot16 == 2, low, 0.0))
    )
    cell16 = jnp.broadcast_to(cell, (HID, K1))
    for r in range(AR):
        for j in range(AW):
            block = base
            for u in range(3):
                for v in range(3):
                    if 0 <= r + u - 1 < AR and 0 <= j + v - 1 < AW:
                        where = (r + u - 1) * AW + j + v - 1
                        block = jnp.where(cell16 == where, spread[u * 3 + v], block)
            start = (r * AW + j) * HID
            w1_ref[start : start + HID, :] = block.astype(BF)
    chan = table_ref[5:6, :]
    pick = jnp.where(
        lax.broadcasted_iota(jnp.int32, (HID, M1), 0) == chan, 1.0, 0.0
    ).astype(BF)
    rows = jnp.dot(lines(k2_ref), pick, preferred_element_type=F32)
    own = lax.broadcasted_iota(jnp.int32, (CELLS, M1), 0)
    own_row = jnp.where(own >= 10, 1, 0) + jnp.where(own >= 20, 1, 0) + jnp.where(own >= 30, 1, 0)
    own_col = own - own_row * AW
    own_cell = lax.bitwise_xor(own_row, me) * AW + own_col
    gap = table_ref[4:5, :] - own_cell
    gaps = [
        jnp.where(own_col >= 1, gap, 1000),
        gap,
        jnp.where(own_col <= AW - 2, gap, 1000),
    ]
    for st in range(9):
        block = jnp.zeros((CELLS, M1), F32)
        for u in range(3):
            for v in range(3):
                line = rows[(u * 3 + v) * 9 + st : (u * 3 + v) * 9 + st + 1, :]
                block = jnp.where(gaps[v] == (u - 1) * AW + v - 1, line, block)
        w2f_ref[st * CELLS : (st + 1) * CELLS, :] = block
    w2f_ref[M2:M2P, :] = jnp.zeros((M2P - M2, M1), F32)
    w2_ref[...] = w2f_ref[...].astype(BF)


def prep(k1, b1, k2):
    vm = pl.BlockSpec(memory_space=pltpu.VMEM)
    return pl.pallas_call(
        prep_kernel,
        out_shape=(
            jax.ShapeDtypeStruct((M1, K1), BF),
            jax.ShapeDtypeStruct((M2P, M1), BF),
        ),
        in_specs=[vm] * 4,
        out_specs=(vm, vm),
        scratch_shapes=[pltpu.VMEM((M2P, M1), F32), pltpu.VMEM((81, HID), F32)],
        compiler_params=pltpu.CompilerParams(vmem_limit_bytes=VMEM_LIMIT),
        cost_estimate=cost(3.0),
        name="prep",
    )(column_tables(), k1, b1, k2)


def correlation(feats, block):
    product = lax.dot_general(
        feats, block, (((1,), (1,)), ((), ())), preferred_element_type=F32
    )
    value = (product * C ** (-0.5)).astype(BF).astype(F32)
    row = lax.broadcasted_iota(jnp.int32, value.shape, 0)
    return jnp.where(row >= CELLS, 1.0, value)


def edge_kernel(s0, s1, s2, s3, target_ref, w1_ref, feats_ref, lo_ref, hi_ref, stage):
    for n, ref in enumerate((s0, s1, s2, s3)):
        stage[n * AW : (n + 1) * AW, :] = ref[0].astype(F32)
    stage[CELLS:PAD, :] = jnp.zeros((PAD - CELLS, C), F32)
    feats = stage[...].astype(BF)
    feats_ref[...] = feats
    for ref, first in ((lo_ref, 0), (hi_ref, BR - 2)):
        for n in range(2):
            ref[:, n * BW : (n + 1) * BW] = correlation(feats, target_ref[first + n]).astype(BF)


def edges(sources, target, w1):
    vm = pl.BlockSpec(memory_space=pltpu.VMEM)
    edge = jax.ShapeDtypeStruct((PAD, 2 * BW), BF)
    return pl.pallas_call(
        edge_kernel,
        out_shape=(jax.ShapeDtypeStruct((PAD, C), BF), edge, edge),
        in_specs=[vm] * 5 + [pl.BlockSpec(memory_space=pl.ANY)],
        out_specs=(vm, vm, vm),
        scratch_shapes=[pltpu.VMEM((PAD, C), F32)],
        compiler_params=pltpu.CompilerParams(vmem_limit_bytes=VMEM_LIMIT),
        cost_estimate=cost(2.0),
        name="edges",
    )(*sources, target, w1)


def three_shifts(value):
    return jnp.concatenate([shifted(value, t).astype(BF) for t in range(3)], axis=0)


def hidden_row(w1, parts):
    x = jnp.concatenate(parts, axis=0)
    return jnp.maximum(jnp.dot(w1, x, preferred_element_type=F32), 0.0)


def spread_row(h, z, acc, seen, keep):
    for s in range(3):
        p = h - s
        if 0 <= p < BR:
            part = z[s * 3 * CELLS : (s + 1) * 3 * CELLS, :]
            at = keep(p)
            if p in seen:
                acc[at] = acc[at] + part
            else:
                acc[at] = part
                seen.add(p)


def logit_row(sums, b2):
    return (
        sums[CELLS : 2 * CELLS, :]
        + shifted(sums[0:CELLS, :], 0)
        + shifted(sums[2 * CELLS : 3 * CELLS, :], 2)
        + b2
    )


def emit_row(n, logits, s_ref, bt_ref, best):
    bt_ref[n : n + 1, :] = softplus(jnp.max(logits, axis=0, keepdims=True))
    mine = logits[0:AW, :]
    score = softplus(mine)
    for j in range(AW):
        s_ref[j, n : n + 1, :] = score[j : j + 1, :]
    return mine if best is None else jnp.maximum(best, mine)


INNER = (2, 3, 4, 5)
OUTER = (0, 1, 6, 7)


def inner_kernel(
    feats_ref, target_ref, lo_ref, hi_ref, w1_ref, w2_ref, b2_ref,
    s_ref, bt_ref, best_ref, sums_ref, x, acc,
):
    feats = feats_ref[...]
    for n in range(2):
        x[n] = three_shifts(lo_ref[:, n * BW : (n + 1) * BW].astype(F32))
        x[BR - 2 + n] = three_shifts(hi_ref[:, n * BW : (n + 1) * BW].astype(F32))
    for p in range(2, BR - 2):
        x[p] = three_shifts(correlation(feats, target_ref[p]))
    seen = set()
    for h in range(2, BR):
        hidden = hidden_row(w1_ref[...], [x[h - 2], x[h - 1], x[h]])
        z = jnp.dot(w2_ref[...], hidden.astype(BF), preferred_element_type=F32)
        spread_row(h, z, acc, seen, lambda p: p)
    best = None
    for n, p in enumerate(INNER):
        best = emit_row(n, logit_row(acc[p], b2_ref[0]), s_ref, bt_ref, best)
    best_ref[...] = best
    for n, p in enumerate(OUTER):
        sums_ref[n] = acc[p]


def inner(feats, target, lo, hi, w1, w2, b2):
    vm = pl.BlockSpec(memory_space=pltpu.VMEM)
    return pl.pallas_call(
        inner_kernel,
        out_shape=(
            jax.ShapeDtypeStruct((AW, 4, BW), F32),
            jax.ShapeDtypeStruct((4, BW), F32),
            jax.ShapeDtypeStruct((AW, BW), F32),
            jax.ShapeDtypeStruct((4, 3 * CELLS, BW), F32),
        ),
        in_specs=[vm] * 6 + [pl.BlockSpec(memory_space=pltpu.SMEM)],
        out_specs=(vm, vm, vm, vm),
        scratch_shapes=[
            pltpu.VMEM((BR, 3 * PAD, BW), BF),
            pltpu.VMEM((BR, 3 * CELLS, BW), F32),
        ],
        compiler_params=pltpu.CompilerParams(vmem_limit_bytes=VMEM_LIMIT),
        cost_estimate=cost(8.0),
        name="inner",
    )(feats, target, lo, hi, w1, w2, b2)


def outer_kernel(
    blocks, lo_ref, hi_ref, before_ref, after_ref, w1_ref, w2_ref, b2_ref, sums_ref, best_ref,
    s_ref, bt_ref, mx_ref, acc,
):
    place = lax.axis_index("ba")
    first, last = place == 0, place == blocks - 1

    def row(ref, n, drop=None):
        value = ref[:, n * BW : (n + 1) * BW].astype(F32)
        if drop is not None:
            value = jnp.where(drop, 0.0, value)
        return three_shifts(value)

    near = [row(before_ref, 0, first), row(before_ref, 1, first), row(lo_ref, 0), row(lo_ref, 1)]
    far = [row(hi_ref, 0), row(hi_ref, 1), row(after_ref, 0, last), row(after_ref, 1, last)]
    for n in range(4):
        acc[n] = sums_ref[n]
    seen = set(OUTER)
    for h, parts, drop in (
        (0, near[0:3], first),
        (1, near[1:4], None),
        (BR, far[0:3], None),
        (BR + 1, far[1:4], last),
    ):
        hidden = hidden_row(w1_ref[...], parts)
        if drop is not None:
            hidden = jnp.where(drop, 0.0, hidden)
        z = jnp.dot(w2_ref[...], hidden.astype(BF), preferred_element_type=F32)
        spread_row(h, z, acc, seen, OUTER.index)
    best = best_ref[...]
    for n in range(4):
        best = emit_row(n, logit_row(acc[n], b2_ref[0]), s_ref, bt_ref, best)
    top = jnp.max(best, axis=1, keepdims=True)
    row_id = lax.broadcasted_iota(jnp.int32, (AW, 128), 0)
    lane = lax.broadcasted_iota(jnp.int32, (AW, 128), 1)
    line = jnp.sum(jnp.where(row_id == lane, top, 0.0), axis=0, keepdims=True)
    mx_ref[...] = jnp.broadcast_to(line, mx_ref.shape)


def outer(blocks, lo, hi, before, after, w1, w2, b2, sums, best):
    vm = pl.BlockSpec(memory_space=pltpu.VMEM)
    return pl.pallas_call(
        functools.partial(outer_kernel, blocks),
        out_shape=(
            jax.ShapeDtypeStruct((AW, 4, BW), F32),
            jax.ShapeDtypeStruct((4, BW), F32),
            jax.ShapeDtypeStruct((blocks, 128), F32),
        ),
        in_specs=[vm] * 6 + [pl.BlockSpec(memory_space=pltpu.SMEM)] + [vm] * 2,
        out_specs=(vm, vm, vm),
        scratch_shapes=[pltpu.VMEM((4, 3 * CELLS, BW), F32)],
        compiler_params=pltpu.CompilerParams(vmem_limit_bytes=VMEM_LIMIT),
        cost_estimate=cost(4.0),
        name="outer",
    )(lo, hi, before, after, w1, w2, b2, sums, best)


def final_kernel(s1_ref, bt1_ref, s2_ref, bt2_ref, mx_ref, out_ref):
    top = softplus(jnp.max(mx_ref[...], axis=0, keepdims=True))
    best1 = bt1_ref[...] + EPS
    best2 = bt2_ref[...] + EPS
    for j in range(AW):
        cell = top[:, j : j + 1] + EPS
        s = s1_ref[j]
        out_ref[0, j, 2:6, :] = s * (s / best1) * (s / cell)
        s = s2_ref[j]
        both = s * (s / best2) * (s / cell)
        out_ref[0, j, 0:2, :] = both[0:2]
        out_ref[0, j, 6:8, :] = both[2:4]


def finish(s1, bt1, s2, bt2, mx):
    vm = pl.BlockSpec(memory_space=pltpu.VMEM)
    return pl.pallas_call(
        final_kernel,
        out_shape=jax.ShapeDtypeStruct((1, AW, BR, BW), F32),
        in_specs=[vm] * 5,
        out_specs=vm,
        compiler_params=pltpu.CompilerParams(vmem_limit_bytes=4 * 1024 * 1024),
        name="finish",
    )(s1, bt1, s2, bt2, mx)


def per_device(source, target, first_kernel, first_bias, second_kernel, second_bias):
    blocks = lax.axis_size("ba")
    size = lax.axis_size("aa")
    sources = [source] + [
        lax.ppermute(source, "aa", [(i, i ^ k) for i in range(size)]) for k in range(1, size)
    ]
    w1, w2 = prep(
        jnp.transpose(first_kernel[:, 0], (1, 2, 3, 4, 0)),
        first_bias[None, :],
        jnp.transpose(second_kernel[0], (1, 2, 3, 4, 0)),
    )
    feats, lo, hi = edges(sources, target, w1)
    up = [(i, (i + 1) % blocks) for i in range(blocks)]
    before = lax.ppermute(hi, "ba", up)
    after = lax.ppermute(lo, "ba", [(j, i) for i, j in up])
    s1, bt1, best, sums = inner(feats, target, lo, hi, w1, w2, second_bias)
    s2, bt2, mx = outer(blocks, lo, hi, before, after, w1, w2, second_bias, sums, best)
    mx = lax.all_to_all(mx, "ba", 0, 0, tiled=True)
    return finish(s1, bt1, s2, bt2, mx)


def solution(mesh):
    return jax.shard_map(
        per_device,
        mesh=mesh,
        in_specs=(P("aa", None, None), P("ba", None, None), P(), P(), P(), P()),
        out_specs=P("aa", None, "ba", None),
        check_vma=False,
    )
```

time: 60.2 us -> 39.7 us (0.66)
  Pallas kernels: 22.7 us -> 12.1 us
  blocking collectives: 19.1 us -> 13.1 us
  waiting for transfers between devices: 5.1 us -> 0.15 us
  starting transfers between devices: 8.94 us -> 10.4 us
    pallas_call x2 -> x3, Pallas kernels: 18.2 us -> 10 us  [the longest x1 5.55 us: inner(): pl.pallas_call(inner_kernel, out_shape=(jax.ShapeDtypeStruct((AW, 4, BW),...]
    all_to_all x1, blocking collectives: 19.1 us -> 13.1 us  [per_device(): mx = lax.all_to_all(mx, 'ba', 0, 0, tiled=True)]
    ppermute x3, waiting for transfers between devices: 4.83 us -> 0.14 us  [per_device(): lax.ppermute(source, 'aa', [(i, i ^ k) for i in range(size)])]
    ppermute x1, starting transfers between devices: 1.29 us -> 4.76 us  [per_device(): after = lax.ppermute(lo, 'ba', [(j, i) for i, j in up])]
    ppermute x1, starting transfers between devices: 3.39 us -> 1.56 us  [per_device(): before = lax.ppermute(hi, 'ba', up)]
    unnamed x16 -> x12, local copies, waits for them, and re-layouts: 1.26 us -> 2.88 us
    pallas_call x1, Pallas kernels: 2.79 us -> 1.31 us  [prep(): pl.pallas_call(prep_kernel, out_shape=(jax.ShapeDtypeStruct((M1, K1), BF)...]
    reshape x3 -> x0, local copies, waits for them, and re-layouts: 1.33 us -> none  [the longest x2 0.7 us: per_device(): first_kernel.reshape(HID, 81)]
  transfers between devices with their start and end apart: 5 -> 5, of which waited for: 3 -> 1; matrix products, arithmetic and copies ran while one was open for 3% -> 0% of each run, Pallas kernels for 5% -> 17%
where the time goes in v2:
time: 39.7 us; the launch traced here: 39.4 us
  blocking collectives  13.1 us (33%)
  Pallas kernels  12.1 us (30%)
  starting transfers between devices  10.4 us (26%)
  local copies, waits for them, and re-layouts  2.88 us (7%)
  between operations  0.71 us (2%)
    all_to_all x1, blocking collectives, per_device(): mx = lax.all_to_all(mx, 'ba', 0, 0, tiled=True)  13.1 us
    pallas_call x1, Pallas kernels, inner(): pl.pallas_call(inner_kernel, out_shape=(jax.ShapeDtypeStruct((AW, 4, BW),...  5.55 us
    ppermute x1, starting transfers between devices, per_device(): after = lax.ppermute(lo, 'ba', [(j, i) for i, j in up])  4.76 us
    ppermute x3, starting transfers between devices, per_device(): lax.ppermute(source, 'aa', [(i, i ^ k) for i in range(size)])  4.11 us
    pallas_call x1, Pallas kernels, outer(): pl.pallas_call(functools.partial(outer_kernel, blocks), out_shape=(jax.Sh...  3.12 us
    unnamed x12, local copies, waits for them, and re-layouts  2.88 us
    ppermute x1, starting transfers between devices, per_device(): before = lax.ppermute(hi, 'ba', up)  1.56 us
    pallas_call x1, Pallas kernels, edges(): pl.pallas_call(edge_kernel, out_shape=(jax.ShapeDtypeStruct((PAD, C), BF)...  1.37 us
  transfers between devices with their start and end apart: 5, of which 1 were waited for; matrix products, arithmetic and copies ran while one was open for 0% of the time, Pallas kernels for 17%

profile of v2, /device:TPU:0, one launch (start us, length us, event | category | flops | bytes accessed | tf_op | source)
XLA Modules:
  0.0 39.4 jit_solution(11893683102073309992)
XLA Ops:
  0.0 0.0 copy-start.1
  0.0 0.0 copy-start
  0.0 0.0 collective-permute-start
  0.0 4.0 %collective-permute-start.1 = (bf16[1,10,1024]{2,1,0:T(8,128)(2,1)}, bf16[1,10,1024]{2,1,0:T(8,128)(2,1)S(1)}, u32[]{:S(2)}, u32[]{:S(2)}) collective-permute-start(bf16[1,10,1024]{2,1,0:T(8,128)(2,1)} %s0.1), channel_id=1, source_target_pairs={{0,64},{32,96},{64,0},{96,32},{1,65},{33,97},{65,1},{97,33},{2,66}... | collective-permute-start | bytes 61448 | tf_op jit(solution)/shard_map/ppermute | solution.py:361
  4.1 0.1 collective-permute-start.2
  4.1 0.7 %copy-done.2 = bf16[16,1,3,3,3,3]{0,5,4,3,2,1:T(4,128)(2,1)S(1)} copy-done((bf16[16,1,3,3,3,3]{0,5,4,3,2,1:T(4,128)(2,1)S(1)}, bf16[16,1,3,3,3,3]{0,5,4,3,2,1:T(4,128)(2,1)}, u32[]{:S(2)}) %copy-start.2) | copy-done | bytes 2616
  4.9 0.7 %copy-done.3 = bf16[1,16,3,3,3,3]{1,5,4,3,2,0:T(4,128)(2,1)S(1)} copy-done((bf16[1,16,3,3,3,3]{1,5,4,3,2,0:T(4,128)(2,1)S(1)}, bf16[1,16,3,3,3,3]{1,5,4,3,2,0:T(4,128)(2,1)}, u32[]{:S(2)}) %copy-start.3) | copy-done | bytes 2616
  5.6 0.7 %copy-done.4 = f32[16]{0:T(128)S(1)} copy-done((f32[16]{0:T(128)S(1)}, f32[16]{0:T(128)}, u32[]{:S(2)}) %copy-start.4) | copy-done | bytes 88
  6.3 0.7 %copy-done.5 = s32[8,640]{1,0:T(8,128)S(1)} copy-done((s32[8,640]{1,0:T(8,128)S(1)}, s32[8,640]{1,0:T(8,128)}, u32[]{:S(2)}) %copy-start.5) | copy-done | bytes 20504
  7.0 1.3 %prep.1 = (bf16[640,432]{1,0:T(8,128)(2,1)S(1)}, bf16[368,640]{1,0:T(8,128)(2,1)S(1)}) custom-call(s32[8,640]{1,0:T(8,128)S(1)} %copy-done.5, bf16[3,3,3,3,16]{4,3,2,1,0:T(4,128)(2,1)S(1)} %bitcast.13, f32[1,16]{1,0:T(1,128)S(1)} %bitcast.15, bf16[3,3,3,3,16]{4,3,2,1,0:T(4,128)(2,1)S(1)} %bitcast.14), custom_call_target="tpu_custom_call" | custom-call | flops 3000000000 | bytes 9000000 | tf_op jit(solution)/shard_map/prep/pallas_call | solution.py:135
  9.0 0.0 collective-permute-done.s1
  9.0 0.0 collective-permute-done.1.s2
  9.0 0.1 collective-permute-done.2.s3
  9.1 0.0 copy-done.1
  9.1 0.0 copy-done
  9.1 1.4 %edges.1 = (bf16[48,1024]{1,0:T(8,128)(2,1)S(1)}, bf16[48,1024]{1,0:T(8,128)(2,1)S(1)}, bf16[48,1024]{1,0:T(8,128)(2,1)S(1)}) custom-call(bf16[1,10,1024]{2,1,0:T(8,128)(2,1)S(1)} %copy-done.1, bf16[1,10,1024]{2,1,0:T(8,128)(2,1)S(1)} %collective-permute-done.s1, bf16[1,10,1024]{2,1,0:T(8,128)(2,1)S(1)} %collective-permute-done.1.s2, ...), custom_call_target="tpu_custom_call" | custom-call | flops 2000000000 | bytes 6000000 | tf_op jit(solution)/shard_map/edges/pallas_call | solution.py:173
  10.5 1.6 %collective-permute-start.3 = (bf16[48,1024]{1,0:T(8,128)(2,1)S(1)}, bf16[48,1024]{1,0:T(8,128)(2,1)S(1)}, u32[]{:S(2)}, u32[]{:S(2)}) collective-permute-start(bf16[48,1024]{1,0:T(8,128)(2,1)S(1)} %get-tuple-element.20.hi_ref), channel_id=1, source_target_pairs={{0,1},{1,2},{2,3},{3,4},{4,5},{5,6},{6,7},{7,8},{8,9},{9,10},{10,1... | collective-permute-start | bytes 294920 | tf_op jit(solution)/shard_map/ppermute | solution.py:370
  12.1 4.8 %collective-permute-start.4 = (bf16[48,1024]{1,0:T(8,128)(2,1)S(1)}, bf16[48,1024]{1,0:T(8,128)(2,1)S(1)}, u32[]{:S(2)}, u32[]{:S(2)}) collective-permute-start(bf16[48,1024]{1,0:T(8,128)(2,1)S(1)} %get-tuple-element.19.lo_ref), channel_id=1, source_target_pairs={{1,0},{2,1},{3,2},{4,3},{5,4},{6,5},{7,6},{8,7},{9,8},{10,9},{11,1... | collective-permute-start | bytes 294920 | tf_op jit(solution)/shard_map/ppermute | solution.py:371
  16.8 5.5 %inner.1 = (f32[10,4,512]{2,1,0:T(4,128)S(1)}, f32[4,512]{1,0:T(4,128)S(1)}, f32[10,512]{1,0:T(8,128)S(1)}, f32[4,120,512]{2,1,0:T(8,128)S(1)}) custom-call(bf16[48,1024]{1,0:T(8,128)(2,1)S(1)} %get-tuple-element.18.feats_ref, bf16[8,512,1024]{2,1,0:T(8,128)(2,1)S(1)} %copy-done, bf16[48,1024]{1,0:T(8,128)(2,1)S(1)} %get-tuple-element.19.lo_ref, ...), custom_call_target="tpu_custom_call" | custom-call | flops 8000000000 | bytes 24000000 | tf_op jit(solution)/shard_map/inner/pallas_call | solution.py:254
  22.4 0.0 collective-permute-done.3.before_ref
  22.4 0.0 collective-permute-done.4.after_ref
  22.4 3.1 %outer.1 = (f32[10,4,512]{2,1,0:T(4,128)S(1)}, f32[4,512]{1,0:T(4,128)S(1)}, f32[32,128]{1,0:T(8,128)S(1)}) custom-call(bf16[48,1024]{1,0:T(8,128)(2,1)S(1)} %get-tuple-element.19.lo_ref, bf16[48,1024]{1,0:T(8,128)(2,1)S(1)} %get-tuple-element.20.hi_ref, bf16[48,1024]{1,0:T(8,128)(2,1)S(1)} %collective-permute-done.3.before_ref, ...), custom_call_target="tpu_custom_call" | custom-call | flops 4000000000 | bytes 12000000 | tf_op jit(solution)/shard_map/outer/pallas_call | solution.py:315
  25.5 13.1 %all_to_all.11 = f32[32,1,128]{2,1,0:T(1,128)S(1)} all-to-all(f32[32,1,128]{2,1,0:T(1,128)S(1)} %bitcast.12), channel_id=1, replica_groups=mesh['aa'=4,'ba'=32] {'ba'}, dimensions={0} | all-to-all | bytes 32768 | tf_op jit(solution)/shard_map/all_to_all | solution.py:374
  38.6 0.8 %finish.1 = f32[1,10,8,512]{3,2,1,0:T(8,128)} custom-call(f32[10,4,512]{2,1,0:T(4,128)S(1)} %get-tuple-element.22.s1_ref, f32[4,512]{1,0:T(4,128)S(1)} %get-tuple-element.23.bt1_ref, f32[10,4,512]{2,1,0:T(4,128)S(1)} %get-tuple-element.26.s2_ref, f32[4,512]{1,0:T(4,128)S(1)} %get-tuple-element.27.bt2_ref, f32[32,128]{1,0:T(8,128)S(1)} %bitcast.11), custom_call_target="tpu_custom_call" | custom-call | tf_op jit(solution)/shard_map/finish/pallas_call | solution.py:347
  (4 shorter events, 0.0 us)
Async XLA Ops:
  0.0 9.1 %copy-start.1 = (bf16[1,10,1024]{2,1,0:T(8,128)(2,1)S(1)}, bf16[1,10,1024]{2,1,0:T(8,128)(2,1)}, u32[]{:S(2)}) copy-start(bf16[1,10,1024]{2,1,0:T(8,128)(2,1)} %s0.1) | copy-start | bytes 61444
  0.0 9.1 %copy-start = (bf16[8,512,1024]{2,1,0:T(8,128)(2,1)S(1)}, bf16[8,512,1024]{2,1,0:T(8,128)(2,1)}, u32[]{:S(2)}) copy-start(bf16[8,512,1024]{2,1,0:T(8,128)(2,1)} %target_ref.3) | copy-start | bytes 25165828
  0.0 9.0 %collective-permute-start = (bf16[1,10,1024]{2,1,0:T(8,128)(2,1)}, bf16[1,10,1024]{2,1,0:T(8,128)(2,1)S(1)}, u32[]{:S(2)}, u32[]{:S(2)}) collective-permute-start(bf16[1,10,1024]{2,1,0:T(8,128)(2,1)} %s0.1), channel_id=1, source_target_pairs={{0,32},{32,0},{64,96},{96,64},{1,33},{33,1},{65,97},{97,65},{2,34}... | collective-permute-start | bytes 61448 | tf_op jit(solution)/shard_map/ppermute | solution.py:361
  0.0 9.0 %collective-permute-start.1 = (bf16[1,10,1024]{2,1,0:T(8,128)(2,1)}, bf16[1,10,1024]{2,1,0:T(8,128)(2,1)S(1)}, u32[]{:S(2)}, u32[]{:S(2)}) collective-permute-start(bf16[1,10,1024]{2,1,0:T(8,128)(2,1)} %s0.1), channel_id=1, source_target_pairs={{0,64},{32,96},{64,0},{96,32},{1,65},{33,97},{65,1},{97,33},{2,66}... | collective-permute-start | bytes 61448 | tf_op jit(solution)/shard_map/ppermute | solution.py:361
  4.1 5.1 %collective-permute-start.2 = (bf16[1,10,1024]{2,1,0:T(8,128)(2,1)}, bf16[1,10,1024]{2,1,0:T(8,128)(2,1)S(1)}, u32[]{:S(2)}, u32[]{:S(2)}) collective-permute-start(bf16[1,10,1024]{2,1,0:T(8,128)(2,1)} %s0.1), channel_id=1, source_target_pairs={{0,96},{32,64},{64,32},{96,0},{1,97},{33,65},{65,33},{97,1},{2,98}... | collective-permute-start | bytes 61448 | tf_op jit(solution)/shard_map/ppermute | solution.py:361
  4.1 0.7 %copy-start.2 = (bf16[16,1,3,3,3,3]{0,5,4,3,2,1:T(4,128)(2,1)S(1)}, bf16[16,1,3,3,3,3]{0,5,4,3,2,1:T(4,128)(2,1)}, u32[]{:S(2)}) copy-start(bf16[16,1,3,3,3,3]{0,5,4,3,2,1:T(4,128)(2,1)} %param.9) | copy-start | bytes 7780
  4.9 0.7 %copy-start.3 = (bf16[1,16,3,3,3,3]{1,5,4,3,2,0:T(4,128)(2,1)S(1)}, bf16[1,16,3,3,3,3]{1,5,4,3,2,0:T(4,128)(2,1)}, u32[]{:S(2)}) copy-start(bf16[1,16,3,3,3,3]{1,5,4,3,2,0:T(4,128)(2,1)} %param.11) | copy-start | bytes 7780
  5.6 0.7 %copy-start.4 = (f32[16]{0:T(128)S(1)}, f32[16]{0:T(128)}, u32[]{:S(2)}) copy-start(f32[16]{0:T(128)} %param.10) | copy-start | bytes 196
  6.3 0.7 %copy-start.5 = (s32[8,640]{1,0:T(8,128)S(1)}, s32[8,640]{1,0:T(8,128)}, u32[]{:S(2)}) copy-start(s32[8,640]{1,0:T(8,128)} %constant.2.clone.table_ref) | copy-start | bytes 61444
  10.5 11.9 %collective-permute-start.3 = (bf16[48,1024]{1,0:T(8,128)(2,1)S(1)}, bf16[48,1024]{1,0:T(8,128)(2,1)S(1)}, u32[]{:S(2)}, u32[]{:S(2)}) collective-permute-start(bf16[48,1024]{1,0:T(8,128)(2,1)S(1)} %get-tuple-element.20.hi_ref), channel_id=1, source_target_pairs={{0,1},{1,2},{2,3},{3,4},{4,5},{5,6},{6,7},{7,8},{8,9},{9,10},{10,1... | collective-permute-start | bytes 294920 | tf_op jit(solution)/shard_map/ppermute | solution.py:370
  12.1 10.3 %collective-permute-start.4 = (bf16[48,1024]{1,0:T(8,128)(2,1)S(1)}, bf16[48,1024]{1,0:T(8,128)(2,1)S(1)}, u32[]{:S(2)}, u32[]{:S(2)}) collective-permute-start(bf16[48,1024]{1,0:T(8,128)(2,1)S(1)} %get-tuple-element.19.lo_ref), channel_id=1, source_target_pairs={{1,0},{2,1},{3,2},{4,3},{5,4},{6,5},{7,6},{8,7},{9,8},{10,9},{11,1... | collective-permute-start | bytes 294920 | tf_op jit(solution)/shard_map/ppermute | solution.py:371

commit v3 on v2

v3 whole, which is shorter than its diff:
```python
import functools

import jax
import jax.numpy as jnp
from jax import lax
from jax.experimental import pallas as pl
from jax.experimental.pallas import tpu as pltpu
from jax.sharding import PartitionSpec as P

C = 1024
HID = 16
AW = 10
AR = 4
CELLS = AR * AW
PAD = 48
BW = 512
BR = 8
TAPS = 9
K1 = TAPS * PAD
M1 = CELLS * HID
NEAR = 3 * AW * HID
HALF = 24
GROUP = 2 * HALF
M2 = TAPS * GROUP
M3 = 224
EPS = 1e-5
BF = jnp.bfloat16
F32 = jnp.float32
VMEM_LIMIT = 20 * 1024 * 1024


def cost(us):
    return pl.CostEstimate(flops=int(us * 1e9), bytes_accessed=int(us * 3e6), transcendentals=0)


def softplus(v):
    return jnp.maximum(v, 0.0) + jnp.log1p(jnp.exp(-jnp.abs(v)))


def shifted(x, t):
    if t == 1:
        return x
    lane = lax.broadcasted_iota(jnp.int32, x.shape, 1)
    if t == 0:
        return jnp.where(lane == 0, 0.0, pltpu.roll(x, 1, 1))
    return jnp.where(lane == BW - 1, 0.0, pltpu.roll(x, BW - 1, 1))


def rank_of(me, slot):
    return (
        me,
        lax.bitwise_xor(me, 1),
        jnp.where(me < 2, 2, 1),
        jnp.where(me < 2, 3, 0),
    )[slot]


def prep_kernel(
    k1_ref, b1_ref, k2_ref, w1_ref, far1_ref, w2_ref, far2_ref, w2f_ref, far2f_ref, flat_ref
):
    me = lax.axis_index("aa")

    def lines(ref):
        for n in range(27):
            u, v, w = n // 9, n // 3 % 3, n % 3
            flat_ref[3 * n : 3 * n + 3, :] = ref[u, v, w].astype(F32)
        return flat_ref[...].astype(BF)

    col = lax.broadcasted_iota(jnp.int32, (1, K1), 1)
    tap = lax.shift_right_logical(col * 1366, 16)
    place = col - tap * PAD
    rank = lax.shift_right_logical(place * 6554, 16)
    cell = lax.bitwise_xor(rank, me) * AW + place - rank * AW
    cell = jnp.where(place < CELLS, cell, -1000)
    slot = jnp.where((tap == 4) & (place >= CELLS), place - CELLS, -1000)
    weight = lines(k1_ref)
    row_id = lax.broadcasted_iota(jnp.int32, (81, K1), 0)
    spread = []
    for uv in range(9):
        pick = jnp.where(row_id == uv * 9 + tap, 1.0, 0.0).astype(BF)
        spread.append(
            lax.dot_general(weight, pick, (((0,), (0,)), ((), ())), preferred_element_type=F32)
        )
    square = (HID, HID)
    on = lax.broadcasted_iota(jnp.int32, square, 0) == lax.broadcasted_iota(jnp.int32, square, 1)
    bias = jnp.sum(jnp.where(on, b1_ref[...], 0.0), axis=1, keepdims=True)
    hi = bias.astype(BF).astype(F32)
    mid = (bias - hi).astype(BF).astype(F32)
    low = bias - hi - mid
    slot16 = jnp.broadcast_to(slot, (HID, K1))
    base = jnp.where(
        slot16 == 0, hi, jnp.where(slot16 == 1, mid, jnp.where(slot16 == 2, low, 0.0))
    )
    cell16 = jnp.broadcast_to(cell, (HID, K1))
    for r in range(AR):
        away = cell16 - rank_of(me, r) * AW
        for j in range(AW):
            block = base
            for u in range(3):
                for v in range(3):
                    if 0 <= j + v - 1 < AW:
                        where = (u - 1) * AW + j + v - 1
                        block = jnp.where(away == where, spread[u * 3 + v], block)
            start = (r * AW + j) * HID
            if start < NEAR:
                w1_ref[start : start + HID, :] = block.astype(BF)
            else:
                far1_ref[start - NEAR : start - NEAR + HID, :] = block.astype(BF)
    col = lax.broadcasted_iota(jnp.int32, (1, M1), 1)
    chan = lax.bitwise_and(col, HID - 1)
    place = lax.shift_right_logical(col, 4)
    slot = lax.shift_right_logical(place * 6554, 16)
    rank = jnp.where(
        slot == 0,
        rank_of(me, 0),
        jnp.where(slot == 1, rank_of(me, 1), jnp.where(slot == 2, rank_of(me, 2), rank_of(me, 3))),
    )
    cell = rank * AW + place - slot * AW
    pick = jnp.where(lax.broadcasted_iota(jnp.int32, (HID, M1), 0) == chan, 1.0, 0.0).astype(BF)
    rows = jnp.dot(lines(k2_ref), pick, preferred_element_type=F32)
    for first in (0, 2):
        line_id = lax.broadcasted_iota(jnp.int32, (HALF, M1), 0)
        upper = line_id >= AW
        own_col = line_id - jnp.where(upper, AW, 0)
        own = jnp.where(upper, rank_of(me, first + 1), rank_of(me, first)) * AW + own_col
        gap = jnp.where(line_id < 2 * AW, cell - own, 1000)
        gaps = [
            jnp.where(own_col >= 1, gap, 1000),
            gap,
            jnp.where(own_col <= AW - 2, gap, 1000),
        ]
        for st in range(9):
            block = jnp.zeros((HALF, M1), F32)
            for u in range(3):
                for v in range(3):
                    n = (u * 3 + v) * 9 + st
                    block = jnp.where(gaps[v] == (u - 1) * AW + v - 1, rows[n : n + 1, :], block)
            start = st * GROUP + first // 2 * HALF
            w2f_ref[start : start + HALF, :] = block
            if first == 2:
                far2f_ref[st * HALF : (st + 1) * HALF, :] = block[:, NEAR:M1]
    far2f_ref[TAPS * HALF : M3, :] = jnp.zeros((M3 - TAPS * HALF, M1 - NEAR), F32)
    w2_ref[...] = w2f_ref[:, :NEAR].astype(BF)
    far2_ref[...] = far2f_ref[...].astype(BF)


def prep(k1, b1, k2):
    vm = pl.BlockSpec(memory_space=pltpu.VMEM)
    return pl.pallas_call(
        prep_kernel,
        out_shape=(
            jax.ShapeDtypeStruct((NEAR, K1), BF),
            jax.ShapeDtypeStruct((M1 - NEAR, K1), BF),
            jax.ShapeDtypeStruct((M2, NEAR), BF),
            jax.ShapeDtypeStruct((M3, M1 - NEAR), BF),
        ),
        in_specs=[vm] * 3,
        out_specs=(vm,) * 4,
        scratch_shapes=[
            pltpu.VMEM((M2, M1), F32),
            pltpu.VMEM((M3, M1 - NEAR), F32),
            pltpu.VMEM((81, HID), F32),
        ],
        compiler_params=pltpu.CompilerParams(vmem_limit_bytes=VMEM_LIMIT),
        cost_estimate=cost(3.0),
        name="prep",
    )(k1, b1, k2)


def correlation(feats, block):
    product = lax.dot_general(
        feats, block, (((1,), (1,)), ((), ())), preferred_element_type=F32
    )
    value = (product * C ** (-0.5)).astype(BF).astype(F32)
    row = lax.broadcasted_iota(jnp.int32, value.shape, 0)
    return jnp.where(row >= CELLS, 1.0, value)


def edge_kernel(s0, s1, s2, s3, target_ref, w1_ref, feats_ref, lo_ref, hi_ref, stage):
    for n, ref in enumerate((s0, s1, s2, s3)):
        stage[n * AW : (n + 1) * AW, :] = ref[0].astype(F32)
    stage[CELLS:PAD, :] = jnp.zeros((PAD - CELLS, C), F32)
    feats = stage[...].astype(BF)
    feats_ref[...] = feats
    for ref, first in ((lo_ref, 0), (hi_ref, BR - 2)):
        for n in range(2):
            ref[:, n * BW : (n + 1) * BW] = correlation(feats, target_ref[first + n]).astype(BF)


def edges(sources, target, w1):
    vm = pl.BlockSpec(memory_space=pltpu.VMEM)
    edge = jax.ShapeDtypeStruct((PAD, 2 * BW), BF)
    return pl.pallas_call(
        edge_kernel,
        out_shape=(jax.ShapeDtypeStruct((PAD, C), BF), edge, edge),
        in_specs=[vm] * 5 + [pl.BlockSpec(memory_space=pl.ANY)],
        out_specs=(vm, vm, vm),
        scratch_shapes=[pltpu.VMEM((PAD, C), F32)],
        compiler_params=pltpu.CompilerParams(vmem_limit_bytes=VMEM_LIMIT),
        cost_estimate=cost(2.0),
        name="edges",
    )(*sources, target, w1)


def three_shifts(value):
    return jnp.concatenate([shifted(value, t).astype(BF) for t in range(3)], axis=0)


def hidden_row(w1, parts, drop=None):
    x = jnp.concatenate(parts, axis=0)
    value = jnp.maximum(jnp.dot(w1, x, preferred_element_type=F32), 0.0)
    if drop is not None:
        value = jnp.where(drop, 0.0, value)
    return value.astype(BF)


def spread_row(h, group, w2, hidden, acc, seen, at):
    z = jnp.dot(w2, hidden, preferred_element_type=F32)
    for s in range(3):
        p = h - s
        if 0 <= p < BR:
            part = z[s * 3 * group : (s + 1) * 3 * group, :]
            if p in seen:
                acc[at(p)] = acc[at(p)] + part
            else:
                acc[at(p)] = part
                seen.add(p)


def logit_row(sums, b2):
    return sums[1] + shifted(sums[0], 0) + shifted(sums[2], 2) + b2


def halves(acc, n, half):
    starts = [t * GROUP + half * HALF for t in range(3)]
    return [acc[n, start : start + HALF, :] for start in starts]


def emit_row(n, logits, s_ref, top_ref, best):
    top_ref[n : n + 1, :] = jnp.max(logits[0 : 2 * AW, :], axis=0, keepdims=True)
    mine = logits[0:AW, :]
    score = softplus(mine)
    for j in range(AW):
        s_ref[j, n : n + 1, :] = score[j : j + 1, :]
    return mine if best is None else jnp.maximum(best, mine)


def keep_far(acc, n, far_ref):
    for t, part in enumerate(halves(acc, n[0], 1)):
        far_ref[n[1], t * HALF : (t + 1) * HALF, :] = part


INNER = (2, 3, 4, 5)
OUTER = (0, 1, 6, 7)


def inner_kernel(
    feats_ref, target_ref, lo_ref, hi_ref, w1_ref, w2_ref, b2_ref,
    s_ref, top_ref, best_ref, sums_ref, x, far_ref, acc,
):
    feats = feats_ref[...]
    for n in range(2):
        x[n] = three_shifts(lo_ref[:, n * BW : (n + 1) * BW].astype(F32))
        x[BR - 2 + n] = three_shifts(hi_ref[:, n * BW : (n + 1) * BW].astype(F32))
    for p in INNER:
        x[p] = three_shifts(correlation(feats, target_ref[p]))
    seen = set()
    for h in range(2, BR):
        hidden = hidden_row(w1_ref[...], [x[h - 2], x[h - 1], x[h]])
        spread_row(h, GROUP, w2_ref[...], hidden, acc, seen, lambda p: p)
    best = None
    for n, p in enumerate(INNER):
        best = emit_row(n, logit_row(halves(acc, p, 0), b2_ref[0]), s_ref, top_ref, best)
        keep_far(acc, (p, n), far_ref)
    best_ref[...] = best
    for n, p in enumerate(OUTER):
        sums_ref[n] = acc[p]


def inner(feats, target, lo, hi, w1, w2, b2):
    vm = pl.BlockSpec(memory_space=pltpu.VMEM)
    return pl.pallas_call(
        inner_kernel,
        out_shape=(
            jax.ShapeDtypeStruct((AW, 4, BW), F32),
            jax.ShapeDtypeStruct((4, BW), F32),
            jax.ShapeDtypeStruct((AW, BW), F32),
            jax.ShapeDtypeStruct((4, 3 * GROUP, BW), F32),
            jax.ShapeDtypeStruct((BR, 3 * PAD, BW), BF),
            jax.ShapeDtypeStruct((4, 3 * HALF, BW), F32),
        ),
        in_specs=[vm] * 6 + [pl.BlockSpec(memory_space=pltpu.SMEM)],
        out_specs=(vm,) * 6,
        scratch_shapes=[pltpu.VMEM((BR, 3 * GROUP, BW), F32)],
        compiler_params=pltpu.CompilerParams(vmem_limit_bytes=VMEM_LIMIT),
        cost_estimate=cost(3.0),
        name="inner",
    )(feats, target, lo, hi, w1, w2, b2)


def halo_rows(ref, drop):
    cuts = [ref[:, n * BW : (n + 1) * BW] for n in range(2)]
    return [three_shifts(jnp.where(drop, 0.0, cut.astype(F32))) for cut in cuts]


def outer_kernel(
    blocks, x_ref, before_ref, after_ref, w1_ref, w2_ref, b2_ref, sums_ref, best_ref,
    s_ref, top_ref, mx_ref, far_ref, acc,
):
    place = lax.axis_index("ba")
    first, last = place == 0, place == blocks - 1
    halo = halo_rows(before_ref, first) + halo_rows(after_ref, last)
    for n in range(4):
        acc[n] = sums_ref[n]
    seen = set(OUTER)
    near = [halo[0], halo[1], x_ref[0], x_ref[1]]
    far = [x_ref[BR - 2], x_ref[BR - 1], halo[2], halo[3]]
    for h, parts, drop in (
        (0, near[0:3], first),
        (1, near[1:4], None),
        (BR, far[0:3], None),
        (BR + 1, far[1:4], last),
    ):
        hidden = hidden_row(w1_ref[...], parts, drop)
        spread_row(h, GROUP, w2_ref[...], hidden, acc, seen, OUTER.index)
    best = best_ref[...]
    for n in range(4):
        best = emit_row(n, logit_row(halves(acc, n, 0), b2_ref[0]), s_ref, top_ref, best)
        keep_far(acc, (n, n), far_ref)
    top = jnp.max(best, axis=1, keepdims=True)
    row_id = lax.broadcasted_iota(jnp.int32, (AW, 128), 0)
    lane = lax.broadcasted_iota(jnp.int32, (AW, 128), 1)
    line = jnp.sum(jnp.where(row_id == lane, top, 0.0), axis=0, keepdims=True)
    mx_ref[...] = jnp.broadcast_to(line, mx_ref.shape)


def outer(blocks, x, before, after, w1, w2, b2, sums, best):
    vm = pl.BlockSpec(memory_space=pltpu.VMEM)
    return pl.pallas_call(
        functools.partial(outer_kernel, blocks),
        out_shape=(
            jax.ShapeDtypeStruct((AW, 4, BW), F32),
            jax.ShapeDtypeStruct((4, BW), F32),
            jax.ShapeDtypeStruct((blocks, 128), F32),
            jax.ShapeDtypeStruct((4, 3 * HALF, BW), F32),
        ),
        in_specs=[vm] * 5 + [pl.BlockSpec(memory_space=pltpu.SMEM)] + [vm] * 2,
        out_specs=(vm,) * 4,
        scratch_shapes=[pltpu.VMEM((4, 3 * GROUP, BW), F32)],
        compiler_params=pltpu.CompilerParams(vmem_limit_bytes=VMEM_LIMIT),
        cost_estimate=cost(1),
        name="outer",
    )(x, before, after, w1, w2, b2, sums, best)


def rest_kernel(
    blocks, x_ref, before_ref, after_ref, far1_ref, far2_ref, w1_ref, w2_ref, b2_ref,
    s1_ref, top1_ref, s2_ref, top2_ref, s_ref, q_ref, acc, tops,
):
    place = lax.axis_index("ba")
    first, last = place == 0, place == blocks - 1
    rows = [
        *halo_rows(before_ref, first),
        *(x_ref[p] for p in range(BR)),
        *halo_rows(after_ref, last),
    ]
    for p in range(BR):
        acc[p] = far1_ref[INNER.index(p)] if p in INNER else far2_ref[OUTER.index(p)]
    seen = set(range(BR))
    for h in range(BR + 2):
        drop = first if h == 0 else last if h == BR + 1 else None
        hidden = hidden_row(w1_ref[...], rows[h : h + 3], drop)
        spread_row(h, HALF, w2_ref[...], hidden, acc, seen, lambda p: p)
    for p in range(BR):
        sums = [acc[p, t * HALF : (t + 1) * HALF, :] for t in range(3)]
        logits = logit_row(sums, b2_ref[0])
        top = jnp.max(logits[0 : 2 * AW, :], axis=0, keepdims=True)
        ref, n = (top1_ref, INNER.index(p)) if p in INNER else (top2_ref, OUTER.index(p))
        tops[p : p + 1, :] = jnp.maximum(top, ref[n : n + 1, :])
    best = softplus(tops[...]) + EPS
    for j in range(AW):
        s = jnp.concatenate([s2_ref[j, 0:2], s1_ref[j], s2_ref[j, 2:4]], axis=0)
        s_ref[j] = s
        q_ref[j] = s * (s / best)


def rest(blocks, x, before, after, far1, far2, w1, w2, b2, s1, top1, s2, top2):
    vm = pl.BlockSpec(memory_space=pltpu.VMEM)
    full = jax.ShapeDtypeStruct((AW, BR, BW), F32)
    return pl.pallas_call(
        functools.partial(rest_kernel, blocks),
        out_shape=(full, full),
        in_specs=[vm] * 7 + [pl.BlockSpec(memory_space=pltpu.SMEM)] + [vm] * 4,
        out_specs=(vm, vm),
        scratch_shapes=[pltpu.VMEM((BR, 3 * HALF, BW), F32), pltpu.VMEM((BR, BW), F32)],
        compiler_params=pltpu.CompilerParams(vmem_limit_bytes=VMEM_LIMIT),
        cost_estimate=cost(1),
        name="rest",
    )(x, before, after, far1, far2, w1, w2, b2, s1, top1, s2, top2)


def final_kernel(s_ref, q_ref, mx_ref, out_ref):
    top = softplus(jnp.max(mx_ref[...], axis=0, keepdims=True))
    for j in range(AW):
        out_ref[0, j] = q_ref[j] * (s_ref[j] / (top[:, j : j + 1] + EPS))


def finish(s, q, mx):
    vm = pl.BlockSpec(memory_space=pltpu.VMEM)
    return pl.pallas_call(
        final_kernel,
        out_shape=jax.ShapeDtypeStruct((1, AW, BR, BW), F32),
        in_specs=[vm] * 3,
        out_specs=vm,
        compiler_params=pltpu.CompilerParams(vmem_limit_bytes=4 * 1024 * 1024),
        name="finish",
    )(s, q, mx)


def per_device(source, target, first_kernel, first_bias, second_kernel, second_bias):
    blocks = lax.axis_size("ba")
    size = lax.axis_size("aa")
    sources = [source] + [
        lax.ppermute(source, "aa", [(i, i ^ k) for i in range(size)]) for k in range(1, size)
    ]
    w1, w1_far, w2, w2_far = prep(
        jnp.transpose(first_kernel[:, 0], (1, 2, 3, 4, 0)),
        first_bias[None, :],
        jnp.transpose(second_kernel[0], (1, 2, 3, 4, 0)),
    )
    feats, lo, hi = edges(sources, target, w1)
    up = [(i, (i + 1) % blocks) for i in range(blocks)]
    before = lax.ppermute(hi, "ba", up)
    after = lax.ppermute(lo, "ba", [(j, i) for i, j in up])
    s1, top1, best, sums, x, far1 = inner(feats, target, lo, hi, w1, w2, second_bias)
    s2, top2, mx, far2 = outer(
        blocks, x, before, after, w1, w2, second_bias, sums, best
    )
    mx = lax.all_to_all(mx, "ba", 0, 0, tiled=True)
    s, q = rest(
        blocks, x, before, after, far1, far2, w1_far, w2_far, second_bias, s1, top1, s2, top2
    )
    return finish(s, q, mx)


def solution(mesh):
    return jax.shard_map(
        per_device,
        mesh=mesh,
        in_specs=(P("aa", None, None), P("ba", None, None), P(), P(), P(), P()),
        out_specs=P("aa", None, "ba", None),
        check_vma=False,
    )
```

time: 39.7 us -> 42.7 us (1.076)
  blocking collectives: 13.1 us -> 0 us
  waiting for transfers between devices: 0.15 us -> 8.9 us
  starting transfers between devices: 10.4 us -> 14.4 us
  Pallas kernels: 12.1 us -> 15.4 us
  between operations: 0.71 us -> 1.35 us
  local copies, waits for them, and re-layouts: 2.88 us -> 2.45 us
    all_to_all x1 -> x0, blocking collectives: 13.1 us -> none  [per_device(): mx = lax.all_to_all(mx, 'ba', 0, 0, tiled=True)]
    all_to_all x0 -> x1, waiting for transfers between devices: none -> 4.99 us  [per_device(): mx = lax.all_to_all(mx, 'ba', 0, 0, tiled=True)]
    all_to_all x0 -> x1, starting transfers between devices: none -> 4.03 us  [per_device(): mx = lax.all_to_all(mx, 'ba', 0, 0, tiled=True)]
    ppermute x1, waiting for transfers between devices: 0.01 us -> 3.9 us  [per_device(): before = lax.ppermute(hi, 'ba', up)]
    pallas_call x1 -> x2, Pallas kernels: 1.31 us -> 4.98 us  [the longest x1 3.21 us: rest(): pl.pallas_call(functools.partial(rest_kernel, blocks), out_shape=(full, f...]
    ppermute x1, starting transfers between devices: 1.56 us -> 0.01 us  [per_device(): before = lax.ppermute(hi, 'ba', up)]
    ppermute x1, starting transfers between devices: 4.76 us -> 6.26 us  [per_device(): after = lax.ppermute(lo, 'ba', [(j, i) for i, j in up])]
    pallas_call x1, Pallas kernels: 5.55 us -> 4.92 us  [inner(): pl.pallas_call(inner_kernel, out_shape=(jax.ShapeDtypeStruct((AW, 4, BW),...]
  transfers between devices with their start and end apart: 5 -> 6, of which waited for: 1 -> 2; matrix products, arithmetic and copies ran while one was open for 0% -> 0% of each run, Pallas kernels for 17% -> 23%
where the time goes in v3:
time: 42.7 us; the launch traced here: 42.4 us
  Pallas kernels  15.4 us (36%)
  starting transfers between devices  14.4 us (34%)
  waiting for transfers between devices  8.9 us (21%)
  local copies, waits for them, and re-layouts  2.45 us (6%)
  between operations  1.35 us (3%)
    ppermute x1, starting transfers between devices, per_device(): after = lax.ppermute(lo, 'ba', [(j, i) for i, j in up])  6.26 us
    all_to_all x1, waiting for transfers between devices, per_device(): mx = lax.all_to_all(mx, 'ba', 0, 0, tiled=True)  4.99 us
    pallas_call x1, Pallas kernels, inner(): pl.pallas_call(inner_kernel, out_shape=(jax.ShapeDtypeStruct((AW, 4, BW),...  4.92 us
    ppermute x3, starting transfers between devices, per_device(): lax.ppermute(source, 'aa', [(i, i ^ k) for i in range(size)])  4.09 us
    all_to_all x1, starting transfers between devices, per_device(): mx = lax.all_to_all(mx, 'ba', 0, 0, tiled=True)  4.03 us
    ppermute x1, waiting for transfers between devices, per_device(): before = lax.ppermute(hi, 'ba', up)  3.9 us
    pallas_call x1, Pallas kernels, outer(): pl.pallas_call(functools.partial(outer_kernel, blocks), out_shape=(jax.Sh...  3.29 us
    pallas_call x1, Pallas kernels, rest(): pl.pallas_call(functools.partial(rest_kernel, blocks), out_shape=(full, f...  3.21 us
  transfers between devices with their start and end apart: 6, of which 2 were waited for; matrix products, arithmetic and copies ran while one was open for 0% of the time, Pallas kernels for 23%

profile of v3, /device:TPU:0, one launch (start us, length us, event | category | flops | bytes accessed | tf_op | source)
XLA Modules:
  0.0 42.4 jit_solution(12888160370941903971)
XLA Ops:
  0.0 4.0 %collective-permute-start.1 = (bf16[1,10,1024]{2,1,0:T(8,128)(2,1)}, bf16[1,10,1024]{2,1,0:T(8,128)(2,1)S(1)}, u32[]{:S(2)}, u32[]{:S(2)}) collective-permute-start(bf16[1,10,1024]{2,1,0:T(8,128)(2,1)} %s0.1), channel_id=1, source_target_pairs={{0,64},{32,96},{64,0},{96,32},{1,65},{33,97},{65,1},{97,33},{2,66}... | collective-permute-start | bytes 61448 | tf_op jit(solution)/shard_map/ppermute | solution.py:424
  4.0 0.0 collective-permute-start
  4.0 0.1 collective-permute-start.2
  4.1 0.0 copy-start.2
  4.1 0.7 %copy-done.2 = bf16[16,1,3,3,3,3]{0,5,4,3,2,1:T(4,128)(2,1)S(1)} copy-done((bf16[16,1,3,3,3,3]{0,5,4,3,2,1:T(4,128)(2,1)S(1)}, bf16[16,1,3,3,3,3]{0,5,4,3,2,1:T(4,128)(2,1)}, u32[]{:S(2)}) %copy-start.2) | copy-done | bytes 2616
  4.8 0.7 %copy-done.3 = bf16[1,16,3,3,3,3]{1,5,4,3,2,0:T(4,128)(2,1)S(1)} copy-done((bf16[1,16,3,3,3,3]{1,5,4,3,2,0:T(4,128)(2,1)S(1)}, bf16[1,16,3,3,3,3]{1,5,4,3,2,0:T(4,128)(2,1)}, u32[]{:S(2)}) %copy-start.3) | copy-done | bytes 2616
  5.6 0.7 %copy-done.4 = f32[16]{0:T(128)S(1)} copy-done((f32[16]{0:T(128)S(1)}, f32[16]{0:T(128)}, u32[]{:S(2)}) %copy-start.4) | copy-done | bytes 88
  6.2 1.8 %prep.1 = (bf16[480,432]{1,0:T(8,128)(2,1)S(1)}, bf16[160,432]{1,0:T(8,128)(2,1)S(1)}, bf16[432,480]{1,0:T(8,128)(2,1)S(1)}, bf16[224,160]{1,0:T(8,128)(2,1)S(1)}) custom-call(bf16[3,3,3,3,16]{4,3,2,1,0:T(4,128)(2,1)S(1)} %bitcast.12, f32[1,16]{1,0:T(1,128)S(1)} %bitcast.14, bf16[3,3,3,3,16]{4,3,2,1,0:T(4,128)(2,1)S(1)} %bitcast.13), custom_call_target="tpu_custom_call" | custom-call | flops 3000000000 | bytes 9000000 | tf_op jit(solution)/shard_map/prep/pallas_call | solution.py:149
  9.3 0.0 collective-permute-done.1.s2
  9.3 0.0 collective-permute-done.s1
  9.3 0.0 collective-permute-done.2.s3
  9.3 0.3 copy-done
  9.6 0.0 copy-done.1
  9.6 1.4 %edges.1 = (bf16[48,1024]{1,0:T(8,128)(2,1)S(1)}, bf16[48,1024]{1,0:T(8,128)(2,1)S(1)}, bf16[48,1024]{1,0:T(8,128)(2,1)S(1)}) custom-call(bf16[1,10,1024]{2,1,0:T(8,128)(2,1)S(1)} %copy-done.1, bf16[1,10,1024]{2,1,0:T(8,128)(2,1)S(1)} %collective-permute-done.s1, bf16[1,10,1024]{2,1,0:T(8,128)(2,1)S(1)} %collective-permute-done.1.s2, ...), custom_call_target="tpu_custom_call" | custom-call | flops 2000000000 | bytes 6000000 | tf_op jit(solution)/shard_map/edges/pallas_call | solution.py:193
  11.0 6.3 %collective-permute-start.4 = (bf16[48,1024]{1,0:T(8,128)(2,1)S(1)}, bf16[48,1024]{1,0:T(8,128)(2,1)S(1)}, u32[]{:S(2)}, u32[]{:S(2)}) collective-permute-start(bf16[48,1024]{1,0:T(8,128)(2,1)S(1)} %get-tuple-element.26.lo_ref), channel_id=1, source_target_pairs={{1,0},{2,1},{3,2},{4,3},{5,4},{6,5},{7,6},{8,7},{9,8},{10,9},{11,1... | collective-permute-start | bytes 294920 | tf_op jit(solution)/shard_map/ppermute | solution.py:434
  17.3 0.0 collective-permute-start.3
  17.3 4.9 %inner.1 = (f32[10,4,512]{2,1,0:T(4,128)S(1)}, f32[4,512]{1,0:T(4,128)S(1)}, f32[10,512]{1,0:T(8,128)S(1)}, f32[4,144,512]{2,1,0:T(8,128)S(1)}, bf16[8,144,512]{...) custom-call(bf16[48,1024]{1,0:T(8,128)(2,1)S(1)} %get-tuple-element.25.feats_ref, bf16[8,512,1024]{2,1,0:T(8,128)(2,1)S(1)} %copy-done, ...), custom_call_target="tpu_custom_call" | custom-call | flops 3000000000 | bytes 9000000 | tf_op jit(solution)/shard_map/inner/pallas_call | solution.py:282
  22.2 0.0 collective-permute-done.4.after_ref
  22.2 3.9 %collective-permute-done.3.before_ref = bf16[48,1024]{1,0:T(8,128)(2,1)S(1)} collective-permute-done((bf16[48,1024]{1,0:T(8,128)(2,1)S(1)}, bf16[48,1024]{1,0:T(8,128)(2,1)S(1)}, u32[]{:S(2)}, u32[]{:S(2)}) %collective-permute-start.3) | collective-permute-done | bytes 98336 | tf_op jit(solution)/shard_map/ppermute | solution.py:433
  26.1 3.3 %outer.1 = (f32[10,4,512]{2,1,0:T(4,128)S(1)}, f32[4,512]{1,0:T(4,128)S(1)}, f32[32,128]{1,0:T(8,128)}, f32[4,72,512]{2,1,0:T(8,128)S(1)}) custom-call(bf16[8,144,512]{2,1,0:T(8,128)(2,1)S(1)} %get-tuple-element.29.x_ref, bf16[48,1024]{1,0:T(8,128)(2,1)S(1)} %collective-permute-done.3.before_ref, bf16[48,1024]{1,0:T(8,128)(2,1)S(1)} %collective-permute-done.4.after_ref, ...), custom_call_target="tpu_custom_call" | custom-call | flops 1000000000 | bytes 3000000 | tf_op jit(solution)/shard_map/outer/pallas_call | solution.py:339
  29.4 4.0 %all-to-all-start = ((f32[32,1,128]{2,1,0:T(1,128)}), f32[32,1,128]{2,1,0:T(1,128)S(1)}, u32[]{:S(2)}, u32[]{:S(2)}) async-start(f32[32,1,128]{2,1,0:T(1,128)} %bitcast.6), calls=%async_computation | async-start | bytes 32768 | tf_op jit(solution)/shard_map/all_to_all | solution.py:439
  33.4 3.2 %rest.1 = (f32[10,8,512]{2,1,0:T(8,128)S(1)}, f32[10,8,512]{2,1,0:T(8,128)S(1)}) custom-call(bf16[8,144,512]{2,1,0:T(8,128)(2,1)S(1)} %get-tuple-element.29.x_ref, bf16[48,1024]{1,0:T(8,128)(2,1)S(1)} %collective-permute-done.3.before_ref, bf16[48,1024]{1,0:T(8,128)(2,1)S(1)} %collective-permute-done.4.after_ref, ...), custom_call_target="tpu_custom_call" | custom-call | flops 1000000000 | bytes 3000000 | tf_op jit(solution)/shard_map/rest/pallas_call | solution.py:390
  36.7 5.0 %all-to-all-done = f32[32,1,128]{2,1,0:T(1,128)S(1)} async-done(((f32[32,1,128]{2,1,0:T(1,128)}), f32[32,1,128]{2,1,0:T(1,128)S(1)}, u32[]{:S(2)}, u32[]{:S(2)}) %all-to-all-start) | async-done | bytes 16416 | tf_op jit(solution)/shard_map/all_to_all | solution.py:439
  41.7 0.8 %finish.1 = f32[1,10,8,512]{3,2,1,0:T(8,128)} custom-call(f32[10,8,512]{2,1,0:T(8,128)S(1)} %get-tuple-element.40.s_ref, f32[10,8,512]{2,1,0:T(8,128)S(1)} %get-tuple-element.41.q_ref, f32[32,128]{1,0:T(8,128)S(1)} %bitcast.11), custom_call_target="tpu_custom_call" | custom-call | tf_op jit(solution)/shard_map/finish/pallas_call | solution.py:410
  (4 shorter events, 0.0 us)
Async XLA Ops:
  0.0 9.3 %collective-permute-start.1 = (bf16[1,10,1024]{2,1,0:T(8,128)(2,1)}, bf16[1,10,1024]{2,1,0:T(8,128)(2,1)S(1)}, u32[]{:S(2)}, u32[]{:S(2)}) collective-permute-start(bf16[1,10,1024]{2,1,0:T(8,128)(2,1)} %s0.1), channel_id=1, source_target_pairs={{0,64},{32,96},{64,0},{96,32},{1,65},{33,97},{65,1},{97,33},{2,66}... | collective-permute-start | bytes 61448 | tf_op jit(solution)/shard_map/ppermute | solution.py:424
  4.0 5.3 %collective-permute-start = (bf16[1,10,1024]{2,1,0:T(8,128)(2,1)}, bf16[1,10,1024]{2,1,0:T(8,128)(2,1)S(1)}, u32[]{:S(2)}, u32[]{:S(2)}) collective-permute-start(bf16[1,10,1024]{2,1,0:T(8,128)(2,1)} %s0.1), channel_id=1, source_target_pairs={{0,32},{32,0},{64,96},{96,64},{1,33},{33,1},{65,97},{97,65},{2,34}... | collective-permute-start | bytes 61448 | tf_op jit(solution)/shard_map/ppermute | solution.py:424
  4.0 5.4 %collective-permute-start.2 = (bf16[1,10,1024]{2,1,0:T(8,128)(2,1)}, bf16[1,10,1024]{2,1,0:T(8,128)(2,1)S(1)}, u32[]{:S(2)}, u32[]{:S(2)}) collective-permute-start(bf16[1,10,1024]{2,1,0:T(8,128)(2,1)} %s0.1), channel_id=1, source_target_pairs={{0,96},{32,64},{64,32},{96,0},{1,97},{33,65},{65,33},{97,1},{2,98}... | collective-permute-start | bytes 61448 | tf_op jit(solution)/shard_map/ppermute | solution.py:424
  4.1 0.7 %copy-start.2 = (bf16[16,1,3,3,3,3]{0,5,4,3,2,1:T(4,128)(2,1)S(1)}, bf16[16,1,3,3,3,3]{0,5,4,3,2,1:T(4,128)(2,1)}, u32[]{:S(2)}) copy-start(bf16[16,1,3,3,3,3]{0,5,4,3,2,1:T(4,128)(2,1)} %param.8) | copy-start | bytes 7780
  4.8 0.7 %copy-start.3 = (bf16[1,16,3,3,3,3]{1,5,4,3,2,0:T(4,128)(2,1)S(1)}, bf16[1,16,3,3,3,3]{1,5,4,3,2,0:T(4,128)(2,1)}, u32[]{:S(2)}) copy-start(bf16[1,16,3,3,3,3]{1,5,4,3,2,0:T(4,128)(2,1)} %param.10) | copy-start | bytes 7780
  5.6 0.7 %copy-start.4 = (f32[16]{0:T(128)S(1)}, f32[16]{0:T(128)}, u32[]{:S(2)}) copy-start(f32[16]{0:T(128)} %param.9) | copy-start | bytes 196
  6.2 3.4 %copy-start = (bf16[8,512,1024]{2,1,0:T(8,128)(2,1)S(1)}, bf16[8,512,1024]{2,1,0:T(8,128)(2,1)}, u32[]{:S(2)}) copy-start(bf16[8,512,1024]{2,1,0:T(8,128)(2,1)} %target_ref.3) | copy-start | bytes 25165828
  6.2 3.4 %copy-start.1 = (bf16[1,10,1024]{2,1,0:T(8,128)(2,1)S(1)}, bf16[1,10,1024]{2,1,0:T(8,128)(2,1)}, u32[]{:S(2)}) copy-start(bf16[1,10,1024]{2,1,0:T(8,128)(2,1)} %s0.1) | copy-start | bytes 61444
  11.0 11.2 %collective-permute-start.4 = (bf16[48,1024]{1,0:T(8,128)(2,1)S(1)}, bf16[48,1024]{1,0:T(8,128)(2,1)S(1)}, u32[]{:S(2)}, u32[]{:S(2)}) collective-permute-start(bf16[48,1024]{1,0:T(8,128)(2,1)S(1)} %get-tuple-element.26.lo_ref), channel_id=1, source_target_pairs={{1,0},{2,1},{3,2},{4,3},{5,4},{6,5},{7,6},{8,7},{9,8},{10,9},{11,1... | collective-permute-start | bytes 294920 | tf_op jit(solution)/shard_map/ppermute | solution.py:434
  17.3 8.8 %collective-permute-start.3 = (bf16[48,1024]{1,0:T(8,128)(2,1)S(1)}, bf16[48,1024]{1,0:T(8,128)(2,1)S(1)}, u32[]{:S(2)}, u32[]{:S(2)}) collective-permute-start(bf16[48,1024]{1,0:T(8,128)(2,1)S(1)} %get-tuple-element.27.hi_ref), channel_id=1, source_target_pairs={{0,1},{1,2},{2,3},{3,4},{4,5},{5,6},{6,7},{7,8},{8,9},{9,10},{10,1... | collective-permute-start | bytes 294920 | tf_op jit(solution)/shard_map/ppermute | solution.py:433
  29.4 12.3 %all-to-all-start = ((f32[32,1,128]{2,1,0:T(1,128)}), f32[32,1,128]{2,1,0:T(1,128)S(1)}, u32[]{:S(2)}, u32[]{:S(2)}) async-start(f32[32,1,128]{2,1,0:T(1,128)} %bitcast.6), calls=%async_computation | async-start | bytes 32768 | tf_op jit(solution)/shard_map/all_to_all | solution.py:439

commit v4 on v2

--- a/solution.py
+++ b/solution.py
@@ -2,7 +2,6 @@
 
 import jax
 import jax.numpy as jnp
-import numpy as np
 from jax import lax
 from jax.experimental import pallas as pl
 from jax.experimental.pallas import tpu as pltpu
@@ -13,14 +12,17 @@
 AW = 10
 AR = 4
 CELLS = AR * AW
-PAD = 48
+PAIR = 24
+PAD = 2 * PAIR
 BW = 512
 BR = 8
-TAPS = 9
-K1 = TAPS * PAD
-M1 = CELLS * HID
-M2 = TAPS * CELLS
-M2P = 368
+LINE = 80
+HALF = 3 * LINE
+GAP = 16
+K1 = 2 * (HALF + GAP)
+ROW = AW * HID
+M1 = AR * ROW
+M2 = 3 * CELLS
 EPS = 1e-5
 BF = jnp.bfloat16
 F32 = jnp.float32
@@ -44,18 +46,29 @@
     return jnp.where(lane == BW - 1, 0.0, pltpu.roll(x, BW - 1, 1))
 
 
-def column_tables():
-    table = np.full((8, 640), -1000, np.int32)
-    col = np.arange(K1)
-    cell = col % PAD
-    table[0, :K1] = np.where(cell < CELLS, cell // AW, -1000)
-    table[1, :K1] = np.where(cell < CELLS, cell % AW, 0)
-    table[2, :K1] = col // PAD
-    table[3, :K1] = np.where((col // PAD == 4) & (cell >= CELLS), cell - CELLS, -1000)
-    col = np.arange(M1)
-    table[4] = col // HID
-    table[5] = col % HID
-    return table
+def table_kernel(out_ref):
+    col = lax.broadcasted_iota(jnp.int32, (8, K1 // 2), 1)
+    s = lax.shift_right_logical(col * 820, 16)
+    rest = col - s * LINE
+    t = lax.shift_right_logical(rest * 2731, 16)
+    place = rest - t * PAIR
+    real = (s < 3) & (t < 3)
+    tap = s * 3 + t
+    cell = jnp.where(real & (place < 2 * AW), place, -1000)
+    one = jnp.where(real & (tap == 4) & (place >= 2 * AW), place - 2 * AW, -1000)
+    row = lax.broadcasted_iota(jnp.int32, (8, K1 // 2), 0)
+    out_ref[...] = jnp.where(row == 0, tap, jnp.where(row == 1, cell, one))
+
+
+def tables():
+    return pl.pallas_call(
+        table_kernel,
+        out_shape=jax.ShapeDtypeStruct((8, K1 // 2), jnp.int32),
+        out_specs=pl.BlockSpec(memory_space=pltpu.VMEM),
+        compiler_params=pltpu.CompilerParams(vmem_limit_bytes=4 * 1024 * 1024),
+        cost_estimate=cost(4.0),
+        name="tables",
+    )()
 
 
 def prep_kernel(table_ref, k1_ref, b1_ref, k2_ref, w1_ref, w2_ref, w2f_ref, flat_ref):
@@ -67,21 +80,14 @@
             flat_ref[3 * n : 3 * n + 3, :] = ref[u, v, w].astype(F32)
         return flat_ref[...].astype(BF)
 
-    rank = table_ref[0:1, :K1]
-    real = rank >= 0
-    rank = jnp.where(real, lax.bitwise_xor(jnp.where(real, rank, 0), me), -1000)
-    cell = rank * AW + table_ref[1:2, :K1]
-    tap = table_ref[2:3, :K1]
-    slot = table_ref[3:4, :K1]
+    tap = table_ref[0:1, :]
     weight = lines(k1_ref)
-    row_id = lax.broadcasted_iota(jnp.int32, (81, K1), 0)
+    row_id = lax.broadcasted_iota(jnp.int32, (81, K1 // 2), 0)
     spread = []
     for uv in range(9):
         pick = jnp.where(row_id == uv * 9 + tap, 1.0, 0.0).astype(BF)
         spread.append(
-            lax.dot_general(
-                weight, pick, (((0,), (0,)), ((), ())), preferred_element_type=F32
-            )
+            lax.dot_general(weight, pick, (((0,), (0,)), ((), ())), preferred_element_type=F32)
         )
     square = (HID, HID)
     on = lax.broadcasted_iota(jnp.int32, square, 0) == lax.broadcasted_iota(jnp.int32, square, 1)
@@ -89,31 +95,31 @@
     hi = bias.astype(BF).astype(F32)
     mid = (bias - hi).astype(BF).astype(F32)
     low = bias - hi - mid
-    slot16 = jnp.broadcast_to(slot, (HID, K1))
-    base = jnp.where(
-        slot16 == 0, hi, jnp.where(slot16 == 1, mid, jnp.where(slot16 == 2, low, 0.0))
-    )
-    cell16 = jnp.broadcast_to(cell, (HID, K1))
+    one = jnp.broadcast_to(table_ref[2:3, :], (HID, K1 // 2))
+    base = jnp.where(one == 0, hi, jnp.where(one == 1, mid, jnp.where(one == 2, low, 0.0)))
+    cell = jnp.broadcast_to(table_ref[1:2, :], (HID, K1 // 2))
     for r in range(AR):
         for j in range(AW):
-            block = base
-            for u in range(3):
-                for v in range(3):
-                    if 0 <= r + u - 1 < AR and 0 <= j + v - 1 < AW:
-                        where = (r + u - 1) * AW + j + v - 1
-                        block = jnp.where(cell16 == where, spread[u * 3 + v], block)
-            start = (r * AW + j) * HID
-            w1_ref[start : start + HID, :] = block.astype(BF)
-    chan = table_ref[5:6, :]
-    pick = jnp.where(
-        lax.broadcasted_iota(jnp.int32, (HID, M1), 0) == chan, 1.0, 0.0
-    ).astype(BF)
+            for half in range(2):
+                block = base if half == r // 3 else jnp.zeros_like(base)
+                for u in range(3):
+                    for v in range(3):
+                        i = r + u - 1
+                        if i // 2 == half and 0 <= j + v - 1 < AW:
+                            where = i % 2 * AW + j + v - 1
+                            block = jnp.where(cell == where, spread[u * 3 + v], block)
+                start = (r * AW + j) * HID
+                cut = slice(half * (K1 // 2), (half + 1) * (K1 // 2))
+                w1_ref[start : start + HID, cut] = block.astype(BF)
+    col = lax.broadcasted_iota(jnp.int32, (1, M1), 1)
+    chan = lax.bitwise_and(col, HID - 1)
+    pick = jnp.where(lax.broadcasted_iota(jnp.int32, (HID, M1), 0) == chan, 1.0, 0.0).astype(BF)
     rows = jnp.dot(lines(k2_ref), pick, preferred_element_type=F32)
     own = lax.broadcasted_iota(jnp.int32, (CELLS, M1), 0)
     own_row = jnp.where(own >= 10, 1, 0) + jnp.where(own >= 20, 1, 0) + jnp.where(own >= 30, 1, 0)
     own_col = own - own_row * AW
     own_cell = lax.bitwise_xor(own_row, me) * AW + own_col
-    gap = table_ref[4:5, :] - own_cell
+    gap = lax.shift_right_logical(col, 4) - own_cell
     gaps = [
         jnp.where(own_col >= 1, gap, 1000),
         gap,
@@ -123,10 +129,10 @@
         block = jnp.zeros((CELLS, M1), F32)
         for u in range(3):
             for v in range(3):
-                line = rows[(u * 3 + v) * 9 + st : (u * 3 + v) * 9 + st + 1, :]
-                block = jnp.where(gaps[v] == (u - 1) * AW + v - 1, line, block)
-        w2f_ref[st * CELLS : (st + 1) * CELLS, :] = block
-    w2f_ref[M2:M2P, :] = jnp.zeros((M2P - M2, M1), F32)
+                n = (u * 3 + v) * 9 + st
+                block = jnp.where(gaps[v] == (u - 1) * AW + v - 1, rows[n : n + 1, :], block)
+        s, t = st // 3, st % 3
+        w2f_ref[t * CELLS : (t + 1) * CELLS, s * M1 : (s + 1) * M1] = block
     w2_ref[...] = w2f_ref[...].astype(BF)
 
 
@@ -136,15 +142,15 @@
         prep_kernel,
         out_shape=(
             jax.ShapeDtypeStruct((M1, K1), BF),
-            jax.ShapeDtypeStruct((M2P, M1), BF),
+            jax.ShapeDtypeStruct((M2, 3 * M1), BF),
         ),
         in_specs=[vm] * 4,
         out_specs=(vm, vm),
-        scratch_shapes=[pltpu.VMEM((M2P, M1), F32), pltpu.VMEM((81, HID), F32)],
+        scratch_shapes=[pltpu.VMEM((M2, 3 * M1), F32), pltpu.VMEM((81, HID), F32)],
         compiler_params=pltpu.CompilerParams(vmem_limit_bytes=VMEM_LIMIT),
-        cost_estimate=cost(3.0),
+        cost_estimate=cost(2.0),
         name="prep",
-    )(column_tables(), k1, b1, k2)
+    )(tables(), k1, b1, k2)
 
 
 def correlation(feats, block):
@@ -153,13 +159,20 @@
     )
     value = (product * C ** (-0.5)).astype(BF).astype(F32)
     row = lax.broadcasted_iota(jnp.int32, value.shape, 0)
-    return jnp.where(row >= CELLS, 1.0, value)
+    filler = (row >= PAD - 4) | ((row >= PAIR - 4) & (row < PAIR))
+    return jnp.where(filler, 1.0, value)
 
 
 def edge_kernel(s0, s1, s2, s3, target_ref, w1_ref, feats_ref, lo_ref, hi_ref, stage):
-    for n, ref in enumerate((s0, s1, s2, s3)):
-        stage[n * AW : (n + 1) * AW, :] = ref[0].astype(F32)
-    stage[CELLS:PAD, :] = jnp.zeros((PAD - CELLS, C), F32)
+    me = lax.axis_index("aa")
+    given = [ref[0].astype(F32) for ref in (s0, s1, s2, s3)]
+    stage[...] = jnp.zeros_like(stage)
+    for n in range(AR):
+        pick = given[n ^ 3]
+        for k in range(3):
+            pick = jnp.where(me == k, given[n ^ k], pick)
+        start = n // 2 * PAIR + n % 2 * AW
+        stage[start : start + AW, :] = pick
     feats = stage[...].astype(BF)
     feats_ref[...] = feats
     for ref, first in ((lo_ref, 0), (hi_ref, BR - 2)):
@@ -183,25 +196,40 @@
 
 
 def three_shifts(value):
-    return jnp.concatenate([shifted(value, t).astype(BF) for t in range(3)], axis=0)
-
-
-def hidden_row(w1, parts):
-    x = jnp.concatenate(parts, axis=0)
-    return jnp.maximum(jnp.dot(w1, x, preferred_element_type=F32), 0.0)
-
-
-def spread_row(h, z, acc, seen, keep):
-    for s in range(3):
-        p = h - s
-        if 0 <= p < BR:
-            part = z[s * 3 * CELLS : (s + 1) * 3 * CELLS, :]
-            at = keep(p)
-            if p in seen:
-                acc[at] = acc[at] + part
-            else:
-                acc[at] = part
-                seen.add(p)
+    moved = [shifted(value, t) for t in range(3)]
+    fill = jnp.zeros((LINE - 3 * PAIR, BW), F32)
+    return jnp.concatenate(
+        [
+            piece
+            for n in range(2)
+            for piece in (*(m[n * PAIR : (n + 1) * PAIR] for m in moved), fill)
+        ],
+        axis=0,
+    ).astype(BF)
+
+
+def hidden_row(w1_ref, parts, out_ref, start, drop=None):
+    low = jnp.concatenate([part[0:LINE] for part in parts], axis=0)
+    high = jnp.concatenate([part[LINE : 2 * LINE] for part in parts], axis=0)
+    both = jnp.concatenate([low, jnp.zeros((GAP, BW), BF), high], axis=0)
+    for first, rows, begin, x in (
+        (0, ROW, 0, low),
+        (ROW, 2 * ROW, 0, both),
+        (3 * ROW, ROW, HALF + GAP, high),
+    ):
+        w1 = w1_ref[first : first + rows, begin : begin + x.shape[0]]
+        value = jnp.maximum(jnp.dot(w1, x, preferred_element_type=F32), 0.0)
+        if drop is not None:
+            value = jnp.where(drop, 0.0, value)
+        out_ref[start + first : start + first + rows, :] = value.astype(BF)
+
+
+def sums_of(w2_ref, hidden_ref, s, first, count):
+    return jnp.dot(
+        w2_ref[:, s * M1 : (s + count) * M1],
+        hidden_ref[first * M1 : (first + count) * M1, :],
+        preferred_element_type=F32,
+    )
 
 
 def logit_row(sums, b2):
@@ -222,13 +250,9 @@
     return mine if best is None else jnp.maximum(best, mine)
 
 
-INNER = (2, 3, 4, 5)
-OUTER = (0, 1, 6, 7)
-
-
 def inner_kernel(
     feats_ref, target_ref, lo_ref, hi_ref, w1_ref, w2_ref, b2_ref,
-    s_ref, bt_ref, best_ref, sums_ref, x, acc,
+    s_ref, bt_ref, best_ref, sums_ref, x, hidden,
 ):
     feats = feats_ref[...]
     for n in range(2):
@@ -236,17 +260,17 @@
         x[BR - 2 + n] = three_shifts(hi_ref[:, n * BW : (n + 1) * BW].astype(F32))
     for p in range(2, BR - 2):
         x[p] = three_shifts(correlation(feats, target_ref[p]))
-    seen = set()
-    for h in range(2, BR):
-        hidden = hidden_row(w1_ref[...], [x[h - 2], x[h - 1], x[h]])
-        z = jnp.dot(w2_ref[...], hidden.astype(BF), preferred_element_type=F32)
-        spread_row(h, z, acc, seen, lambda p: p)
     best = None
-    for n, p in enumerate(INNER):
-        best = emit_row(n, logit_row(acc[p], b2_ref[0]), s_ref, bt_ref, best)
+    for h in range(BR - 2):
+        hidden_row(w1_ref, [x[h], x[h + 1], x[h + 2]], hidden, h * M1)
+        if h >= 2:
+            logits = logit_row(sums_of(w2_ref, hidden, 0, h - 2, 3), b2_ref[0])
+            best = emit_row(h - 2, logits, s_ref, bt_ref, best)
     best_ref[...] = best
-    for n, p in enumerate(OUTER):
-        sums_ref[n] = acc[p]
+    sums_ref[0] = sums_of(w2_ref, hidden, 2, 0, 1)
+    sums_ref[1] = sums_of(w2_ref, hidden, 1, 0, 2)
+    sums_ref[2] = sums_of(w2_ref, hidden, 0, 4, 2)
+    sums_ref[3] = sums_of(w2_ref, hidden, 0, 5, 1)
 
 
 def inner(feats, target, lo, hi, w1, w2, b2):
@@ -262,8 +286,8 @@
         in_specs=[vm] * 6 + [pl.BlockSpec(memory_space=pltpu.SMEM)],
         out_specs=(vm, vm, vm, vm),
         scratch_shapes=[
-            pltpu.VMEM((BR, 3 * PAD, BW), BF),
-            pltpu.VMEM((BR, 3 * CELLS, BW), F32),
+            pltpu.VMEM((BR, 2 * LINE, BW), BF),
+            pltpu.VMEM(((BR - 2) * M1, BW), BF),
         ],
         compiler_params=pltpu.CompilerParams(vmem_limit_bytes=VMEM_LIMIT),
         cost_estimate=cost(8.0),
@@ -273,7 +297,7 @@
 
 def outer_kernel(
     blocks, lo_ref, hi_ref, before_ref, after_ref, w1_ref, w2_ref, b2_ref, sums_ref, best_ref,
-    s_ref, bt_ref, mx_ref, acc,
+    s_ref, bt_ref, mx_ref, hidden,
 ):
     place = lax.axis_index("ba")
     first, last = place == 0, place == blocks - 1
@@ -286,23 +310,14 @@
 
     near = [row(before_ref, 0, first), row(before_ref, 1, first), row(lo_ref, 0), row(lo_ref, 1)]
     far = [row(hi_ref, 0), row(hi_ref, 1), row(after_ref, 0, last), row(after_ref, 1, last)]
-    for n in range(4):
-        acc[n] = sums_ref[n]
-    seen = set(OUTER)
-    for h, parts, drop in (
-        (0, near[0:3], first),
-        (1, near[1:4], None),
-        (BR, far[0:3], None),
-        (BR + 1, far[1:4], last),
-    ):
-        hidden = hidden_row(w1_ref[...], parts)
-        if drop is not None:
-            hidden = jnp.where(drop, 0.0, hidden)
-        z = jnp.dot(w2_ref[...], hidden.astype(BF), preferred_element_type=F32)
-        spread_row(h, z, acc, seen, OUTER.index)
+    hidden_row(w1_ref, near[0:3], hidden, 0, first)
+    hidden_row(w1_ref, near[1:4], hidden, M1)
+    hidden_row(w1_ref, far[0:3], hidden, 2 * M1)
+    hidden_row(w1_ref, far[1:4], hidden, 3 * M1, last)
     best = best_ref[...]
-    for n in range(4):
-        best = emit_row(n, logit_row(acc[n], b2_ref[0]), s_ref, bt_ref, best)
+    for n, (s, begin, count) in enumerate(((0, 0, 2), (0, 1, 1), (2, 2, 1), (1, 2, 2))):
+        sums = sums_ref[n] + sums_of(w2_ref, hidden, s, begin, count)
+        best = emit_row(n, logit_row(sums, b2_ref[0]), s_ref, bt_ref, best)
     top = jnp.max(best, axis=1, keepdims=True)
     row_id = lax.broadcasted_iota(jnp.int32, (AW, 128), 0)
     lane = lax.broadcasted_iota(jnp.int32, (AW, 128), 1)
@@ -321,7 +336,7 @@
         ),
         in_specs=[vm] * 6 + [pl.BlockSpec(memory_space=pltpu.SMEM)] + [vm] * 2,
         out_specs=(vm, vm, vm),
-        scratch_shapes=[pltpu.VMEM((4, 3 * CELLS, BW), F32)],
+        scratch_shapes=[pltpu.VMEM((4 * M1, BW), BF)],
         compiler_params=pltpu.CompilerParams(vmem_limit_bytes=VMEM_LIMIT),
         cost_estimate=cost(4.0),
         name="outer",

time: 39.7 us -> 38.6 us (0.972)
  waiting for transfers between devices: 0.15 us -> 3.37 us
  local copies, waits for them, and re-layouts: 2.88 us -> 0.02 us
  Pallas kernels: 12.1 us -> 9.91 us
  blocking collectives: 13.1 us -> 13.9 us
    ppermute x3, waiting for transfers between devices: 0.14 us -> 3.36 us  [per_device(): lax.ppermute(source, 'aa', [(i, i ^ k) for i in range(size)])]
    unnamed x12 -> x10, local copies, waits for them, and re-layouts: 2.88 us -> 0.02 us
    pallas_call x1, Pallas kernels: 3.12 us -> 2.08 us  [outer(): pl.pallas_call(functools.partial(outer_kernel, blocks), out_shape=(jax.Sh...]
    pallas_call x1, Pallas kernels: 5.55 us -> 4.68 us  [inner(): pl.pallas_call(inner_kernel, out_shape=(jax.ShapeDtypeStruct((AW, 4, BW),...]
    all_to_all x1, blocking collectives: 13.1 us -> 13.9 us  [per_device(): mx = lax.all_to_all(mx, 'ba', 0, 0, tiled=True)]
  transfers between devices with their start and end apart: 5 -> 5, of which waited for: 1 -> 2; matrix products, arithmetic and copies ran while one was open for 0% -> 0% of each run, Pallas kernels for 17% -> 15%
where the time goes in v4:
time: 38.6 us; the launch traced here: 38.4 us
  blocking collectives  13.9 us (36%)
  starting transfers between devices  10.5 us (27%)
  Pallas kernels  9.91 us (26%)
  waiting for transfers between devices  3.37 us (9%)
  between operations  0.74 us (2%)
    all_to_all x1, blocking collectives, per_device(): mx = lax.all_to_all(mx, 'ba', 0, 0, tiled=True)  13.9 us
    ppermute x1, starting transfers between devices, per_device(): after = lax.ppermute(lo, 'ba', [(j, i) for i, j in up])  4.75 us
    pallas_call x1, Pallas kernels, inner(): pl.pallas_call(inner_kernel, out_shape=(jax.ShapeDtypeStruct((AW, 4, BW),...  4.68 us
    ppermute x3, starting transfers between devices, per_device(): lax.ppermute(source, 'aa', [(i, i ^ k) for i in range(size)])  4.2 us
    ppermute x3, waiting for transfers between devices, per_device(): lax.ppermute(source, 'aa', [(i, i ^ k) for i in range(size)])  3.36 us
    pallas_call x1, Pallas kernels, outer(): pl.pallas_call(functools.partial(outer_kernel, blocks), out_shape=(jax.Sh...  2.08 us
    ppermute x1, starting transfers between devices, per_device(): before = lax.ppermute(hi, 'ba', up)  1.56 us
    pallas_call x1, Pallas kernels, edges(): pl.pallas_call(edge_kernel, out_shape=(jax.ShapeDtypeStruct((PAD, C), BF)...  1.39 us
  transfers between devices with their start and end apart: 5, of which 2 were waited for; matrix products, arithmetic and copies ran while one was open for 0% of the time, Pallas kernels for 15%

profile of v4, /device:TPU:0, one launch (start us, length us, event | category | flops | bytes accessed | tf_op | source)
XLA Modules:
  0.0 38.4 jit_solution(17745740596309769814)
XLA Ops:
  0.0 0.0 copy-start.1
  0.0 0.0 copy-start.2
  0.0 0.0 copy-start.4
  0.0 0.1 collective-permute-start
  0.1 4.1 %collective-permute-start.1 = (bf16[1,10,1024]{2,1,0:T(8,128)(2,1)}, bf16[1,10,1024]{2,1,0:T(8,128)(2,1)S(1)}, u32[]{:S(2)}, u32[]{:S(2)}) collective-permute-start(bf16[1,10,1024]{2,1,0:T(8,128)(2,1)} %s0.1), channel_id=1, source_target_pairs={{0,64},{32,96},{64,0},{96,32},{1,65},{33,97},{65,1},{97,33},{2,66}... | collective-permute-start | bytes 61448 | tf_op jit(solution)/shard_map/ppermute | solution.py:376
  4.2 0.1 collective-permute-start.2
  4.2 0.0 copy-done.2
  4.2 0.0 copy-done.4
  4.3 0.0 copy-done.3
  4.3 0.9 %prep.1 = (bf16[640,512]{1,0:T(8,128)(2,1)S(1)}, bf16[120,1920]{1,0:T(8,128)(2,1)S(1)}) custom-call(s32[8,256]{1,0:T(8,128)S(1)} %tables.1.table_ref, bf16[3,3,3,3,16]{4,3,2,1,0:T(4,128)(2,1)S(1)} %bitcast.13, f32[1,16]{1,0:T(1,128)S(1)} %bitcast.15, bf16[3,3,3,3,16]{4,3,2,1,0:T(4,128)(2,1)S(1)} %bitcast.14), custom_call_target="tpu_custom_call" | custom-call | flops 2000000000 | bytes 6000000 | tf_op jit(solution)/shard_map/prep/pallas_call | solution.py:141
  5.9 0.0 collective-permute-done.s1
  5.9 0.5 %collective-permute-done.1.s2 = bf16[1,10,1024]{2,1,0:T(8,128)(2,1)S(1)} collective-permute-done((bf16[1,10,1024]{2,1,0:T(8,128)(2,1)}, bf16[1,10,1024]{2,1,0:T(8,128)(2,1)S(1)}, u32[]{:S(2)}, u32[]{:S(2)}) %collective-permute-start.1) | collective-permute-done | bytes 20512 | tf_op jit(solution)/shard_map/ppermute | solution.py:376
  6.3 2.9 %collective-permute-done.2.s3 = bf16[1,10,1024]{2,1,0:T(8,128)(2,1)S(1)} collective-permute-done((bf16[1,10,1024]{2,1,0:T(8,128)(2,1)}, bf16[1,10,1024]{2,1,0:T(8,128)(2,1)S(1)}, u32[]{:S(2)}, u32[]{:S(2)}) %collective-permute-start.2) | collective-permute-done | bytes 20512 | tf_op jit(solution)/shard_map/ppermute | solution.py:376
  9.2 0.0 copy-done.1
  9.2 0.0 copy-done
  9.2 1.4 %edges.1 = (bf16[48,1024]{1,0:T(8,128)(2,1)S(1)}, bf16[48,1024]{1,0:T(8,128)(2,1)S(1)}, bf16[48,1024]{1,0:T(8,128)(2,1)S(1)}) custom-call(bf16[1,10,1024]{2,1,0:T(8,128)(2,1)S(1)} %copy-done.1, bf16[1,10,1024]{2,1,0:T(8,128)(2,1)S(1)} %collective-permute-done.s1, bf16[1,10,1024]{2,1,0:T(8,128)(2,1)S(1)} %collective-permute-done.1.s2, ...), custom_call_target="tpu_custom_call" | custom-call | flops 2000000000 | bytes 6000000 | tf_op jit(solution)/shard_map/edges/pallas_call | solution.py:186
  10.6 1.6 %collective-permute-start.3 = (bf16[48,1024]{1,0:T(8,128)(2,1)S(1)}, bf16[48,1024]{1,0:T(8,128)(2,1)S(1)}, u32[]{:S(2)}, u32[]{:S(2)}) collective-permute-start(bf16[48,1024]{1,0:T(8,128)(2,1)S(1)} %get-tuple-element.20.hi_ref), channel_id=1, source_target_pairs={{0,1},{1,2},{2,3},{3,4},{4,5},{5,6},{6,7},{7,8},{8,9},{9,10},{10,1... | collective-permute-start | bytes 294920 | tf_op jit(solution)/shard_map/ppermute | solution.py:385
  12.2 4.8 %collective-permute-start.4 = (bf16[48,1024]{1,0:T(8,128)(2,1)S(1)}, bf16[48,1024]{1,0:T(8,128)(2,1)S(1)}, u32[]{:S(2)}, u32[]{:S(2)}) collective-permute-start(bf16[48,1024]{1,0:T(8,128)(2,1)S(1)} %get-tuple-element.19.lo_ref), channel_id=1, source_target_pairs={{1,0},{2,1},{3,2},{4,3},{5,4},{6,5},{7,6},{8,7},{9,8},{10,9},{11,1... | collective-permute-start | bytes 294920 | tf_op jit(solution)/shard_map/ppermute | solution.py:386
  17.0 4.7 %inner.1 = (f32[10,4,512]{2,1,0:T(4,128)S(1)}, f32[4,512]{1,0:T(4,128)S(1)}, f32[10,512]{1,0:T(8,128)S(1)}, f32[4,120,512]{2,1,0:T(8,128)S(1)}) custom-call(bf16[48,1024]{1,0:T(8,128)(2,1)S(1)} %get-tuple-element.18.feats_ref, bf16[8,512,1024]{2,1,0:T(8,128)(2,1)S(1)} %copy-done, bf16[48,1024]{1,0:T(8,128)(2,1)S(1)} %get-tuple-element.19.lo_ref, ...), custom_call_target="tpu_custom_call" | custom-call | flops 8000000000 | bytes 24000000 | tf_op jit(solution)/shard_map/inner/pallas_call | solution.py:278
  21.6 0.0 collective-permute-done.3.before_ref
  21.6 0.0 collective-permute-done.4.after_ref
  21.7 2.1 %outer.1 = (f32[10,4,512]{2,1,0:T(4,128)S(1)}, f32[4,512]{1,0:T(4,128)S(1)}, f32[32,128]{1,0:T(8,128)S(1)}) custom-call(bf16[48,1024]{1,0:T(8,128)(2,1)S(1)} %get-tuple-element.19.lo_ref, bf16[48,1024]{1,0:T(8,128)(2,1)S(1)} %get-tuple-element.20.hi_ref, bf16[48,1024]{1,0:T(8,128)(2,1)S(1)} %collective-permute-done.3.before_ref, ...), custom_call_target="tpu_custom_call" | custom-call | flops 4000000000 | bytes 12000000 | tf_op jit(solution)/shard_map/outer/pallas_call | solution.py:330
  23.7 13.9 %all_to_all.11 = f32[32,1,128]{2,1,0:T(1,128)S(1)} all-to-all(f32[32,1,128]{2,1,0:T(1,128)S(1)} %bitcast.12), channel_id=1, replica_groups=mesh['aa'=4,'ba'=32] {'ba'}, dimensions={0} | all-to-all | bytes 32768 | tf_op jit(solution)/shard_map/all_to_all | solution.py:389
  37.6 0.8 %finish.1 = f32[1,10,8,512]{3,2,1,0:T(8,128)} custom-call(f32[10,4,512]{2,1,0:T(4,128)S(1)} %get-tuple-element.22.s1_ref, f32[4,512]{1,0:T(4,128)S(1)} %get-tuple-element.23.bt1_ref, f32[10,4,512]{2,1,0:T(4,128)S(1)} %get-tuple-element.26.s2_ref, f32[4,512]{1,0:T(4,128)S(1)} %get-tuple-element.27.bt2_ref, f32[32,128]{1,0:T(8,128)S(1)} %bitcast.11), custom_call_target="tpu_custom_call" | custom-call | tf_op jit(solution)/shard_map/finish/pallas_call | solution.py:362
  (3 shorter events, 0.0 us)
Async XLA Ops:
  0.0 9.2 %copy-start.1 = (bf16[1,10,1024]{2,1,0:T(8,128)(2,1)S(1)}, bf16[1,10,1024]{2,1,0:T(8,128)(2,1)}, u32[]{:S(2)}) copy-start(bf16[1,10,1024]{2,1,0:T(8,128)(2,1)} %s0.1) | copy-start | bytes 61444
  0.0 4.2 %copy-start.2 = (bf16[16,1,3,3,3,3]{0,5,4,3,2,1:T(4,128)(2,1)S(1)}, bf16[16,1,3,3,3,3]{0,5,4,3,2,1:T(4,128)(2,1)}, u32[]{:S(2)}) copy-start(bf16[16,1,3,3,3,3]{0,5,4,3,2,1:T(4,128)(2,1)} %param.8) | copy-start | bytes 7780
  0.0 4.2 %copy-start.4 = (f32[16]{0:T(128)S(1)}, f32[16]{0:T(128)}, u32[]{:S(2)}) copy-start(f32[16]{0:T(128)} %param.9) | copy-start | bytes 196
  0.0 4.3 %copy-start.3 = (bf16[1,16,3,3,3,3]{1,5,4,3,2,0:T(4,128)(2,1)S(1)}, bf16[1,16,3,3,3,3]{1,5,4,3,2,0:T(4,128)(2,1)}, u32[]{:S(2)}) copy-start(bf16[1,16,3,3,3,3]{1,5,4,3,2,0:T(4,128)(2,1)} %param.10) | copy-start | bytes 7780
  0.0 9.2 %copy-start = (bf16[8,512,1024]{2,1,0:T(8,128)(2,1)S(1)}, bf16[8,512,1024]{2,1,0:T(8,128)(2,1)}, u32[]{:S(2)}) copy-start(bf16[8,512,1024]{2,1,0:T(8,128)(2,1)} %target_ref.3) | copy-start | bytes 25165828
  0.0 5.9 %collective-permute-start = (bf16[1,10,1024]{2,1,0:T(8,128)(2,1)}, bf16[1,10,1024]{2,1,0:T(8,128)(2,1)S(1)}, u32[]{:S(2)}, u32[]{:S(2)}) collective-permute-start(bf16[1,10,1024]{2,1,0:T(8,128)(2,1)} %s0.1), channel_id=1, source_target_pairs={{0,32},{32,0},{64,96},{96,64},{1,33},{33,1},{65,97},{97,65},{2,34}... | collective-permute-start | bytes 61448 | tf_op jit(solution)/shard_map/ppermute | solution.py:376
  0.1 6.2 %collective-permute-start.1 = (bf16[1,10,1024]{2,1,0:T(8,128)(2,1)}, bf16[1,10,1024]{2,1,0:T(8,128)(2,1)S(1)}, u32[]{:S(2)}, u32[]{:S(2)}) collective-permute-start(bf16[1,10,1024]{2,1,0:T(8,128)(2,1)} %s0.1), channel_id=1, source_target_pairs={{0,64},{32,96},{64,0},{96,32},{1,65},{33,97},{65,1},{97,33},{2,66}... | collective-permute-start | bytes 61448 | tf_op jit(solution)/shard_map/ppermute | solution.py:376
  4.2 5.1 %collective-permute-start.2 = (bf16[1,10,1024]{2,1,0:T(8,128)(2,1)}, bf16[1,10,1024]{2,1,0:T(8,128)(2,1)S(1)}, u32[]{:S(2)}, u32[]{:S(2)}) collective-permute-start(bf16[1,10,1024]{2,1,0:T(8,128)(2,1)} %s0.1), channel_id=1, source_target_pairs={{0,96},{32,64},{64,32},{96,0},{1,97},{33,65},{65,33},{97,1},{2,98}... | collective-permute-start | bytes 61448 | tf_op jit(solution)/shard_map/ppermute | solution.py:376
  10.6 11.0 %collective-permute-start.3 = (bf16[48,1024]{1,0:T(8,128)(2,1)S(1)}, bf16[48,1024]{1,0:T(8,128)(2,1)S(1)}, u32[]{:S(2)}, u32[]{:S(2)}) collective-permute-start(bf16[48,1024]{1,0:T(8,128)(2,1)S(1)} %get-tuple-element.20.hi_ref), channel_id=1, source_target_pairs={{0,1},{1,2},{2,3},{3,4},{4,5},{5,6},{6,7},{7,8},{8,9},{9,10},{10,1... | collective-permute-start | bytes 294920 | tf_op jit(solution)/shard_map/ppermute | solution.py:385
  12.2 9.5 %collective-permute-start.4 = (bf16[48,1024]{1,0:T(8,128)(2,1)S(1)}, bf16[48,1024]{1,0:T(8,128)(2,1)S(1)}, u32[]{:S(2)}, u32[]{:S(2)}) collective-permute-start(bf16[48,1024]{1,0:T(8,128)(2,1)S(1)} %get-tuple-element.19.lo_ref), channel_id=1, source_target_pairs={{1,0},{2,1},{3,2},{4,3},{5,4},{6,5},{7,6},{8,7},{9,8},{10,9},{11,1... | collective-permute-start | bytes 294920 | tf_op jit(solution)/shard_map/ppermute | solution.py:386

commit v5 on v4

--- a/solution.py
+++ b/solution.py
@@ -21,6 +21,7 @@
 GAP = 16
 K1 = 2 * (HALF + GAP)
 ROW = AW * HID
+OWN = BR // 2
 M1 = AR * ROW
 M2 = 3 * CELLS
 EPS = 1e-5
@@ -77,6 +78,7 @@
     def lines(ref):
         for n in range(27):
             u, v, w = n // 9, n // 3 % 3, n % 3
+            w = w if w == 1 else jnp.where(lax.rem(me, 2) == 0, w, 2 - w)
             flat_ref[3 * n : 3 * n + 3, :] = ref[u, v, w].astype(F32)
         return flat_ref[...].astype(BF)
 
@@ -163,7 +165,11 @@
     return jnp.where(filler, 1.0, value)
 
 
-def edge_kernel(s0, s1, s2, s3, target_ref, w1_ref, feats_ref, lo_ref, hi_ref, stage):
+def target_row(target_ref, n):
+    return target_ref[jnp.where(lax.rem(lax.axis_index("aa"), 2) == 0, n, BR - 1 - n)]
+
+
+def edge_kernel(s0, s1, s2, s3, target_ref, w1_ref, feats_ref, edge_ref, stage):
     me = lax.axis_index("aa")
     given = [ref[0].astype(F32) for ref in (s0, s1, s2, s3)]
     stage[...] = jnp.zeros_like(stage)
@@ -175,19 +181,21 @@
         stage[start : start + AW, :] = pick
     feats = stage[...].astype(BF)
     feats_ref[...] = feats
-    for ref, first in ((lo_ref, 0), (hi_ref, BR - 2)):
-        for n in range(2):
-            ref[:, n * BW : (n + 1) * BW] = correlation(feats, target_ref[first + n]).astype(BF)
+    for n in range(2):
+        value = correlation(feats, target_row(target_ref, n))
+        edge_ref[:, n * BW : (n + 1) * BW] = value.astype(BF)
 
 
 def edges(sources, target, w1):
     vm = pl.BlockSpec(memory_space=pltpu.VMEM)
-    edge = jax.ShapeDtypeStruct((PAD, 2 * BW), BF)
     return pl.pallas_call(
         edge_kernel,
-        out_shape=(jax.ShapeDtypeStruct((PAD, C), BF), edge, edge),
+        out_shape=(
+            jax.ShapeDtypeStruct((PAD, C), BF),
+            jax.ShapeDtypeStruct((PAD, 2 * BW), BF),
+        ),
         in_specs=[vm] * 5 + [pl.BlockSpec(memory_space=pl.ANY)],
-        out_specs=(vm, vm, vm),
+        out_specs=(vm, vm),
         scratch_shapes=[pltpu.VMEM((PAD, C), F32)],
         compiler_params=pltpu.CompilerParams(vmem_limit_bytes=VMEM_LIMIT),
         cost_estimate=cost(2.0),
@@ -241,132 +249,134 @@
     )
 
 
-def emit_row(n, logits, s_ref, bt_ref, best):
-    bt_ref[n : n + 1, :] = softplus(jnp.max(logits, axis=0, keepdims=True))
-    mine = logits[0:AW, :]
-    score = softplus(mine)
-    for j in range(AW):
-        s_ref[j, n : n + 1, :] = score[j : j + 1, :]
+def emit_row(logits, out_ref, n, best):
+    mine = logits[0 : 2 * AW, :]
+    out_ref[n, 0 : 2 * AW, :] = softplus(mine)
+    top = jnp.max(logits, axis=0, keepdims=True)
+    out_ref[n, 2 * AW : 2 * AW + 1, :] = softplus(top)
     return mine if best is None else jnp.maximum(best, mine)
 
 
 def inner_kernel(
-    feats_ref, target_ref, lo_ref, hi_ref, w1_ref, w2_ref, b2_ref,
-    s_ref, bt_ref, best_ref, sums_ref, x, hidden,
+    feats_ref, target_ref, edge_ref, w1_ref, w2_ref, b2_ref,
+    ready_ref, best_ref, sums_ref, near_ref, x, hidden,
 ):
     feats = feats_ref[...]
     for n in range(2):
-        x[n] = three_shifts(lo_ref[:, n * BW : (n + 1) * BW].astype(F32))
-        x[BR - 2 + n] = three_shifts(hi_ref[:, n * BW : (n + 1) * BW].astype(F32))
-    for p in range(2, BR - 2):
-        x[p] = three_shifts(correlation(feats, target_ref[p]))
+        near_ref[n] = three_shifts(edge_ref[:, n * BW : (n + 1) * BW].astype(F32))
+    for n in range(2, OWN + 2):
+        x[n - 2] = three_shifts(correlation(feats, target_row(target_ref, n)))
+    rows = [near_ref[0], near_ref[1], *(x[n] for n in range(OWN))]
     best = None
-    for h in range(BR - 2):
-        hidden_row(w1_ref, [x[h], x[h + 1], x[h + 2]], hidden, h * M1)
+    for h in range(OWN):
+        hidden_row(w1_ref, rows[h : h + 3], hidden, h * M1)
         if h >= 2:
             logits = logit_row(sums_of(w2_ref, hidden, 0, h - 2, 3), b2_ref[0])
-            best = emit_row(h - 2, logits, s_ref, bt_ref, best)
+            best = emit_row(logits, ready_ref, h - 2, best)
     best_ref[...] = best
     sums_ref[0] = sums_of(w2_ref, hidden, 2, 0, 1)
     sums_ref[1] = sums_of(w2_ref, hidden, 1, 0, 2)
-    sums_ref[2] = sums_of(w2_ref, hidden, 0, 4, 2)
-    sums_ref[3] = sums_of(w2_ref, hidden, 0, 5, 1)
-
-
-def inner(feats, target, lo, hi, w1, w2, b2):
+
+
+def inner(feats, target, edge, w1, w2, b2):
     vm = pl.BlockSpec(memory_space=pltpu.VMEM)
     return pl.pallas_call(
         inner_kernel,
         out_shape=(
-            jax.ShapeDtypeStruct((AW, 4, BW), F32),
-            jax.ShapeDtypeStruct((4, BW), F32),
-            jax.ShapeDtypeStruct((AW, BW), F32),
-            jax.ShapeDtypeStruct((4, 3 * CELLS, BW), F32),
+            jax.ShapeDtypeStruct((2, PAIR, BW), F32),
+            jax.ShapeDtypeStruct((2 * AW, BW), F32),
+            jax.ShapeDtypeStruct((2, M2, BW), F32),
+            jax.ShapeDtypeStruct((2, 2 * LINE, BW), BF),
         ),
-        in_specs=[vm] * 6 + [pl.BlockSpec(memory_space=pltpu.SMEM)],
-        out_specs=(vm, vm, vm, vm),
+        in_specs=[vm] * 5 + [pl.BlockSpec(memory_space=pltpu.SMEM)],
+        out_specs=(vm,) * 4,
         scratch_shapes=[
-            pltpu.VMEM((BR, 2 * LINE, BW), BF),
-            pltpu.VMEM(((BR - 2) * M1, BW), BF),
+            pltpu.VMEM((OWN, 2 * LINE, BW), BF),
+            pltpu.VMEM((OWN * M1, BW), BF),
         ],
         compiler_params=pltpu.CompilerParams(vmem_limit_bytes=VMEM_LIMIT),
         cost_estimate=cost(8.0),
         name="inner",
-    )(feats, target, lo, hi, w1, w2, b2)
+    )(feats, target, edge, w1, w2, b2)
 
 
 def outer_kernel(
-    blocks, lo_ref, hi_ref, before_ref, after_ref, w1_ref, w2_ref, b2_ref, sums_ref, best_ref,
-    s_ref, bt_ref, mx_ref, hidden,
+    blocks, near_ref, halo_ref, w1_ref, w2_ref, b2_ref, sums_ref, best_ref, inner_ref,
+    out_ref, mx_ref, hidden,
 ):
-    place = lax.axis_index("ba")
-    first, last = place == 0, place == blocks - 1
-
-    def row(ref, n, drop=None):
-        value = ref[:, n * BW : (n + 1) * BW].astype(F32)
-        if drop is not None:
-            value = jnp.where(drop, 0.0, value)
-        return three_shifts(value)
-
-    near = [row(before_ref, 0, first), row(before_ref, 1, first), row(lo_ref, 0), row(lo_ref, 1)]
-    far = [row(hi_ref, 0), row(hi_ref, 1), row(after_ref, 0, last), row(after_ref, 1, last)]
-    hidden_row(w1_ref, near[0:3], hidden, 0, first)
-    hidden_row(w1_ref, near[1:4], hidden, M1)
-    hidden_row(w1_ref, far[0:3], hidden, 2 * M1)
-    hidden_row(w1_ref, far[1:4], hidden, 3 * M1, last)
+    core = lax.rem(lax.axis_index("aa"), 2)
+    outside = lax.axis_index("ba") == jnp.where(core == 0, 0, blocks - 1)
+    rows = [
+        three_shifts(jnp.where(outside, 0.0, halo_ref[:, n * BW : (n + 1) * BW].astype(F32)))
+        for n in (1, 0)
+    ] + [near_ref[0], near_ref[1]]
+    hidden_row(w1_ref, rows[0:3], hidden, 0, outside)
+    hidden_row(w1_ref, rows[1:4], hidden, M1)
     best = best_ref[...]
-    for n, (s, begin, count) in enumerate(((0, 0, 2), (0, 1, 1), (2, 2, 1), (1, 2, 2))):
-        sums = sums_ref[n] + sums_of(w2_ref, hidden, s, begin, count)
-        best = emit_row(n, logit_row(sums, b2_ref[0]), s_ref, bt_ref, best)
+    for n in range(2):
+        sums = sums_ref[n] + sums_of(w2_ref, hidden, 0, n, 2 - n)
+        best = emit_row(logit_row(sums, b2_ref[0]), out_ref, n, best)
+    out_ref[2:OWN] = inner_ref[...]
     top = jnp.max(best, axis=1, keepdims=True)
-    row_id = lax.broadcasted_iota(jnp.int32, (AW, 128), 0)
-    lane = lax.broadcasted_iota(jnp.int32, (AW, 128), 1)
-    line = jnp.sum(jnp.where(row_id == lane, top, 0.0), axis=0, keepdims=True)
-    mx_ref[...] = jnp.broadcast_to(line, mx_ref.shape)
-
-
-def outer(blocks, lo, hi, before, after, w1, w2, b2, sums, best):
+    row_id = lax.broadcasted_iota(jnp.int32, (2 * AW, 128), 0)
+    lane = lax.broadcasted_iota(jnp.int32, (2 * AW, 128), 1)
+    lines = [
+        jnp.sum(jnp.where(row_id - n * AW == lane, top, 0.0), axis=0, keepdims=True)
+        for n in range(2)
+    ]
+    lane = lane[0:1]
+    lines = [jnp.where(lane < AW, line, 0.0) for line in lines]
+    for n in range(2):
+        line = jnp.where(core == n, lines[0], lines[1])
+        mx_ref[n * blocks : (n + 1) * blocks, :] = jnp.broadcast_to(line, (blocks, 128))
+
+
+def outer(blocks, near, halo, w1, w2, b2, sums, best, ready):
     vm = pl.BlockSpec(memory_space=pltpu.VMEM)
     return pl.pallas_call(
         functools.partial(outer_kernel, blocks),
         out_shape=(
-            jax.ShapeDtypeStruct((AW, 4, BW), F32),
-            jax.ShapeDtypeStruct((4, BW), F32),
-            jax.ShapeDtypeStruct((blocks, 128), F32),
+            jax.ShapeDtypeStruct((OWN, PAIR, BW), F32),
+            jax.ShapeDtypeStruct((2 * blocks, 128), F32),
         ),
-        in_specs=[vm] * 6 + [pl.BlockSpec(memory_space=pltpu.SMEM)] + [vm] * 2,
-        out_specs=(vm, vm, vm),
-        scratch_shapes=[pltpu.VMEM((4 * M1, BW), BF)],
+        in_specs=[vm] * 4 + [pl.BlockSpec(memory_space=pltpu.SMEM)] + [vm] * 3,
+        out_specs=(vm, vm),
+        scratch_shapes=[pltpu.VMEM((2 * M1, BW), BF)],
         compiler_params=pltpu.CompilerParams(vmem_limit_bytes=VMEM_LIMIT),
         cost_estimate=cost(4.0),
         name="outer",
-    )(lo, hi, before, after, w1, w2, b2, sums, best)
-
-
-def final_kernel(s1_ref, bt1_ref, s2_ref, bt2_ref, mx_ref, out_ref):
+    )(near, halo, w1, w2, b2, sums, best, ready)
+
+
+def final_kernel(own_ref, other_ref, mx_ref, out_ref):
+    upper = lax.rem(lax.axis_index("aa"), 2) == 0
     top = softplus(jnp.max(mx_ref[...], axis=0, keepdims=True))
-    best1 = bt1_ref[...] + EPS
-    best2 = bt2_ref[...] + EPS
-    for j in range(AW):
-        cell = top[:, j : j + 1] + EPS
-        s = s1_ref[j]
-        out_ref[0, j, 2:6, :] = s * (s / best1) * (s / cell)
-        s = s2_ref[j]
-        both = s * (s / best2) * (s / cell)
-        out_ref[0, j, 0:2, :] = both[0:2]
-        out_ref[0, j, 6:8, :] = both[2:4]
-
-
-def finish(s1, bt1, s2, bt2, mx):
+    row_id = lax.broadcasted_iota(jnp.int32, (AW, 128), 0)
+    lane = lax.broadcasted_iota(jnp.int32, (AW, 128), 1)
+    cell = jnp.sum(jnp.where(row_id == lane, top, 0.0), axis=1, keepdims=True) + EPS
+    for p in range(BR):
+        n = min(p, BR - 1 - p)
+        here = upper if p < OWN else jnp.logical_not(upper)
+        s = jnp.where(here, own_ref[n, 0:AW, :], other_ref[n, AW : 2 * AW, :])
+        best = 2 * AW, 2 * AW + 1
+        best = jnp.where(
+            here, own_ref[n, best[0] : best[1], :], other_ref[n, best[0] : best[1], :]
+        )
+        value = s * (s / (best + EPS)) * (s / cell)
+        for j in range(AW):
+            out_ref[0, j, p : p + 1, :] = value[j : j + 1, :]
+
+
+def finish(own, other, mx):
     vm = pl.BlockSpec(memory_space=pltpu.VMEM)
     return pl.pallas_call(
         final_kernel,
         out_shape=jax.ShapeDtypeStruct((1, AW, BR, BW), F32),
-        in_specs=[vm] * 5,
+        in_specs=[vm] * 3,
         out_specs=vm,
         compiler_params=pltpu.CompilerParams(vmem_limit_bytes=4 * 1024 * 1024),
         name="finish",
-    )(s1, bt1, s2, bt2, mx)
+    )(own, other, mx)
 
 
 def per_device(source, target, first_kernel, first_bias, second_kernel, second_bias):
@@ -380,14 +390,31 @@
         first_bias[None, :],
         jnp.transpose(second_kernel[0], (1, 2, 3, 4, 0)),
     )
-    feats, lo, hi = edges(sources, target, w1)
-    up = [(i, (i + 1) % blocks) for i in range(blocks)]
-    before = lax.ppermute(hi, "ba", up)
-    after = lax.ppermute(lo, "ba", [(j, i) for i, j in up])
-    s1, bt1, best, sums = inner(feats, target, lo, hi, w1, w2, second_bias)
-    s2, bt2, mx = outer(blocks, lo, hi, before, after, w1, w2, second_bias, sums, best)
-    mx = lax.all_to_all(mx, "ba", 0, 0, tiled=True)
-    return finish(s1, bt1, s2, bt2, mx)
+    feats, edge = edges(sources, target, w1)
+    halo = lax.ppermute(
+        edge,
+        ("aa", "ba"),
+        [
+            (a * blocks + i, (a ^ 1) * blocks + (i + 2 * (a % 2) - 1) % blocks)
+            for a in range(size)
+            for i in range(blocks)
+        ],
+    )
+    ready, best, sums, near = inner(feats, target, edge, w1, w2, second_bias)
+    own, mx = outer(blocks, near, halo, w1, w2, second_bias, sums, best, ready)
+    other = lax.ppermute(own, "aa", [(i, i ^ 1) for i in range(size)])
+    mx = lax.all_to_all(
+        mx,
+        ("aa", "ba"),
+        0,
+        0,
+        tiled=True,
+        axis_index_groups=[
+            [(a + c) * blocks + i for c in range(2) for i in range(blocks)]
+            for a in range(0, size, 2)
+        ],
+    )
+    return finish(own, other, mx)
 
 
 def solution(mesh):

time: 38.6 us -> 37.3 us (0.966); the launches traced: 38.4 us -> 36.7 us
  Pallas kernels: 9.91 us -> 7.14 us
  blocking collectives: 13.9 us -> 15.4 us
    all_to_all x1, blocking collectives: 13.9 us -> 15.4 us  [per_device(): lax.all_to_all(mx, ('aa', 'ba'), 0, 0, tiled=True, axis_index_groups=[[(a...]
    pallas_call x1, Pallas kernels: 4.68 us -> 3.31 us  [inner(): pl.pallas_call(inner_kernel, out_shape=(jax.ShapeDtypeStruct((2, PAIR, BW...]
    pallas_call x1, Pallas kernels: 2.08 us -> 1.25 us  [outer(): pl.pallas_call(functools.partial(outer_kernel, blocks), out_shape=(jax.Sh...]
    pallas_call x1, Pallas kernels: 1.39 us -> 0.77 us  [edges(): pl.pallas_call(edge_kernel, out_shape=(jax.ShapeDtypeStruct((PAD, C), BF)...]
  transfers between devices with their start and end apart: 5 -> 5, of which waited for: 2 -> 2; matrix products, arithmetic and copies ran while one was open for 0% -> 0% of each run, Pallas kernels for 15% -> 12%
where the time goes in v5:
time: 37.3 us; the launch traced here: 36.7 us
  blocking collectives  15.4 us (41%)
  starting transfers between devices  10.2 us (27%)
  Pallas kernels  7.14 us (19%)
  waiting for transfers between devices  3.18 us (9%)
  between operations  0.73 us (2%)
    all_to_all x1, blocking collectives, per_device(): lax.all_to_all(mx, ('aa', 'ba'), 0, 0, tiled=True, axis_index_groups=[[(a...  15.4 us
    ppermute x1, starting transfers between devices, per_device(): lax.ppermute(edge, ('aa', 'ba'), [(a * blocks + i, (a ^ 1) * blocks + (i...  5.85 us
    ppermute x3, starting transfers between devices, per_device(): lax.ppermute(source, 'aa', [(i, i ^ k) for i in range(size)])  4.28 us
    pallas_call x1, Pallas kernels, inner(): pl.pallas_call(inner_kernel, out_shape=(jax.ShapeDtypeStruct((2, PAIR, BW...  3.31 us
    ppermute x3, waiting for transfers between devices, per_device(): lax.ppermute(source, 'aa', [(i, i ^ k) for i in range(size)])  3.18 us
    pallas_call x1, Pallas kernels, outer(): pl.pallas_call(functools.partial(outer_kernel, blocks), out_shape=(jax.Sh...  1.25 us
    pallas_call x1, Pallas kernels, prep(): pl.pallas_call(prep_kernel, out_shape=(jax.ShapeDtypeStruct((M1, K1), BF)...  0.95 us
    pallas_call x1, Pallas kernels, finish(): pl.pallas_call(final_kernel, out_shape=jax.ShapeDtypeStruct((1, AW, BR, B...  0.84 us
  transfers between devices with their start and end apart: 5, of which 2 were waited for; matrix products, arithmetic and copies ran while one was open for 0% of the time, Pallas kernels for 12%

profile of v5, /device:TPU:0, one launch (start us, length us, event | category | flops | bytes accessed | tf_op | source)
XLA Modules:
  0.0 36.7 jit_solution(4465902101392554549)
XLA Ops:
  0.0 0.0 copy-start.1
  0.0 0.0 copy-start.3
  0.0 0.0 copy-start.4
  0.0 4.1 %collective-permute-start.1 = (bf16[1,10,1024]{2,1,0:T(8,128)(2,1)}, bf16[1,10,1024]{2,1,0:T(8,128)(2,1)S(1)}, u32[]{:S(2)}, u32[]{:S(2)}) collective-permute-start(bf16[1,10,1024]{2,1,0:T(8,128)(2,1)} %s0.1), channel_id=1, source_target_pairs={{0,64},{32,96},{64,0},{96,32},{1,65},{33,97},{65,1},{97,33},{2,66}... | collective-permute-start | bytes 61448 | tf_op jit(solution)/shard_map/ppermute | solution.py:386
  4.1 0.0 collective-permute-start
  4.1 0.2 collective-permute-start.2
  4.3 0.0 copy-done.3
  4.3 0.0 copy-done.4
  4.3 0.0 copy-done.2
  4.3 1.0 %prep.1 = (bf16[640,512]{1,0:T(8,128)(2,1)S(1)}, bf16[120,1920]{1,0:T(8,128)(2,1)S(1)}) custom-call(s32[8,256]{1,0:T(8,128)S(1)} %tables.1.table_ref, bf16[3,3,3,3,16]{4,3,2,1,0:T(4,128)(2,1)S(1)} %bitcast.13, f32[1,16]{1,0:T(1,128)S(1)} %bitcast.15, bf16[3,3,3,3,16]{4,3,2,1,0:T(4,128)(2,1)S(1)} %bitcast.14), custom_call_target="tpu_custom_call" | custom-call | flops 2000000000 | bytes 6000000 | tf_op jit(solution)/shard_map/prep/pallas_call | solution.py:143
  5.9 0.2 collective-permute-done.1.s2
  6.2 0.0 collective-permute-done.s1
  6.2 3.0 %collective-permute-done.2.s3 = bf16[1,10,1024]{2,1,0:T(8,128)(2,1)S(1)} collective-permute-done((bf16[1,10,1024]{2,1,0:T(8,128)(2,1)}, bf16[1,10,1024]{2,1,0:T(8,128)(2,1)S(1)}, u32[]{:S(2)}, u32[]{:S(2)}) %collective-permute-start.2) | collective-permute-done | bytes 20512 | tf_op jit(solution)/shard_map/ppermute | solution.py:386
  9.1 0.0 copy-done.1
  9.1 0.0 copy-done
  9.1 0.8 %edges.1 = (bf16[48,1024]{1,0:T(8,128)(2,1)S(1)}, bf16[48,1024]{1,0:T(8,128)(2,1)S(1)}) custom-call(bf16[1,10,1024]{2,1,0:T(8,128)(2,1)S(1)} %copy-done.1, bf16[1,10,1024]{2,1,0:T(8,128)(2,1)S(1)} %collective-permute-done.s1, bf16[1,10,1024]{2,1,0:T(8,128)(2,1)S(1)} %collective-permute-done.1.s2, bf16[1,10,1024]{2,1,0:T(8,128)(2,1)S(1)} %collective-permute-done.2.s3, ...), custom_call_target="tpu_custom_call" | custom-call | flops 2000000000 | bytes 6000000 | tf_op jit(solution)/shard_map/edges/pallas_call | solution.py:191
  9.9 5.9 %collective-permute-start.3 = (bf16[48,1024]{1,0:T(8,128)(2,1)S(1)}, bf16[48,1024]{1,0:T(8,128)(2,1)S(1)}, u32[]{:S(2)}, u32[]{:S(2)}) collective-permute-start(bf16[48,1024]{1,0:T(8,128)(2,1)S(1)} %get-tuple-element.17.edge_ref), channel_id=1, source_target_pairs={{0,63},{1,32},{2,33},{3,34},{4,35},{5,36},{6,37},{7,38},{8,39},{9,... | collective-permute-start | bytes 294920 | tf_op jit(solution)/shard_map/ppermute | solution.py:394
  15.8 3.3 %inner.1 = (f32[2,24,512]{2,1,0:T(8,128)S(1)}, f32[20,512]{1,0:T(8,128)S(1)}, f32[2,120,512]{2,1,0:T(8,128)S(1)}, bf16[2,160,512]{2,1,0:T(8,128)(2,1)S(1)}) custom-call(bf16[48,1024]{1,0:T(8,128)(2,1)S(1)} %get-tuple-element.16.feats_ref, bf16[8,512,1024]{2,1,0:T(8,128)(2,1)S(1)} %copy-done, bf16[48,1024]{1,0:T(8,128)(2,1)S(1)} %get-tuple-element.17.edge_ref, ...), custom_call_target="tpu_custom_call" | custom-call | flops 8000000000 | bytes 24000000 | tf_op jit(solution)/shard_map/inner/pallas_call | solution.py:283
  19.1 0.0 collective-permute-done.3.halo_ref
  19.1 1.3 %outer.1 = (f32[4,24,512]{2,1,0:T(8,128)S(1)}, f32[64,128]{1,0:T(8,128)S(1)}) custom-call(bf16[2,160,512]{2,1,0:T(8,128)(2,1)S(1)} %get-tuple-element.19.near_ref, bf16[48,1024]{1,0:T(8,128)(2,1)S(1)} %collective-permute-done.3.halo_ref, bf16[640,512]{1,0:T(8,128)(2,1)S(1)} %get-tuple-element.15.w1_ref, bf16[120,1920]{1,0:T(8,128)(2,1)S(1)} %get-tuple-element.18.w2_ref, ...), custom_call_target="tpu_custom_call" | custom-call | flops 4000000000 | bytes 12000000 | tf_op jit(solution)/shard_map/outer/pallas_call | solution.py:336
  20.3 0.1 collective-permute-start.4
  20.4 15.4 %all_to_all.11 = f32[64,1,128]{2,1,0:T(1,128)S(1)} all-to-all(f32[64,1,128]{2,1,0:T(1,128)S(1)} %bitcast.12), channel_id=1, replica_groups={{0,1,2,3,4,5,6,7,8,9,10,11,12,13,14,15,16,17,18,19,20,21,22,23,24,25,26..., dimensions={0} | all-to-all | bytes 65536 | tf_op jit(solution)/shard_map/all_to_all | solution.py:406
  35.8 0.0 collective-permute-done.4.other_ref
  35.8 0.8 %finish.1 = f32[1,10,8,512]{3,2,1,0:T(8,128)} custom-call(f32[4,24,512]{2,1,0:T(8,128)S(1)} %get-tuple-element.23.own_ref, f32[4,24,512]{2,1,0:T(8,128)S(1)} %collective-permute-done.4.other_ref, f32[64,128]{1,0:T(8,128)S(1)} %bitcast.11), custom_call_target="tpu_custom_call" | custom-call | tf_op jit(solution)/shard_map/finish/pallas_call | solution.py:372
  (3 shorter events, 0.0 us)
Async XLA Ops:
  0.0 9.1 %copy-start.1 = (bf16[1,10,1024]{2,1,0:T(8,128)(2,1)S(1)}, bf16[1,10,1024]{2,1,0:T(8,128)(2,1)}, u32[]{:S(2)}) copy-start(bf16[1,10,1024]{2,1,0:T(8,128)(2,1)} %s0.1) | copy-start | bytes 61444
  0.0 4.3 %copy-start.3 = (bf16[1,16,3,3,3,3]{1,5,4,3,2,0:T(4,128)(2,1)S(1)}, bf16[1,16,3,3,3,3]{1,5,4,3,2,0:T(4,128)(2,1)}, u32[]{:S(2)}) copy-start(bf16[1,16,3,3,3,3]{1,5,4,3,2,0:T(4,128)(2,1)} %param.10) | copy-start | bytes 7780
  0.0 4.3 %copy-start.4 = (f32[16]{0:T(128)S(1)}, f32[16]{0:T(128)}, u32[]{:S(2)}) copy-start(f32[16]{0:T(128)} %param.9) | copy-start | bytes 196
  0.0 4.3 %copy-start.2 = (bf16[16,1,3,3,3,3]{0,5,4,3,2,1:T(4,128)(2,1)S(1)}, bf16[16,1,3,3,3,3]{0,5,4,3,2,1:T(4,128)(2,1)}, u32[]{:S(2)}) copy-start(bf16[16,1,3,3,3,3]{0,5,4,3,2,1:T(4,128)(2,1)} %param.8) | copy-start | bytes 7780
  0.0 9.1 %copy-start = (bf16[8,512,1024]{2,1,0:T(8,128)(2,1)S(1)}, bf16[8,512,1024]{2,1,0:T(8,128)(2,1)}, u32[]{:S(2)}) copy-start(bf16[8,512,1024]{2,1,0:T(8,128)(2,1)} %target_ref.3) | copy-start | bytes 25165828
  0.0 6.2 %collective-permute-start.1 = (bf16[1,10,1024]{2,1,0:T(8,128)(2,1)}, bf16[1,10,1024]{2,1,0:T(8,128)(2,1)S(1)}, u32[]{:S(2)}, u32[]{:S(2)}) collective-permute-start(bf16[1,10,1024]{2,1,0:T(8,128)(2,1)} %s0.1), channel_id=1, source_target_pairs={{0,64},{32,96},{64,0},{96,32},{1,65},{33,97},{65,1},{97,33},{2,66}... | collective-permute-start | bytes 61448 | tf_op jit(solution)/shard_map/ppermute | solution.py:386
  4.1 2.1 %collective-permute-start = (bf16[1,10,1024]{2,1,0:T(8,128)(2,1)}, bf16[1,10,1024]{2,1,0:T(8,128)(2,1)S(1)}, u32[]{:S(2)}, u32[]{:S(2)}) collective-permute-start(bf16[1,10,1024]{2,1,0:T(8,128)(2,1)} %s0.1), channel_id=1, source_target_pairs={{0,32},{32,0},{64,96},{96,64},{1,33},{33,1},{65,97},{97,65},{2,34}... | collective-permute-start | bytes 61448 | tf_op jit(solution)/shard_map/ppermute | solution.py:386
  4.1 5.1 %collective-permute-start.2 = (bf16[1,10,1024]{2,1,0:T(8,128)(2,1)}, bf16[1,10,1024]{2,1,0:T(8,128)(2,1)S(1)}, u32[]{:S(2)}, u32[]{:S(2)}) collective-permute-start(bf16[1,10,1024]{2,1,0:T(8,128)(2,1)} %s0.1), channel_id=1, source_target_pairs={{0,96},{32,64},{64,32},{96,0},{1,97},{33,65},{65,33},{97,1},{2,98}... | collective-permute-start | bytes 61448 | tf_op jit(solution)/shard_map/ppermute | solution.py:386
  9.9 9.2 %collective-permute-start.3 = (bf16[48,1024]{1,0:T(8,128)(2,1)S(1)}, bf16[48,1024]{1,0:T(8,128)(2,1)S(1)}, u32[]{:S(2)}, u32[]{:S(2)}) collective-permute-start(bf16[48,1024]{1,0:T(8,128)(2,1)S(1)} %get-tuple-element.17.edge_ref), channel_id=1, source_target_pairs={{0,63},{1,32},{2,33},{3,34},{4,35},{5,36},{6,37},{7,38},{8,39},{9,... | collective-permute-start | bytes 294920 | tf_op jit(solution)/shard_map/ppermute | solution.py:394
  20.3 15.5 %collective-permute-start.4 = (f32[4,24,512]{2,1,0:T(8,128)S(1)}, f32[4,24,512]{2,1,0:T(8,128)S(1)}, u32[]{:S(2)}, u32[]{:S(2)}) collective-permute-start(f32[4,24,512]{2,1,0:T(8,128)S(1)} %get-tuple-element.23.own_ref), channel_id=1, source_target_pairs={{0,32},{32,0},{64,96},{96,64},{1,33},{33,1},{65,97},{97,65},{2,34}... | collective-permute-start | bytes 589832 | tf_op jit(solution)/shard_map/ppermute | solution.py:405

commit v6 on v5

--- a/solution.py
+++ b/solution.py
@@ -379,6 +379,11 @@
     )(own, other, mx)
 
 
+def neighbour(a, i, blocks):
+    j = i + 2 * (a % 2) - 1
+    return (a ^ 1) * blocks + j if 0 <= j < blocks else a * blocks + i
+
+
 def per_device(source, target, first_kernel, first_bias, second_kernel, second_bias):
     blocks = lax.axis_size("ba")
     size = lax.axis_size("aa")
@@ -395,7 +400,7 @@
         edge,
         ("aa", "ba"),
         [
-            (a * blocks + i, (a ^ 1) * blocks + (i + 2 * (a % 2) - 1) % blocks)
+            (a * blocks + i, neighbour(a, i, blocks))
             for a in range(size)
             for i in range(blocks)
         ],

time: 37.3 us -> 38.1 us (1.021)
  blocking collectives: 15.4 us -> 18.5 us
  starting transfers between devices: 10.2 us -> 7.87 us
    ppermute x1, starting transfers between devices: 5.85 us -> 0.67 us  [per_device(): lax.ppermute(edge, ('aa', 'ba'), [(a * blocks + i, neighbour(a, i, blocks...]
    all_to_all x1, blocking collectives: 15.4 us -> 18.5 us  [per_device(): lax.all_to_all(mx, ('aa', 'ba'), 0, 0, tiled=True, axis_index_groups=[[(a...]
    ppermute x1, starting transfers between devices: 0.08 us -> 2.93 us  [per_device(): other = lax.ppermute(own, 'aa', [(i, i ^ 1) for i in range(size)])]
  transfers between devices with their start and end apart: 5 -> 5, of which waited for: 2 -> 2; matrix products, arithmetic and copies ran while one was open for 0% -> 0% of each run, Pallas kernels for 12% -> 11%
where the time goes in v6:
time: 38.1 us; the launch traced here: 37.5 us
  blocking collectives  18.5 us (49%)
  starting transfers between devices  7.87 us (21%)
  Pallas kernels  7.15 us (19%)
  waiting for transfers between devices  3.18 us (8%)
  between operations  0.73 us (2%)
    all_to_all x1, blocking collectives, per_device(): lax.all_to_all(mx, ('aa', 'ba'), 0, 0, tiled=True, axis_index_groups=[[(a...  18.5 us
    ppermute x3, starting transfers between devices, per_device(): lax.ppermute(source, 'aa', [(i, i ^ k) for i in range(size)])  4.28 us
    pallas_call x1, Pallas kernels, inner(): pl.pallas_call(inner_kernel, out_shape=(jax.ShapeDtypeStruct((2, PAIR, BW...  3.32 us
    ppermute x3, waiting for transfers between devices, per_device(): lax.ppermute(source, 'aa', [(i, i ^ k) for i in range(size)])  3.18 us
    ppermute x1, starting transfers between devices, per_device(): other = lax.ppermute(own, 'aa', [(i, i ^ 1) for i in range(size)])  2.93 us
    pallas_call x1, Pallas kernels, outer(): pl.pallas_call(functools.partial(outer_kernel, blocks), out_shape=(jax.Sh...  1.25 us
    pallas_call x1, Pallas kernels, prep(): pl.pallas_call(prep_kernel, out_shape=(jax.ShapeDtypeStruct((M1, K1), BF)...  0.95 us
    pallas_call x1, Pallas kernels, finish(): pl.pallas_call(final_kernel, out_shape=jax.ShapeDtypeStruct((1, AW, BR, B...  0.84 us
  transfers between devices with their start and end apart: 5, of which 2 were waited for; matrix products, arithmetic and copies ran while one was open for 0% of the time, Pallas kernels for 11%

profile of v6, /device:TPU:0, one launch (start us, length us, event | category | flops | bytes accessed | tf_op | source)
XLA Modules:
  0.0 37.5 jit_solution(2814456664455551285)
XLA Ops:
  0.0 0.0 copy-start.1
  0.0 0.0 copy-start.3
  0.0 0.0 copy-start.4
  0.0 4.1 %collective-permute-start.1 = (bf16[1,10,1024]{2,1,0:T(8,128)(2,1)}, bf16[1,10,1024]{2,1,0:T(8,128)(2,1)S(1)}, u32[]{:S(2)}, u32[]{:S(2)}) collective-permute-start(bf16[1,10,1024]{2,1,0:T(8,128)(2,1)} %s0.1), channel_id=1, source_target_pairs={{0,64},{32,96},{64,0},{96,32},{1,65},{33,97},{65,1},{97,33},{2,66}... | collective-permute-start | bytes 61448 | tf_op jit(solution)/shard_map/ppermute | solution.py:391
  4.1 0.0 collective-permute-start
  4.1 0.2 collective-permute-start.2
  4.3 0.0 copy-done.3
  4.3 0.0 copy-done.4
  4.3 0.0 copy-done.2
  4.3 1.0 %prep.1 = (bf16[640,512]{1,0:T(8,128)(2,1)S(1)}, bf16[120,1920]{1,0:T(8,128)(2,1)S(1)}) custom-call(s32[8,256]{1,0:T(8,128)S(1)} %tables.1.table_ref, bf16[3,3,3,3,16]{4,3,2,1,0:T(4,128)(2,1)S(1)} %bitcast.13, f32[1,16]{1,0:T(1,128)S(1)} %bitcast.15, bf16[3,3,3,3,16]{4,3,2,1,0:T(4,128)(2,1)S(1)} %bitcast.14), custom_call_target="tpu_custom_call" | custom-call | flops 2000000000 | bytes 6000000 | tf_op jit(solution)/shard_map/prep/pallas_call | solution.py:143
  5.9 0.2 collective-permute-done.1.s2
  6.2 0.0 collective-permute-done.s1
  6.2 3.0 %collective-permute-done.2.s3 = bf16[1,10,1024]{2,1,0:T(8,128)(2,1)S(1)} collective-permute-done((bf16[1,10,1024]{2,1,0:T(8,128)(2,1)}, bf16[1,10,1024]{2,1,0:T(8,128)(2,1)S(1)}, u32[]{:S(2)}, u32[]{:S(2)}) %collective-permute-start.2) | collective-permute-done | bytes 20512 | tf_op jit(solution)/shard_map/ppermute | solution.py:391
  9.1 0.0 copy-done.1
  9.1 0.0 copy-done
  9.1 0.8 %edges.1 = (bf16[48,1024]{1,0:T(8,128)(2,1)S(1)}, bf16[48,1024]{1,0:T(8,128)(2,1)S(1)}) custom-call(bf16[1,10,1024]{2,1,0:T(8,128)(2,1)S(1)} %copy-done.1, bf16[1,10,1024]{2,1,0:T(8,128)(2,1)S(1)} %collective-permute-done.s1, bf16[1,10,1024]{2,1,0:T(8,128)(2,1)S(1)} %collective-permute-done.1.s2, bf16[1,10,1024]{2,1,0:T(8,128)(2,1)S(1)} %collective-permute-done.2.s3, ...), custom_call_target="tpu_custom_call" | custom-call | flops 2000000000 | bytes 6000000 | tf_op jit(solution)/shard_map/edges/pallas_call | solution.py:191
  9.9 0.7 %collective-permute-start.3 = (bf16[48,1024]{1,0:T(8,128)(2,1)S(1)}, bf16[48,1024]{1,0:T(8,128)(2,1)S(1)}, u32[]{:S(2)}, u32[]{:S(2)}) collective-permute-start(bf16[48,1024]{1,0:T(8,128)(2,1)S(1)} %get-tuple-element.17.edge_ref), channel_id=1, source_target_pairs={{0,0},{1,32},{2,33},{3,34},{4,35},{5,36},{6,37},{7,38},{8,39},{9,4... | collective-permute-start | bytes 294920 | tf_op jit(solution)/shard_map/ppermute | solution.py:399
  10.6 3.3 %inner.1 = (f32[2,24,512]{2,1,0:T(8,128)S(1)}, f32[20,512]{1,0:T(8,128)S(1)}, f32[2,120,512]{2,1,0:T(8,128)S(1)}, bf16[2,160,512]{2,1,0:T(8,128)(2,1)S(1)}) custom-call(bf16[48,1024]{1,0:T(8,128)(2,1)S(1)} %get-tuple-element.16.feats_ref, bf16[8,512,1024]{2,1,0:T(8,128)(2,1)S(1)} %copy-done, bf16[48,1024]{1,0:T(8,128)(2,1)S(1)} %get-tuple-element.17.edge_ref, ...), custom_call_target="tpu_custom_call" | custom-call | flops 8000000000 | bytes 24000000 | tf_op jit(solution)/shard_map/inner/pallas_call | solution.py:283
  13.9 0.0 collective-permute-done.3.halo_ref
  13.9 1.3 %outer.1 = (f32[4,24,512]{2,1,0:T(8,128)S(1)}, f32[64,128]{1,0:T(8,128)S(1)}) custom-call(bf16[2,160,512]{2,1,0:T(8,128)(2,1)S(1)} %get-tuple-element.19.near_ref, bf16[48,1024]{1,0:T(8,128)(2,1)S(1)} %collective-permute-done.3.halo_ref, bf16[640,512]{1,0:T(8,128)(2,1)S(1)} %get-tuple-element.15.w1_ref, bf16[120,1920]{1,0:T(8,128)(2,1)S(1)} %get-tuple-element.18.w2_ref, ...), custom_call_target="tpu_custom_call" | custom-call | flops 4000000000 | bytes 12000000 | tf_op jit(solution)/shard_map/outer/pallas_call | solution.py:336
  15.2 2.9 %collective-permute-start.4 = (f32[4,24,512]{2,1,0:T(8,128)S(1)}, f32[4,24,512]{2,1,0:T(8,128)S(1)}, u32[]{:S(2)}, u32[]{:S(2)}) collective-permute-start(f32[4,24,512]{2,1,0:T(8,128)S(1)} %get-tuple-element.23.own_ref), channel_id=1, source_target_pairs={{0,32},{32,0},{64,96},{96,64},{1,33},{33,1},{65,97},{97,65},{2,34}... | collective-permute-start | bytes 589832 | tf_op jit(solution)/shard_map/ppermute | solution.py:410
  18.1 18.5 %all_to_all.11 = f32[64,1,128]{2,1,0:T(1,128)S(1)} all-to-all(f32[64,1,128]{2,1,0:T(1,128)S(1)} %bitcast.12), channel_id=1, replica_groups={{0,1,2,3,4,5,6,7,8,9,10,11,12,13,14,15,16,17,18,19,20,21,22,23,24,25,26..., dimensions={0} | all-to-all | bytes 65536 | tf_op jit(solution)/shard_map/all_to_all | solution.py:411
  36.6 0.0 collective-permute-done.4.other_ref
  36.6 0.8 %finish.1 = f32[1,10,8,512]{3,2,1,0:T(8,128)} custom-call(f32[4,24,512]{2,1,0:T(8,128)S(1)} %get-tuple-element.23.own_ref, f32[4,24,512]{2,1,0:T(8,128)S(1)} %collective-permute-done.4.other_ref, f32[64,128]{1,0:T(8,128)S(1)} %bitcast.11), custom_call_target="tpu_custom_call" | custom-call | tf_op jit(solution)/shard_map/finish/pallas_call | solution.py:372
  (3 shorter events, 0.0 us)
Async XLA Ops:
  0.0 9.1 %copy-start.1 = (bf16[1,10,1024]{2,1,0:T(8,128)(2,1)S(1)}, bf16[1,10,1024]{2,1,0:T(8,128)(2,1)}, u32[]{:S(2)}) copy-start(bf16[1,10,1024]{2,1,0:T(8,128)(2,1)} %s0.1) | copy-start | bytes 61444
  0.0 4.3 %copy-start.3 = (bf16[1,16,3,3,3,3]{1,5,4,3,2,0:T(4,128)(2,1)S(1)}, bf16[1,16,3,3,3,3]{1,5,4,3,2,0:T(4,128)(2,1)}, u32[]{:S(2)}) copy-start(bf16[1,16,3,3,3,3]{1,5,4,3,2,0:T(4,128)(2,1)} %param.10) | copy-start | bytes 7780
  0.0 4.3 %copy-start.4 = (f32[16]{0:T(128)S(1)}, f32[16]{0:T(128)}, u32[]{:S(2)}) copy-start(f32[16]{0:T(128)} %param.9) | copy-start | bytes 196
  0.0 4.3 %copy-start.2 = (bf16[16,1,3,3,3,3]{0,5,4,3,2,1:T(4,128)(2,1)S(1)}, bf16[16,1,3,3,3,3]{0,5,4,3,2,1:T(4,128)(2,1)}, u32[]{:S(2)}) copy-start(bf16[16,1,3,3,3,3]{0,5,4,3,2,1:T(4,128)(2,1)} %param.8) | copy-start | bytes 7780
  0.0 9.1 %copy-start = (bf16[8,512,1024]{2,1,0:T(8,128)(2,1)S(1)}, bf16[8,512,1024]{2,1,0:T(8,128)(2,1)}, u32[]{:S(2)}) copy-start(bf16[8,512,1024]{2,1,0:T(8,128)(2,1)} %target_ref.3) | copy-start | bytes 25165828
  0.0 6.2 %collective-permute-start.1 = (bf16[1,10,1024]{2,1,0:T(8,128)(2,1)}, bf16[1,10,1024]{2,1,0:T(8,128)(2,1)S(1)}, u32[]{:S(2)}, u32[]{:S(2)}) collective-permute-start(bf16[1,10,1024]{2,1,0:T(8,128)(2,1)} %s0.1), channel_id=1, source_target_pairs={{0,64},{32,96},{64,0},{96,32},{1,65},{33,97},{65,1},{97,33},{2,66}... | collective-permute-start | bytes 61448 | tf_op jit(solution)/shard_map/ppermute | solution.py:391
  4.1 2.1 %collective-permute-start = (bf16[1,10,1024]{2,1,0:T(8,128)(2,1)}, bf16[1,10,1024]{2,1,0:T(8,128)(2,1)S(1)}, u32[]{:S(2)}, u32[]{:S(2)}) collective-permute-start(bf16[1,10,1024]{2,1,0:T(8,128)(2,1)} %s0.1), channel_id=1, source_target_pairs={{0,32},{32,0},{64,96},{96,64},{1,33},{33,1},{65,97},{97,65},{2,34}... | collective-permute-start | bytes 61448 | tf_op jit(solution)/shard_map/ppermute | solution.py:391
  4.1 5.1 %collective-permute-start.2 = (bf16[1,10,1024]{2,1,0:T(8,128)(2,1)}, bf16[1,10,1024]{2,1,0:T(8,128)(2,1)S(1)}, u32[]{:S(2)}, u32[]{:S(2)}) collective-permute-start(bf16[1,10,1024]{2,1,0:T(8,128)(2,1)} %s0.1), channel_id=1, source_target_pairs={{0,96},{32,64},{64,32},{96,0},{1,97},{33,65},{65,33},{97,1},{2,98}... | collective-permute-start | bytes 61448 | tf_op jit(solution)/shard_map/ppermute | solution.py:391
  9.9 4.0 %collective-permute-start.3 = (bf16[48,1024]{1,0:T(8,128)(2,1)S(1)}, bf16[48,1024]{1,0:T(8,128)(2,1)S(1)}, u32[]{:S(2)}, u32[]{:S(2)}) collective-permute-start(bf16[48,1024]{1,0:T(8,128)(2,1)S(1)} %get-tuple-element.17.edge_ref), channel_id=1, source_target_pairs={{0,0},{1,32},{2,33},{3,34},{4,35},{5,36},{6,37},{7,38},{8,39},{9,4... | collective-permute-start | bytes 294920 | tf_op jit(solution)/shard_map/ppermute | solution.py:399
  15.2 21.4 %collective-permute-start.4 = (f32[4,24,512]{2,1,0:T(8,128)S(1)}, f32[4,24,512]{2,1,0:T(8,128)S(1)}, u32[]{:S(2)}, u32[]{:S(2)}) collective-permute-start(f32[4,24,512]{2,1,0:T(8,128)S(1)} %get-tuple-element.23.own_ref), channel_id=1, source_target_pairs={{0,32},{32,0},{64,96},{96,64},{1,33},{33,1},{65,97},{97,65},{2,34}... | collective-permute-start | bytes 589832 | tf_op jit(solution)/shard_map/ppermute | solution.py:410

commit v7 on v6

--- a/solution.py
+++ b/solution.py
@@ -381,7 +381,7 @@
 
 def neighbour(a, i, blocks):
     j = i + 2 * (a % 2) - 1
-    return (a ^ 1) * blocks + j if 0 <= j < blocks else a * blocks + i
+    return (a ^ 1) * blocks + j if 0 <= j < blocks else (a ^ 2) * blocks + i
 
 
 def per_device(source, target, first_kernel, first_bias, second_kernel, second_bias):

time: 38.1 us -> 36.3 us (0.953)
  waiting for transfers between devices: 3.18 us -> 6.28 us
  starting transfers between devices: 7.87 us -> 5.21 us
  blocking collectives: 18.5 us -> 16.3 us
    ppermute x1, waiting for transfers between devices: 0.01 us -> 3.1 us  [per_device(): lax.ppermute(edge, ('aa', 'ba'), [(a * blocks + i, neighbour(a, i, blocks...]
    ppermute x1, starting transfers between devices: 2.93 us -> 0.08 us  [per_device(): other = lax.ppermute(own, 'aa', [(i, i ^ 1) for i in range(size)])]
    all_to_all x1, blocking collectives: 18.5 us -> 16.3 us  [per_device(): lax.all_to_all(mx, ('aa', 'ba'), 0, 0, tiled=True, axis_index_groups=[[(a...]
  transfers between devices with their start and end apart: 5 -> 5, of which waited for: 2 -> 3; matrix products, arithmetic and copies ran while one was open for 0% -> 0% of each run, Pallas kernels for 11% -> 12%
where the time goes in v7:
time: 36.3 us; the launch traced here: 35.7 us
  blocking collectives  16.3 us (45%)
  Pallas kernels  7.12 us (20%)
  waiting for transfers between devices  6.28 us (17%)
  starting transfers between devices  5.21 us (14%)
  between operations  0.72 us (2%)
    all_to_all x1, blocking collectives, per_device(): lax.all_to_all(mx, ('aa', 'ba'), 0, 0, tiled=True, axis_index_groups=[[(a...  16.3 us
    ppermute x3, starting transfers between devices, per_device(): lax.ppermute(source, 'aa', [(i, i ^ k) for i in range(size)])  4.28 us
    pallas_call x1, Pallas kernels, inner(): pl.pallas_call(inner_kernel, out_shape=(jax.ShapeDtypeStruct((2, PAIR, BW...  3.3 us
    ppermute x3, waiting for transfers between devices, per_device(): lax.ppermute(source, 'aa', [(i, i ^ k) for i in range(size)])  3.18 us
    ppermute x1, waiting for transfers between devices, per_device(): lax.ppermute(edge, ('aa', 'ba'), [(a * blocks + i, neighbour(a, i, blocks...  3.1 us
    pallas_call x1, Pallas kernels, outer(): pl.pallas_call(functools.partial(outer_kernel, blocks), out_shape=(jax.Sh...  1.24 us
    pallas_call x1, Pallas kernels, prep(): pl.pallas_call(prep_kernel, out_shape=(jax.ShapeDtypeStruct((M1, K1), BF)...  0.95 us
    ppermute x1, starting transfers between devices, per_device(): lax.ppermute(edge, ('aa', 'ba'), [(a * blocks + i, neighbour(a, i, blocks...  0.85 us
  transfers between devices with their start and end apart: 5, of which 3 were waited for; matrix products, arithmetic and copies ran while one was open for 0% of the time, Pallas kernels for 12%

profile of v7, /device:TPU:0, one launch (start us, length us, event | category | flops | bytes accessed | tf_op | source)
XLA Modules:
  0.0 35.7 jit_solution(1726372048753131684)
XLA Ops:
  0.0 0.0 copy-start.1
  0.0 0.0 copy-start.3
  0.0 0.0 copy-start.4
  0.0 4.1 %collective-permute-start.1 = (bf16[1,10,1024]{2,1,0:T(8,128)(2,1)}, bf16[1,10,1024]{2,1,0:T(8,128)(2,1)S(1)}, u32[]{:S(2)}, u32[]{:S(2)}) collective-permute-start(bf16[1,10,1024]{2,1,0:T(8,128)(2,1)} %s0.1), channel_id=1, source_target_pairs={{0,64},{32,96},{64,0},{96,32},{1,65},{33,97},{65,1},{97,33},{2,66}... | collective-permute-start | bytes 61448 | tf_op jit(solution)/shard_map/ppermute | solution.py:391
  4.1 0.0 collective-permute-start
  4.1 0.2 collective-permute-start.2
  4.3 0.0 copy-done.3
  4.3 0.0 copy-done.4
  4.3 0.0 copy-done.2
  4.3 1.0 %prep.1 = (bf16[640,512]{1,0:T(8,128)(2,1)S(1)}, bf16[120,1920]{1,0:T(8,128)(2,1)S(1)}) custom-call(s32[8,256]{1,0:T(8,128)S(1)} %tables.1.table_ref, bf16[3,3,3,3,16]{4,3,2,1,0:T(4,128)(2,1)S(1)} %bitcast.13, f32[1,16]{1,0:T(1,128)S(1)} %bitcast.15, bf16[3,3,3,3,16]{4,3,2,1,0:T(4,128)(2,1)S(1)} %bitcast.14), custom_call_target="tpu_custom_call" | custom-call | flops 2000000000 | bytes 6000000 | tf_op jit(solution)/shard_map/prep/pallas_call | solution.py:143
  5.9 0.2 collective-permute-done.1.s2
  6.2 0.0 collective-permute-done.s1
  6.2 3.0 %collective-permute-done.2.s3 = bf16[1,10,1024]{2,1,0:T(8,128)(2,1)S(1)} collective-permute-done((bf16[1,10,1024]{2,1,0:T(8,128)(2,1)}, bf16[1,10,1024]{2,1,0:T(8,128)(2,1)S(1)}, u32[]{:S(2)}, u32[]{:S(2)}) %collective-permute-start.2) | collective-permute-done | bytes 20512 | tf_op jit(solution)/shard_map/ppermute | solution.py:391
  9.1 0.0 copy-done.1
  9.1 0.0 copy-done
  9.1 0.8 %edges.1 = (bf16[48,1024]{1,0:T(8,128)(2,1)S(1)}, bf16[48,1024]{1,0:T(8,128)(2,1)S(1)}) custom-call(bf16[1,10,1024]{2,1,0:T(8,128)(2,1)S(1)} %copy-done.1, bf16[1,10,1024]{2,1,0:T(8,128)(2,1)S(1)} %collective-permute-done.s1, bf16[1,10,1024]{2,1,0:T(8,128)(2,1)S(1)} %collective-permute-done.1.s2, bf16[1,10,1024]{2,1,0:T(8,128)(2,1)S(1)} %collective-permute-done.2.s3, ...), custom_call_target="tpu_custom_call" | custom-call | flops 2000000000 | bytes 6000000 | tf_op jit(solution)/shard_map/edges/pallas_call | solution.py:191
  9.9 0.8 %collective-permute-start.3 = (bf16[48,1024]{1,0:T(8,128)(2,1)S(1)}, bf16[48,1024]{1,0:T(8,128)(2,1)S(1)}, u32[]{:S(2)}, u32[]{:S(2)}) collective-permute-start(bf16[48,1024]{1,0:T(8,128)(2,1)S(1)} %get-tuple-element.17.edge_ref), channel_id=1, source_target_pairs={{0,64},{1,32},{2,33},{3,34},{4,35},{5,36},{6,37},{7,38},{8,39},{9,... | collective-permute-start | bytes 294920 | tf_op jit(solution)/shard_map/ppermute | solution.py:399
  10.8 3.3 %inner.1 = (f32[2,24,512]{2,1,0:T(8,128)S(1)}, f32[20,512]{1,0:T(8,128)S(1)}, f32[2,120,512]{2,1,0:T(8,128)S(1)}, bf16[2,160,512]{2,1,0:T(8,128)(2,1)S(1)}) custom-call(bf16[48,1024]{1,0:T(8,128)(2,1)S(1)} %get-tuple-element.16.feats_ref, bf16[8,512,1024]{2,1,0:T(8,128)(2,1)S(1)} %copy-done, bf16[48,1024]{1,0:T(8,128)(2,1)S(1)} %get-tuple-element.17.edge_ref, ...), custom_call_target="tpu_custom_call" | custom-call | flops 8000000000 | bytes 24000000 | tf_op jit(solution)/shard_map/inner/pallas_call | solution.py:283
  14.1 3.1 %collective-permute-done.3.halo_ref = bf16[48,1024]{1,0:T(8,128)(2,1)S(1)} collective-permute-done((bf16[48,1024]{1,0:T(8,128)(2,1)S(1)}, bf16[48,1024]{1,0:T(8,128)(2,1)S(1)}, u32[]{:S(2)}, u32[]{:S(2)}) %collective-permute-start.3) | collective-permute-done | bytes 98336 | tf_op jit(solution)/shard_map/ppermute | solution.py:399
  17.2 1.2 %outer.1 = (f32[4,24,512]{2,1,0:T(8,128)S(1)}, f32[64,128]{1,0:T(8,128)S(1)}) custom-call(bf16[2,160,512]{2,1,0:T(8,128)(2,1)S(1)} %get-tuple-element.19.near_ref, bf16[48,1024]{1,0:T(8,128)(2,1)S(1)} %collective-permute-done.3.halo_ref, bf16[640,512]{1,0:T(8,128)(2,1)S(1)} %get-tuple-element.15.w1_ref, bf16[120,1920]{1,0:T(8,128)(2,1)S(1)} %get-tuple-element.18.w2_ref, ...), custom_call_target="tpu_custom_call" | custom-call | flops 4000000000 | bytes 12000000 | tf_op jit(solution)/shard_map/outer/pallas_call | solution.py:336
  18.4 0.1 collective-permute-start.4
  18.5 16.3 %all_to_all.11 = f32[64,1,128]{2,1,0:T(1,128)S(1)} all-to-all(f32[64,1,128]{2,1,0:T(1,128)S(1)} %bitcast.12), channel_id=1, replica_groups={{0,1,2,3,4,5,6,7,8,9,10,11,12,13,14,15,16,17,18,19,20,21,22,23,24,25,26..., dimensions={0} | all-to-all | bytes 65536 | tf_op jit(solution)/shard_map/all_to_all | solution.py:411
  34.8 0.0 collective-permute-done.4.other_ref
  34.8 0.8 %finish.1 = f32[1,10,8,512]{3,2,1,0:T(8,128)} custom-call(f32[4,24,512]{2,1,0:T(8,128)S(1)} %get-tuple-element.23.own_ref, f32[4,24,512]{2,1,0:T(8,128)S(1)} %collective-permute-done.4.other_ref, f32[64,128]{1,0:T(8,128)S(1)} %bitcast.11), custom_call_target="tpu_custom_call" | custom-call | tf_op jit(solution)/shard_map/finish/pallas_call | solution.py:372
  (3 shorter events, 0.0 us)
Async XLA Ops:
  0.0 9.1 %copy-start.1 = (bf16[1,10,1024]{2,1,0:T(8,128)(2,1)S(1)}, bf16[1,10,1024]{2,1,0:T(8,128)(2,1)}, u32[]{:S(2)}) copy-start(bf16[1,10,1024]{2,1,0:T(8,128)(2,1)} %s0.1) | copy-start | bytes 61444
  0.0 4.3 %copy-start.3 = (bf16[1,16,3,3,3,3]{1,5,4,3,2,0:T(4,128)(2,1)S(1)}, bf16[1,16,3,3,3,3]{1,5,4,3,2,0:T(4,128)(2,1)}, u32[]{:S(2)}) copy-start(bf16[1,16,3,3,3,3]{1,5,4,3,2,0:T(4,128)(2,1)} %param.10) | copy-start | bytes 7780
  0.0 4.3 %copy-start.4 = (f32[16]{0:T(128)S(1)}, f32[16]{0:T(128)}, u32[]{:S(2)}) copy-start(f32[16]{0:T(128)} %param.9) | copy-start | bytes 196
  0.0 4.3 %copy-start.2 = (bf16[16,1,3,3,3,3]{0,5,4,3,2,1:T(4,128)(2,1)S(1)}, bf16[16,1,3,3,3,3]{0,5,4,3,2,1:T(4,128)(2,1)}, u32[]{:S(2)}) copy-start(bf16[16,1,3,3,3,3]{0,5,4,3,2,1:T(4,128)(2,1)} %param.8) | copy-start | bytes 7780
  0.0 9.1 %copy-start = (bf16[8,512,1024]{2,1,0:T(8,128)(2,1)S(1)}, bf16[8,512,1024]{2,1,0:T(8,128)(2,1)}, u32[]{:S(2)}) copy-start(bf16[8,512,1024]{2,1,0:T(8,128)(2,1)} %target_ref.3) | copy-start | bytes 25165828
  0.0 6.2 %collective-permute-start.1 = (bf16[1,10,1024]{2,1,0:T(8,128)(2,1)}, bf16[1,10,1024]{2,1,0:T(8,128)(2,1)S(1)}, u32[]{:S(2)}, u32[]{:S(2)}) collective-permute-start(bf16[1,10,1024]{2,1,0:T(8,128)(2,1)} %s0.1), channel_id=1, source_target_pairs={{0,64},{32,96},{64,0},{96,32},{1,65},{33,97},{65,1},{97,33},{2,66}... | collective-permute-start | bytes 61448 | tf_op jit(solution)/shard_map/ppermute | solution.py:391
  4.1 2.1 %collective-permute-start = (bf16[1,10,1024]{2,1,0:T(8,128)(2,1)}, bf16[1,10,1024]{2,1,0:T(8,128)(2,1)S(1)}, u32[]{:S(2)}, u32[]{:S(2)}) collective-permute-start(bf16[1,10,1024]{2,1,0:T(8,128)(2,1)} %s0.1), channel_id=1, source_target_pairs={{0,32},{32,0},{64,96},{96,64},{1,33},{33,1},{65,97},{97,65},{2,34}... | collective-permute-start | bytes 61448 | tf_op jit(solution)/shard_map/ppermute | solution.py:391
  4.1 5.1 %collective-permute-start.2 = (bf16[1,10,1024]{2,1,0:T(8,128)(2,1)}, bf16[1,10,1024]{2,1,0:T(8,128)(2,1)S(1)}, u32[]{:S(2)}, u32[]{:S(2)}) collective-permute-start(bf16[1,10,1024]{2,1,0:T(8,128)(2,1)} %s0.1), channel_id=1, source_target_pairs={{0,96},{32,64},{64,32},{96,0},{1,97},{33,65},{65,33},{97,1},{2,98}... | collective-permute-start | bytes 61448 | tf_op jit(solution)/shard_map/ppermute | solution.py:391
  9.9 7.3 %collective-permute-start.3 = (bf16[48,1024]{1,0:T(8,128)(2,1)S(1)}, bf16[48,1024]{1,0:T(8,128)(2,1)S(1)}, u32[]{:S(2)}, u32[]{:S(2)}) collective-permute-start(bf16[48,1024]{1,0:T(8,128)(2,1)S(1)} %get-tuple-element.17.edge_ref), channel_id=1, source_target_pairs={{0,64},{1,32},{2,33},{3,34},{4,35},{5,36},{6,37},{7,38},{8,39},{9,... | collective-permute-start | bytes 294920 | tf_op jit(solution)/shard_map/ppermute | solution.py:399
  18.4 16.4 %collective-permute-start.4 = (f32[4,24,512]{2,1,0:T(8,128)S(1)}, f32[4,24,512]{2,1,0:T(8,128)S(1)}, u32[]{:S(2)}, u32[]{:S(2)}) collective-permute-start(f32[4,24,512]{2,1,0:T(8,128)S(1)} %get-tuple-element.23.own_ref), channel_id=1, source_target_pairs={{0,32},{32,0},{64,96},{96,64},{1,33},{33,1},{65,97},{97,65},{2,34}... | collective-permute-start | bytes 589832 | tf_op jit(solution)/shard_map/ppermute | solution.py:410

commit v8 on v7

--- a/solution.py
+++ b/solution.py
@@ -169,7 +169,7 @@
     return target_ref[jnp.where(lax.rem(lax.axis_index("aa"), 2) == 0, n, BR - 1 - n)]
 
 
-def edge_kernel(s0, s1, s2, s3, target_ref, w1_ref, feats_ref, edge_ref, stage):
+def edge_kernel(s0, s1, s3, s2, target_ref, w1_ref, feats_ref, edge_ref, stage):
     me = lax.axis_index("aa")
     given = [ref[0].astype(F32) for ref in (s0, s1, s2, s3)]
     stage[...] = jnp.zeros_like(stage)
@@ -200,7 +200,7 @@
         compiler_params=pltpu.CompilerParams(vmem_limit_bytes=VMEM_LIMIT),
         cost_estimate=cost(2.0),
         name="edges",
-    )(*sources, target, w1)
+    )(sources[0], sources[1], sources[3], sources[2], target, w1)
 
 
 def three_shifts(value):

time: 36.3 us -> 35.3 us (0.972)
  blocking collectives: 16.3 us -> 14.7 us
  waiting for transfers between devices: 6.28 us -> 7.38 us
  starting transfers between devices: 5.21 us -> 4.76 us
    all_to_all x1, blocking collectives: 16.3 us -> 14.7 us  [per_device(): lax.all_to_all(mx, ('aa', 'ba'), 0, 0, tiled=True, axis_index_groups=[[(a...]
    ppermute x3, waiting for transfers between devices: 3.18 us -> 3.89 us  [per_device(): lax.ppermute(source, 'aa', [(i, i ^ k) for i in range(size)])]
    ppermute x1, starting transfers between devices: 0.85 us -> 0.44 us  [per_device(): lax.ppermute(edge, ('aa', 'ba'), [(a * blocks + i, neighbour(a, i, blocks...]
    ppermute x1, waiting for transfers between devices: 3.1 us -> 3.49 us  [per_device(): lax.ppermute(edge, ('aa', 'ba'), [(a * blocks + i, neighbour(a, i, blocks...]
  transfers between devices with their start and end apart: 5 -> 5, of which waited for: 3 -> 2; matrix products, arithmetic and copies ran while one was open for 0% -> 0% of each run, Pallas kernels for 12% -> 12%
where the time goes in v8:
time: 35.3 us; the launch traced here: 34.7 us
  blocking collectives  14.7 us (42%)
  waiting for transfers between devices  7.38 us (21%)
  Pallas kernels  7.13 us (20%)
  starting transfers between devices  4.76 us (13%)
  between operations  0.73 us (2%)
    all_to_all x1, blocking collectives, per_device(): lax.all_to_all(mx, ('aa', 'ba'), 0, 0, tiled=True, axis_index_groups=[[(a...  14.7 us
    ppermute x3, starting transfers between devices, per_device(): lax.ppermute(source, 'aa', [(i, i ^ k) for i in range(size)])  4.24 us
    ppermute x3, waiting for transfers between devices, per_device(): lax.ppermute(source, 'aa', [(i, i ^ k) for i in range(size)])  3.89 us
    ppermute x1, waiting for transfers between devices, per_device(): lax.ppermute(edge, ('aa', 'ba'), [(a * blocks + i, neighbour(a, i, blocks...  3.49 us
    pallas_call x1, Pallas kernels, inner(): pl.pallas_call(inner_kernel, out_shape=(jax.ShapeDtypeStruct((2, PAIR, BW...  3.31 us
    pallas_call x1, Pallas kernels, outer(): pl.pallas_call(functools.partial(outer_kernel, blocks), out_shape=(jax.Sh...  1.24 us
    pallas_call x1, Pallas kernels, prep(): pl.pallas_call(prep_kernel, out_shape=(jax.ShapeDtypeStruct((M1, K1), BF)...  0.95 us
    pallas_call x1, Pallas kernels, finish(): pl.pallas_call(final_kernel, out_shape=jax.ShapeDtypeStruct((1, AW, BR, B...  0.84 us
  transfers between devices with their start and end apart: 5, of which 2 were waited for; matrix products, arithmetic and copies ran while one was open for 0% of the time, Pallas kernels for 12%

profile of v8, /device:TPU:0, one launch (start us, length us, event | category | flops | bytes accessed | tf_op | source)
XLA Modules:
  0.0 34.7 jit_solution(6446314954808727934)
XLA Ops:
  0.0 0.0 copy-start.1
  0.0 0.0 copy-start.3
  0.0 0.0 copy-start.4
  0.0 3.5 %collective-permute-start.1 = (bf16[1,10,1024]{2,1,0:T(8,128)(2,1)}, bf16[1,10,1024]{2,1,0:T(8,128)(2,1)S(1)}, u32[]{:S(2)}, u32[]{:S(2)}) collective-permute-start(bf16[1,10,1024]{2,1,0:T(8,128)(2,1)} %s0.1), channel_id=1, source_target_pairs={{0,96},{32,64},{64,32},{96,0},{1,97},{33,65},{65,33},{97,1},{2,98}... | collective-permute-start | bytes 61448 | tf_op jit(solution)/shard_map/ppermute | solution.py:391
  3.5 0.7 %collective-permute-start = (bf16[1,10,1024]{2,1,0:T(8,128)(2,1)}, bf16[1,10,1024]{2,1,0:T(8,128)(2,1)S(1)}, u32[]{:S(2)}, u32[]{:S(2)}) collective-permute-start(bf16[1,10,1024]{2,1,0:T(8,128)(2,1)} %s0.1), channel_id=1, source_target_pairs={{0,32},{32,0},{64,96},{96,64},{1,33},{33,1},{65,97},{97,65},{2,34}... | collective-permute-start | bytes 61448 | tf_op jit(solution)/shard_map/ppermute | solution.py:391
  4.2 0.1 collective-permute-start.2
  4.3 0.0 copy-done.3
  4.3 0.0 copy-done.4
  4.3 0.0 copy-done.2
  4.3 1.0 %prep.1 = (bf16[640,512]{1,0:T(8,128)(2,1)S(1)}, bf16[120,1920]{1,0:T(8,128)(2,1)S(1)}) custom-call(s32[8,256]{1,0:T(8,128)S(1)} %tables.1.table_ref, bf16[3,3,3,3,16]{4,3,2,1,0:T(4,128)(2,1)S(1)} %bitcast.13, f32[1,16]{1,0:T(1,128)S(1)} %bitcast.15, bf16[3,3,3,3,16]{4,3,2,1,0:T(4,128)(2,1)S(1)} %bitcast.14), custom_call_target="tpu_custom_call" | custom-call | flops 2000000000 | bytes 6000000 | tf_op jit(solution)/shard_map/prep/pallas_call | solution.py:143
  5.9 0.0 collective-permute-done.1.s3
  5.9 0.0 collective-permute-done.s1
  5.9 3.9 %collective-permute-done.2.s2 = bf16[1,10,1024]{2,1,0:T(8,128)(2,1)S(1)} collective-permute-done((bf16[1,10,1024]{2,1,0:T(8,128)(2,1)}, bf16[1,10,1024]{2,1,0:T(8,128)(2,1)S(1)}, u32[]{:S(2)}, u32[]{:S(2)}) %collective-permute-start.2) | collective-permute-done | bytes 20512 | tf_op jit(solution)/shard_map/ppermute | solution.py:391
  9.8 0.0 copy-done.1
  9.8 0.0 copy-done
  9.8 0.8 %edges.1 = (bf16[48,1024]{1,0:T(8,128)(2,1)S(1)}, bf16[48,1024]{1,0:T(8,128)(2,1)S(1)}) custom-call(bf16[1,10,1024]{2,1,0:T(8,128)(2,1)S(1)} %copy-done.1, bf16[1,10,1024]{2,1,0:T(8,128)(2,1)S(1)} %collective-permute-done.s1, bf16[1,10,1024]{2,1,0:T(8,128)(2,1)S(1)} %collective-permute-done.1.s3, bf16[1,10,1024]{2,1,0:T(8,128)(2,1)S(1)} %collective-permute-done.2.s2, ...), custom_call_target="tpu_custom_call" | custom-call | flops 2000000000 | bytes 6000000 | tf_op jit(solution)/shard_map/edges/pallas_call | solution.py:191
  10.6 0.4 %collective-permute-start.3 = (bf16[48,1024]{1,0:T(8,128)(2,1)S(1)}, bf16[48,1024]{1,0:T(8,128)(2,1)S(1)}, u32[]{:S(2)}, u32[]{:S(2)}) collective-permute-start(bf16[48,1024]{1,0:T(8,128)(2,1)S(1)} %get-tuple-element.17.edge_ref), channel_id=1, source_target_pairs={{0,64},{1,32},{2,33},{3,34},{4,35},{5,36},{6,37},{7,38},{8,39},{9,... | collective-permute-start | bytes 294920 | tf_op jit(solution)/shard_map/ppermute | solution.py:399
  11.0 3.3 %inner.1 = (f32[2,24,512]{2,1,0:T(8,128)S(1)}, f32[20,512]{1,0:T(8,128)S(1)}, f32[2,120,512]{2,1,0:T(8,128)S(1)}, bf16[2,160,512]{2,1,0:T(8,128)(2,1)S(1)}) custom-call(bf16[48,1024]{1,0:T(8,128)(2,1)S(1)} %get-tuple-element.16.feats_ref, bf16[8,512,1024]{2,1,0:T(8,128)(2,1)S(1)} %copy-done, bf16[48,1024]{1,0:T(8,128)(2,1)S(1)} %get-tuple-element.17.edge_ref, ...), custom_call_target="tpu_custom_call" | custom-call | flops 8000000000 | bytes 24000000 | tf_op jit(solution)/shard_map/inner/pallas_call | solution.py:283
  14.4 3.5 %collective-permute-done.3.halo_ref = bf16[48,1024]{1,0:T(8,128)(2,1)S(1)} collective-permute-done((bf16[48,1024]{1,0:T(8,128)(2,1)S(1)}, bf16[48,1024]{1,0:T(8,128)(2,1)S(1)}, u32[]{:S(2)}, u32[]{:S(2)}) %collective-permute-start.3) | collective-permute-done | bytes 98336 | tf_op jit(solution)/shard_map/ppermute | solution.py:399
  17.9 1.2 %outer.1 = (f32[4,24,512]{2,1,0:T(8,128)S(1)}, f32[64,128]{1,0:T(8,128)S(1)}) custom-call(bf16[2,160,512]{2,1,0:T(8,128)(2,1)S(1)} %get-tuple-element.19.near_ref, bf16[48,1024]{1,0:T(8,128)(2,1)S(1)} %collective-permute-done.3.halo_ref, bf16[640,512]{1,0:T(8,128)(2,1)S(1)} %get-tuple-element.15.w1_ref, bf16[120,1920]{1,0:T(8,128)(2,1)S(1)} %get-tuple-element.18.w2_ref, ...), custom_call_target="tpu_custom_call" | custom-call | flops 4000000000 | bytes 12000000 | tf_op jit(solution)/shard_map/outer/pallas_call | solution.py:336
  19.1 0.1 collective-permute-start.4
  19.2 14.7 %all_to_all.11 = f32[64,1,128]{2,1,0:T(1,128)S(1)} all-to-all(f32[64,1,128]{2,1,0:T(1,128)S(1)} %bitcast.12), channel_id=1, replica_groups={{0,1,2,3,4,5,6,7,8,9,10,11,12,13,14,15,16,17,18,19,20,21,22,23,24,25,26..., dimensions={0} | all-to-all | bytes 65536 | tf_op jit(solution)/shard_map/all_to_all | solution.py:411
  33.8 0.0 collective-permute-done.4.other_ref
  33.8 0.8 %finish.1 = f32[1,10,8,512]{3,2,1,0:T(8,128)} custom-call(f32[4,24,512]{2,1,0:T(8,128)S(1)} %get-tuple-element.23.own_ref, f32[4,24,512]{2,1,0:T(8,128)S(1)} %collective-permute-done.4.other_ref, f32[64,128]{1,0:T(8,128)S(1)} %bitcast.11), custom_call_target="tpu_custom_call" | custom-call | tf_op jit(solution)/shard_map/finish/pallas_call | solution.py:372
  (3 shorter events, 0.0 us)
Async XLA Ops:
  0.0 9.8 %copy-start.1 = (bf16[1,10,1024]{2,1,0:T(8,128)(2,1)S(1)}, bf16[1,10,1024]{2,1,0:T(8,128)(2,1)}, u32[]{:S(2)}) copy-start(bf16[1,10,1024]{2,1,0:T(8,128)(2,1)} %s0.1) | copy-start | bytes 61444
  0.0 4.3 %copy-start.3 = (bf16[1,16,3,3,3,3]{1,5,4,3,2,0:T(4,128)(2,1)S(1)}, bf16[1,16,3,3,3,3]{1,5,4,3,2,0:T(4,128)(2,1)}, u32[]{:S(2)}) copy-start(bf16[1,16,3,3,3,3]{1,5,4,3,2,0:T(4,128)(2,1)} %param.10) | copy-start | bytes 7780
  0.0 4.3 %copy-start.4 = (f32[16]{0:T(128)S(1)}, f32[16]{0:T(128)}, u32[]{:S(2)}) copy-start(f32[16]{0:T(128)} %param.9) | copy-start | bytes 196
  0.0 4.3 %copy-start.2 = (bf16[16,1,3,3,3,3]{0,5,4,3,2,1:T(4,128)(2,1)S(1)}, bf16[16,1,3,3,3,3]{0,5,4,3,2,1:T(4,128)(2,1)}, u32[]{:S(2)}) copy-start(bf16[16,1,3,3,3,3]{0,5,4,3,2,1:T(4,128)(2,1)} %param.8) | copy-start | bytes 7780
  0.0 9.8 %copy-start = (bf16[8,512,1024]{2,1,0:T(8,128)(2,1)S(1)}, bf16[8,512,1024]{2,1,0:T(8,128)(2,1)}, u32[]{:S(2)}) copy-start(bf16[8,512,1024]{2,1,0:T(8,128)(2,1)} %target_ref.3) | copy-start | bytes 25165828
  0.0 5.9 %collective-permute-start.1 = (bf16[1,10,1024]{2,1,0:T(8,128)(2,1)}, bf16[1,10,1024]{2,1,0:T(8,128)(2,1)S(1)}, u32[]{:S(2)}, u32[]{:S(2)}) collective-permute-start(bf16[1,10,1024]{2,1,0:T(8,128)(2,1)} %s0.1), channel_id=1, source_target_pairs={{0,96},{32,64},{64,32},{96,0},{1,97},{33,65},{65,33},{97,1},{2,98}... | collective-permute-start | bytes 61448 | tf_op jit(solution)/shard_map/ppermute | solution.py:391
  3.5 2.4 %collective-permute-start = (bf16[1,10,1024]{2,1,0:T(8,128)(2,1)}, bf16[1,10,1024]{2,1,0:T(8,128)(2,1)S(1)}, u32[]{:S(2)}, u32[]{:S(2)}) collective-permute-start(bf16[1,10,1024]{2,1,0:T(8,128)(2,1)} %s0.1), channel_id=1, source_target_pairs={{0,32},{32,0},{64,96},{96,64},{1,33},{33,1},{65,97},{97,65},{2,34}... | collective-permute-start | bytes 61448 | tf_op jit(solution)/shard_map/ppermute | solution.py:391
  4.2 5.6 %collective-permute-start.2 = (bf16[1,10,1024]{2,1,0:T(8,128)(2,1)}, bf16[1,10,1024]{2,1,0:T(8,128)(2,1)S(1)}, u32[]{:S(2)}, u32[]{:S(2)}) collective-permute-start(bf16[1,10,1024]{2,1,0:T(8,128)(2,1)} %s0.1), channel_id=1, source_target_pairs={{0,64},{32,96},{64,0},{96,32},{1,65},{33,97},{65,1},{97,33},{2,66}... | collective-permute-start | bytes 61448 | tf_op jit(solution)/shard_map/ppermute | solution.py:391
  10.6 7.3 %collective-permute-start.3 = (bf16[48,1024]{1,0:T(8,128)(2,1)S(1)}, bf16[48,1024]{1,0:T(8,128)(2,1)S(1)}, u32[]{:S(2)}, u32[]{:S(2)}) collective-permute-start(bf16[48,1024]{1,0:T(8,128)(2,1)S(1)} %get-tuple-element.17.edge_ref), channel_id=1, source_target_pairs={{0,64},{1,32},{2,33},{3,34},{4,35},{5,36},{6,37},{7,38},{8,39},{9,... | collective-permute-start | bytes 294920 | tf_op jit(solution)/shard_map/ppermute | solution.py:399
  19.1 14.8 %collective-permute-start.4 = (f32[4,24,512]{2,1,0:T(8,128)S(1)}, f32[4,24,512]{2,1,0:T(8,128)S(1)}, u32[]{:S(2)}, u32[]{:S(2)}) collective-permute-start(f32[4,24,512]{2,1,0:T(8,128)S(1)} %get-tuple-element.23.own_ref), channel_id=1, source_target_pairs={{0,32},{32,0},{64,96},{96,64},{1,33},{33,1},{65,97},{97,65},{2,34}... | collective-permute-start | bytes 589832 | tf_op jit(solution)/shard_map/ppermute | solution.py:410

commit v9 on v8

--- a/solution.py
+++ b/solution.py
@@ -387,14 +387,16 @@
 def per_device(source, target, first_kernel, first_bias, second_kernel, second_bias):
     blocks = lax.axis_size("ba")
     size = lax.axis_size("aa")
-    sources = [source] + [
-        lax.ppermute(source, "aa", [(i, i ^ k) for i in range(size)]) for k in range(1, size)
-    ]
+    twin = [(i, i ^ 1) for i in range(size)]
+    beside = lax.ppermute(source, "aa", twin)
+    far = lax.ppermute(source, "aa", [(i, i ^ 3) for i in range(size)])
     w1, w2 = prep(
         jnp.transpose(first_kernel[:, 0], (1, 2, 3, 4, 0)),
         first_bias[None, :],
         jnp.transpose(second_kernel[0], (1, 2, 3, 4, 0)),
     )
+    far, w1, w2 = lax.optimization_barrier((far, w1, w2))
+    sources = [source, beside, lax.ppermute(far, "aa", twin), far]
     feats, edge = edges(sources, target, w1)
     halo = lax.ppermute(
         edge,

time: 35.3 us -> 34.6 us (0.980)
  waiting for transfers between devices: 7.38 us -> 1.39 us
  starting transfers between devices: 4.76 us -> 7.59 us
  blocking collectives: 14.7 us -> 17 us
    ppermute x1, waiting for transfers between devices: 3.49 us -> 0.01 us  [per_device(): lax.ppermute(edge, ('aa', 'ba'), [(a * blocks + i, neighbour(a, i, blocks...]
    ppermute x1, starting transfers between devices: 0.44 us -> 3.27 us  [per_device(): lax.ppermute(edge, ('aa', 'ba'), [(a * blocks + i, neighbour(a, i, blocks...]
    ppermute x3, waiting for transfers between devices: 3.89 us -> 1.39 us  [the longest x1 0.91 us: per_device(): far = lax.ppermute(source, 'aa', [(i, i ^ 3) for i in range(size)])]
    all_to_all x1, blocking collectives: 14.7 us -> 17 us  [per_device(): lax.all_to_all(mx, ('aa', 'ba'), 0, 0, tiled=True, axis_index_groups=[[(a...]
  transfers between devices with their start and end apart: 5 -> 5, of which waited for: 2 -> 2; matrix products, arithmetic and copies ran while one was open for 0% -> 0% of each run, Pallas kernels for 12% -> 13%
where the time goes in v9:
time: 34.6 us; the launch traced here: 33.9 us
  blocking collectives  17 us (49%)
  starting transfers between devices  7.59 us (22%)
  Pallas kernels  7.14 us (21%)
  waiting for transfers between devices  1.39 us (4%)
  between operations  0.74 us (2%)
    all_to_all x1, blocking collectives, per_device(): lax.all_to_all(mx, ('aa', 'ba'), 0, 0, tiled=True, axis_index_groups=[[(a...  17 us
    ppermute x1, starting transfers between devices, per_device(): far = lax.ppermute(source, 'aa', [(i, i ^ 3) for i in range(size)])  4.09 us
    pallas_call x1, Pallas kernels, inner(): pl.pallas_call(inner_kernel, out_shape=(jax.ShapeDtypeStruct((2, PAIR, BW...  3.3 us
    ppermute x1, starting transfers between devices, per_device(): lax.ppermute(edge, ('aa', 'ba'), [(a * blocks + i, neighbour(a, i, blocks...  3.27 us
    pallas_call x1, Pallas kernels, outer(): pl.pallas_call(functools.partial(outer_kernel, blocks), out_shape=(jax.Sh...  1.25 us
    pallas_call x1, Pallas kernels, prep(): pl.pallas_call(prep_kernel, out_shape=(jax.ShapeDtypeStruct((M1, K1), BF)...  0.95 us
    ppermute x1, waiting for transfers between devices, per_device(): far = lax.ppermute(source, 'aa', [(i, i ^ 3) for i in range(size)])  0.91 us
    pallas_call x1, Pallas kernels, finish(): pl.pallas_call(final_kernel, out_shape=jax.ShapeDtypeStruct((1, AW, BR, B...  0.84 us
  transfers between devices with their start and end apart: 5, of which 2 were waited for; matrix products, arithmetic and copies ran while one was open for 0% of the time, Pallas kernels for 13%

profile of v9, /device:TPU:0, one launch (start us, length us, event | category | flops | bytes accessed | tf_op | source)
XLA Modules:
  0.0 33.9 jit_solution(1469575357692233870)
XLA Ops:
  0.0 0.0 copy-start.1
  0.0 0.0 copy-start.3
  0.0 0.0 copy-start.4
  0.0 0.1 collective-permute-start
  0.1 4.1 %collective-permute-start.1 = (bf16[1,10,1024]{2,1,0:T(8,128)(2,1)}, bf16[1,10,1024]{2,1,0:T(8,128)(2,1)S(1)}, u32[]{:S(2)}, u32[]{:S(2)}) collective-permute-start(bf16[1,10,1024]{2,1,0:T(8,128)(2,1)} %s0.1), channel_id=1, source_target_pairs={{0,96},{32,64},{64,32},{96,0},{1,97},{33,65},{65,33},{97,1},{2,98}... | collective-permute-start | bytes 61448 | tf_op jit(solution)/shard_map/ppermute | solution.py:392
  4.2 0.0 copy-done.3
  4.2 0.0 copy-done.4
  4.2 0.0 copy-done.2
  4.2 1.0 %prep.1 = (bf16[640,512]{1,0:T(8,128)(2,1)S(1)}, bf16[120,1920]{1,0:T(8,128)(2,1)S(1)}) custom-call(s32[8,256]{1,0:T(8,128)S(1)} %tables.1.table_ref, bf16[3,3,3,3,16]{4,3,2,1,0:T(4,128)(2,1)S(1)} %bitcast.13, f32[1,16]{1,0:T(1,128)S(1)} %bitcast.15, bf16[3,3,3,3,16]{4,3,2,1,0:T(4,128)(2,1)S(1)} %bitcast.14), custom_call_target="tpu_custom_call" | custom-call | flops 2000000000 | bytes 6000000 | tf_op jit(solution)/shard_map/prep/pallas_call | solution.py:143
  5.2 0.9 %collective-permute-done.1.s3 = bf16[1,10,1024]{2,1,0:T(8,128)(2,1)S(1)} collective-permute-done((bf16[1,10,1024]{2,1,0:T(8,128)(2,1)}, bf16[1,10,1024]{2,1,0:T(8,128)(2,1)S(1)}, u32[]{:S(2)}, u32[]{:S(2)}) %collective-permute-start.1) | collective-permute-done | bytes 20512 | tf_op jit(solution)/shard_map/ppermute | solution.py:392
  6.1 0.1 collective-permute-start.2
  6.8 0.0 collective-permute-done.s1
  6.8 0.5 %collective-permute-done.2.s2 = bf16[1,10,1024]{2,1,0:T(8,128)(2,1)S(1)} collective-permute-done((bf16[1,10,1024]{2,1,0:T(8,128)(2,1)S(1)}, bf16[1,10,1024]{2,1,0:T(8,128)(2,1)S(1)}, u32[]{:S(2)}, u32[]{:S(2)}) %collective-permute-start.2) | collective-permute-done | bytes 20512 | tf_op jit(solution)/shard_map/ppermute | solution.py:399
  7.3 0.0 copy-done.1
  7.3 0.0 copy-done
  7.3 0.8 %edges.1 = (bf16[48,1024]{1,0:T(8,128)(2,1)S(1)}, bf16[48,1024]{1,0:T(8,128)(2,1)S(1)}) custom-call(bf16[1,10,1024]{2,1,0:T(8,128)(2,1)S(1)} %copy-done.1, bf16[1,10,1024]{2,1,0:T(8,128)(2,1)S(1)} %collective-permute-done.s1, bf16[1,10,1024]{2,1,0:T(8,128)(2,1)S(1)} %collective-permute-done.1.s3, bf16[1,10,1024]{2,1,0:T(8,128)(2,1)S(1)} %collective-permute-done.2.s2, ...), custom_call_target="tpu_custom_call" | custom-call | flops 2000000000 | bytes 6000000 | tf_op jit(solution)/shard_map/edges/pallas_call | solution.py:191
  8.1 3.3 %collective-permute-start.3 = (bf16[48,1024]{1,0:T(8,128)(2,1)S(1)}, bf16[48,1024]{1,0:T(8,128)(2,1)S(1)}, u32[]{:S(2)}, u32[]{:S(2)}) collective-permute-start(bf16[48,1024]{1,0:T(8,128)(2,1)S(1)} %get-tuple-element.23.edge_ref), channel_id=1, source_target_pairs={{0,64},{1,32},{2,33},{3,34},{4,35},{5,36},{6,37},{7,38},{8,39},{9,... | collective-permute-start | bytes 294920 | tf_op jit(solution)/shard_map/ppermute | solution.py:401
  11.4 3.3 %inner.1 = (f32[2,24,512]{2,1,0:T(8,128)S(1)}, f32[20,512]{1,0:T(8,128)S(1)}, f32[2,120,512]{2,1,0:T(8,128)S(1)}, bf16[2,160,512]{2,1,0:T(8,128)(2,1)S(1)}) custom-call(bf16[48,1024]{1,0:T(8,128)(2,1)S(1)} %get-tuple-element.22.feats_ref, bf16[8,512,1024]{2,1,0:T(8,128)(2,1)S(1)} %copy-done, bf16[48,1024]{1,0:T(8,128)(2,1)S(1)} %get-tuple-element.23.edge_ref, ...), custom_call_target="tpu_custom_call" | custom-call | flops 8000000000 | bytes 24000000 | tf_op jit(solution)/shard_map/inner/pallas_call | solution.py:283
  14.7 0.0 collective-permute-done.3.halo_ref
  14.7 1.3 %outer.1 = (f32[4,24,512]{2,1,0:T(8,128)S(1)}, f32[64,128]{1,0:T(8,128)S(1)}) custom-call(bf16[2,160,512]{2,1,0:T(8,128)(2,1)S(1)} %get-tuple-element.25.near_ref, bf16[48,1024]{1,0:T(8,128)(2,1)S(1)} %collective-permute-done.3.halo_ref, bf16[640,512]{1,0:T(8,128)(2,1)S(1)} %get-tuple-element.21.w1_ref, bf16[120,1920]{1,0:T(8,128)(2,1)S(1)} %get-tuple-element.24.w2_ref, ...), custom_call_target="tpu_custom_call" | custom-call | flops 4000000000 | bytes 12000000 | tf_op jit(solution)/shard_map/outer/pallas_call | solution.py:336
  16.0 0.1 collective-permute-start.4
  16.0 17.0 %all_to_all.11 = f32[64,1,128]{2,1,0:T(1,128)S(1)} all-to-all(f32[64,1,128]{2,1,0:T(1,128)S(1)} %bitcast.12), channel_id=1, replica_groups={{0,1,2,3,4,5,6,7,8,9,10,11,12,13,14,15,16,17,18,19,20,21,22,23,24,25,26..., dimensions={0} | all-to-all | bytes 65536 | tf_op jit(solution)/shard_map/all_to_all | solution.py:413
  33.1 0.0 collective-permute-done.4.other_ref
  33.1 0.8 %finish.1 = f32[1,10,8,512]{3,2,1,0:T(8,128)} custom-call(f32[4,24,512]{2,1,0:T(8,128)S(1)} %get-tuple-element.29.own_ref, f32[4,24,512]{2,1,0:T(8,128)S(1)} %collective-permute-done.4.other_ref, f32[64,128]{1,0:T(8,128)S(1)} %bitcast.11), custom_call_target="tpu_custom_call" | custom-call | tf_op jit(solution)/shard_map/finish/pallas_call | solution.py:372
  (3 shorter events, 0.0 us)
Async XLA Ops:
  0.0 7.3 %copy-start.1 = (bf16[1,10,1024]{2,1,0:T(8,128)(2,1)S(1)}, bf16[1,10,1024]{2,1,0:T(8,128)(2,1)}, u32[]{:S(2)}) copy-start(bf16[1,10,1024]{2,1,0:T(8,128)(2,1)} %s0.1) | copy-start | bytes 61444
  0.0 4.2 %copy-start.3 = (bf16[1,16,3,3,3,3]{1,5,4,3,2,0:T(4,128)(2,1)S(1)}, bf16[1,16,3,3,3,3]{1,5,4,3,2,0:T(4,128)(2,1)}, u32[]{:S(2)}) copy-start(bf16[1,16,3,3,3,3]{1,5,4,3,2,0:T(4,128)(2,1)} %param.10) | copy-start | bytes 7780
  0.0 4.2 %copy-start.4 = (f32[16]{0:T(128)S(1)}, f32[16]{0:T(128)}, u32[]{:S(2)}) copy-start(f32[16]{0:T(128)} %param.9) | copy-start | bytes 196
  0.0 4.2 %copy-start.2 = (bf16[16,1,3,3,3,3]{0,5,4,3,2,1:T(4,128)(2,1)S(1)}, bf16[16,1,3,3,3,3]{0,5,4,3,2,1:T(4,128)(2,1)}, u32[]{:S(2)}) copy-start(bf16[16,1,3,3,3,3]{0,5,4,3,2,1:T(4,128)(2,1)} %param.8) | copy-start | bytes 7780
  0.0 7.3 %copy-start = (bf16[8,512,1024]{2,1,0:T(8,128)(2,1)S(1)}, bf16[8,512,1024]{2,1,0:T(8,128)(2,1)}, u32[]{:S(2)}) copy-start(bf16[8,512,1024]{2,1,0:T(8,128)(2,1)} %target_ref.3) | copy-start | bytes 25165828
  0.0 6.8 %collective-permute-start = (bf16[1,10,1024]{2,1,0:T(8,128)(2,1)}, bf16[1,10,1024]{2,1,0:T(8,128)(2,1)S(1)}, u32[]{:S(2)}, u32[]{:S(2)}) collective-permute-start(bf16[1,10,1024]{2,1,0:T(8,128)(2,1)} %s0.1), channel_id=1, source_target_pairs={{0,32},{32,0},{64,96},{96,64},{1,33},{33,1},{65,97},{97,65},{2,34}... | collective-permute-start | bytes 61448 | tf_op jit(solution)/shard_map/ppermute | solution.py:391
  0.1 6.0 %collective-permute-start.1 = (bf16[1,10,1024]{2,1,0:T(8,128)(2,1)}, bf16[1,10,1024]{2,1,0:T(8,128)(2,1)S(1)}, u32[]{:S(2)}, u32[]{:S(2)}) collective-permute-start(bf16[1,10,1024]{2,1,0:T(8,128)(2,1)} %s0.1), channel_id=1, source_target_pairs={{0,96},{32,64},{64,32},{96,0},{1,97},{33,65},{65,33},{97,1},{2,98}... | collective-permute-start | bytes 61448 | tf_op jit(solution)/shard_map/ppermute | solution.py:392
  6.1 1.2 %collective-permute-start.2 = (bf16[1,10,1024]{2,1,0:T(8,128)(2,1)S(1)}, bf16[1,10,1024]{2,1,0:T(8,128)(2,1)S(1)}, u32[]{:S(2)}, u32[]{:S(2)}) collective-permute-start(bf16[1,10,1024]{2,1,0:T(8,128)(2,1)S(1)} %collective-permute-done.1.s3), channel_id=1, source_target_pairs={{0,32},{32,0},{64,96},{96,64},{1,33},{33,1},{65,97},{97,65},{2,34}... | collective-permute-start | bytes 61448 | tf_op jit(solution)/shard_map/ppermute | solution.py:399
  8.1 6.6 %collective-permute-start.3 = (bf16[48,1024]{1,0:T(8,128)(2,1)S(1)}, bf16[48,1024]{1,0:T(8,128)(2,1)S(1)}, u32[]{:S(2)}, u32[]{:S(2)}) collective-permute-start(bf16[48,1024]{1,0:T(8,128)(2,1)S(1)} %get-tuple-element.23.edge_ref), channel_id=1, source_target_pairs={{0,64},{1,32},{2,33},{3,34},{4,35},{5,36},{6,37},{7,38},{8,39},{9,... | collective-permute-start | bytes 294920 | tf_op jit(solution)/shard_map/ppermute | solution.py:401
  16.0 17.1 %collective-permute-start.4 = (f32[4,24,512]{2,1,0:T(8,128)S(1)}, f32[4,24,512]{2,1,0:T(8,128)S(1)}, u32[]{:S(2)}, u32[]{:S(2)}) collective-permute-start(f32[4,24,512]{2,1,0:T(8,128)S(1)} %get-tuple-element.29.own_ref), channel_id=1, source_target_pairs={{0,32},{32,0},{64,96},{96,64},{1,33},{33,1},{65,97},{97,65},{2,34}... | collective-permute-start | bytes 589832 | tf_op jit(solution)/shard_map/ppermute | solution.py:412

commit v10 on v9

--- a/solution.py
+++ b/solution.py
@@ -354,6 +354,7 @@
     row_id = lax.broadcasted_iota(jnp.int32, (AW, 128), 0)
     lane = lax.broadcasted_iota(jnp.int32, (AW, 128), 1)
     cell = jnp.sum(jnp.where(row_id == lane, top, 0.0), axis=1, keepdims=True) + EPS
+    share = 1.0 / cell
     for p in range(BR):
         n = min(p, BR - 1 - p)
         here = upper if p < OWN else jnp.logical_not(upper)
@@ -362,7 +363,7 @@
         best = jnp.where(
             here, own_ref[n, best[0] : best[1], :], other_ref[n, best[0] : best[1], :]
         )
-        value = s * (s / (best + EPS)) * (s / cell)
+        value = s * (s * (1.0 / (best + EPS))) * (s * share)
         for j in range(AW):
             out_ref[0, j, p : p + 1, :] = value[j : j + 1, :]
 
@@ -417,7 +418,7 @@
         0,
         tiled=True,
         axis_index_groups=[
-            [(a + c) * blocks + i for c in range(2) for i in range(blocks)]
+            [(a + c) * blocks + i for c in range(2) for i in reversed(range(blocks))]
             for a in range(0, size, 2)
         ],
     )

time: 34.6 us -> 31.3 us (0.905)
  the two profiles are of different devices: /device:TPU:0 before, /device:TPU:1 now
where the time goes in v10:
time: 31.3 us; the launch traced here: 31.2 us
  blocking collectives  12.9 us (41%)
  starting transfers between devices  9.29 us (30%)
  Pallas kernels  7.14 us (23%)
  waiting for transfers between devices  1.1 us (4%)
  between operations  0.74 us (2%)
    all_to_all x1, blocking collectives, per_device(): lax.all_to_all(mx, ('aa', 'ba'), 0, 0, tiled=True, axis_index_groups=[[(a...  12.9 us
    ppermute x1, starting transfers between devices, per_device(): far = lax.ppermute(source, 'aa', [(i, i ^ 3) for i in range(size)])  3.67 us
    pallas_call x1, Pallas kernels, inner(): pl.pallas_call(inner_kernel, out_shape=(jax.ShapeDtypeStruct((2, PAIR, BW...  3.31 us
    ppermute x1, starting transfers between devices, per_device(): other = lax.ppermute(own, 'aa', [(i, i ^ 1) for i in range(size)])  2.17 us
    ppermute x1, starting transfers between devices, per_device(): lax.ppermute(edge, ('aa', 'ba'), [(a * blocks + i, neighbour(a, i, blocks...  1.52 us
    ppermute x1, starting transfers between devices, per_device(): beside = lax.ppermute(source, 'aa', twin)  1.49 us
    pallas_call x1, Pallas kernels, outer(): pl.pallas_call(functools.partial(outer_kernel, blocks), out_shape=(jax.Sh...  1.25 us
    pallas_call x1, Pallas kernels, prep(): pl.pallas_call(prep_kernel, out_shape=(jax.ShapeDtypeStruct((M1, K1), BF)...  0.95 us
  transfers between devices with their start and end apart: 5, of which 2 were waited for; matrix products, arithmetic and copies ran while one was open for 0% of the time, Pallas kernels for 14%

profile of v10, /device:TPU:1, one launch (start us, length us, event | category | flops | bytes accessed | tf_op | source)
XLA Modules:
  0.0 31.2 jit_solution(4676443558876432920)
XLA Ops:
  0.0 0.0 copy-start.1
  0.0 0.0 copy-start.2
  0.0 0.0 copy-start
  0.0 1.5 %collective-permute-start = (bf16[1,10,1024]{2,1,0:T(8,128)(2,1)}, bf16[1,10,1024]{2,1,0:T(8,128)(2,1)S(1)}, u32[]{:S(2)}, u32[]{:S(2)}) collective-permute-start(bf16[1,10,1024]{2,1,0:T(8,128)(2,1)} %s0.1), channel_id=1, source_target_pairs={{0,32},{32,0},{64,96},{96,64},{1,33},{33,1},{65,97},{97,65},{2,34}... | collective-permute-start | bytes 61448 | tf_op jit(solution)/shard_map/ppermute | solution.py:392
  1.5 3.7 %collective-permute-start.1 = (bf16[1,10,1024]{2,1,0:T(8,128)(2,1)}, bf16[1,10,1024]{2,1,0:T(8,128)(2,1)S(1)}, u32[]{:S(2)}, u32[]{:S(2)}) collective-permute-start(bf16[1,10,1024]{2,1,0:T(8,128)(2,1)} %s0.1), channel_id=1, source_target_pairs={{0,96},{32,64},{64,32},{96,0},{1,97},{33,65},{65,33},{97,1},{2,98}... | collective-permute-start | bytes 61448 | tf_op jit(solution)/shard_map/ppermute | solution.py:393
  5.2 0.0 copy-done.3
  5.2 0.0 copy-done.4
  5.2 0.0 copy-done.2
  5.2 1.0 %prep.1 = (bf16[640,512]{1,0:T(8,128)(2,1)S(1)}, bf16[120,1920]{1,0:T(8,128)(2,1)S(1)}) custom-call(s32[8,256]{1,0:T(8,128)S(1)} %tables.1.table_ref, bf16[3,3,3,3,16]{4,3,2,1,0:T(4,128)(2,1)S(1)} %bitcast.13, f32[1,16]{1,0:T(1,128)S(1)} %bitcast.15, bf16[3,3,3,3,16]{4,3,2,1,0:T(4,128)(2,1)S(1)} %bitcast.14), custom_call_target="tpu_custom_call" | custom-call | flops 2000000000 | bytes 6000000 | tf_op jit(solution)/shard_map/prep/pallas_call | solution.py:143
  6.2 0.9 %collective-permute-done.1.s3 = bf16[1,10,1024]{2,1,0:T(8,128)(2,1)S(1)} collective-permute-done((bf16[1,10,1024]{2,1,0:T(8,128)(2,1)}, bf16[1,10,1024]{2,1,0:T(8,128)(2,1)S(1)}, u32[]{:S(2)}, u32[]{:S(2)}) %collective-permute-start.1) | collective-permute-done | bytes 20512 | tf_op jit(solution)/shard_map/ppermute | solution.py:393
  7.1 0.4 %collective-permute-start.2 = (bf16[1,10,1024]{2,1,0:T(8,128)(2,1)S(1)}, bf16[1,10,1024]{2,1,0:T(8,128)(2,1)S(1)}, u32[]{:S(2)}, u32[]{:S(2)}) collective-permute-start(bf16[1,10,1024]{2,1,0:T(8,128)(2,1)S(1)} %collective-permute-done.1.s3), channel_id=1, source_target_pairs={{0,32},{32,0},{64,96},{96,64},{1,33},{33,1},{65,97},{97,65},{2,34}... | collective-permute-start | bytes 61448 | tf_op jit(solution)/shard_map/ppermute | solution.py:400
  8.2 0.0 collective-permute-done.s1
  8.2 0.2 collective-permute-done.2.s2
  8.4 0.0 copy-done.1
  8.4 0.0 copy-done
  8.4 0.8 %edges.1 = (bf16[48,1024]{1,0:T(8,128)(2,1)S(1)}, bf16[48,1024]{1,0:T(8,128)(2,1)S(1)}) custom-call(bf16[1,10,1024]{2,1,0:T(8,128)(2,1)S(1)} %copy-done.1, bf16[1,10,1024]{2,1,0:T(8,128)(2,1)S(1)} %collective-permute-done.s1, bf16[1,10,1024]{2,1,0:T(8,128)(2,1)S(1)} %collective-permute-done.1.s3, bf16[1,10,1024]{2,1,0:T(8,128)(2,1)S(1)} %collective-permute-done.2.s2, ...), custom_call_target="tpu_custom_call" | custom-call | flops 2000000000 | bytes 6000000 | tf_op jit(solution)/shard_map/edges/pallas_call | solution.py:191
  9.2 1.5 %collective-permute-start.3 = (bf16[48,1024]{1,0:T(8,128)(2,1)S(1)}, bf16[48,1024]{1,0:T(8,128)(2,1)S(1)}, u32[]{:S(2)}, u32[]{:S(2)}) collective-permute-start(bf16[48,1024]{1,0:T(8,128)(2,1)S(1)} %get-tuple-element.23.edge_ref), channel_id=1, source_target_pairs={{0,64},{1,32},{2,33},{3,34},{4,35},{5,36},{6,37},{7,38},{8,39},{9,... | collective-permute-start | bytes 294920 | tf_op jit(solution)/shard_map/ppermute | solution.py:402
  10.7 3.3 %inner.1 = (f32[2,24,512]{2,1,0:T(8,128)S(1)}, f32[20,512]{1,0:T(8,128)S(1)}, f32[2,120,512]{2,1,0:T(8,128)S(1)}, bf16[2,160,512]{2,1,0:T(8,128)(2,1)S(1)}) custom-call(bf16[48,1024]{1,0:T(8,128)(2,1)S(1)} %get-tuple-element.22.feats_ref, bf16[8,512,1024]{2,1,0:T(8,128)(2,1)S(1)} %copy-done, bf16[48,1024]{1,0:T(8,128)(2,1)S(1)} %get-tuple-element.23.edge_ref, ...), custom_call_target="tpu_custom_call" | custom-call | flops 8000000000 | bytes 24000000 | tf_op jit(solution)/shard_map/inner/pallas_call | solution.py:283
  14.0 0.0 collective-permute-done.3.halo_ref
  14.0 1.3 %outer.1 = (f32[4,24,512]{2,1,0:T(8,128)S(1)}, f32[64,128]{1,0:T(8,128)S(1)}) custom-call(bf16[2,160,512]{2,1,0:T(8,128)(2,1)S(1)} %get-tuple-element.25.near_ref, bf16[48,1024]{1,0:T(8,128)(2,1)S(1)} %collective-permute-done.3.halo_ref, bf16[640,512]{1,0:T(8,128)(2,1)S(1)} %get-tuple-element.21.w1_ref, bf16[120,1920]{1,0:T(8,128)(2,1)S(1)} %get-tuple-element.24.w2_ref, ...), custom_call_target="tpu_custom_call" | custom-call | flops 4000000000 | bytes 12000000 | tf_op jit(solution)/shard_map/outer/pallas_call | solution.py:336
  15.3 2.2 %collective-permute-start.4 = (f32[4,24,512]{2,1,0:T(8,128)S(1)}, f32[4,24,512]{2,1,0:T(8,128)S(1)}, u32[]{:S(2)}, u32[]{:S(2)}) collective-permute-start(f32[4,24,512]{2,1,0:T(8,128)S(1)} %get-tuple-element.29.own_ref), channel_id=1, source_target_pairs={{0,32},{32,0},{64,96},{96,64},{1,33},{33,1},{65,97},{97,65},{2,34}... | collective-permute-start | bytes 589832 | tf_op jit(solution)/shard_map/ppermute | solution.py:413
  17.4 12.9 %all_to_all.11 = f32[64,1,128]{2,1,0:T(1,128)S(1)} all-to-all(f32[64,1,128]{2,1,0:T(1,128)S(1)} %bitcast.12), channel_id=1, replica_groups={{31,30,29,28,27,26,25,24,23,22,21,20,19,18,17,16,15,14,13,12,11,10,9,8,..., dimensions={0} | all-to-all | bytes 65536 | tf_op jit(solution)/shard_map/all_to_all | solution.py:414
  30.3 0.0 collective-permute-done.4.other_ref
  30.3 0.8 %finish.1 = f32[1,10,8,512]{3,2,1,0:T(8,128)} custom-call(f32[4,24,512]{2,1,0:T(8,128)S(1)} %get-tuple-element.29.own_ref, f32[4,24,512]{2,1,0:T(8,128)S(1)} %collective-permute-done.4.other_ref, f32[64,128]{1,0:T(8,128)S(1)} %bitcast.11), custom_call_target="tpu_custom_call" | custom-call | tf_op jit(solution)/shard_map/finish/pallas_call | solution.py:373
  (3 shorter events, 0.0 us)
Async XLA Ops:
  0.0 8.4 %copy-start.1 = (bf16[1,10,1024]{2,1,0:T(8,128)(2,1)S(1)}, bf16[1,10,1024]{2,1,0:T(8,128)(2,1)}, u32[]{:S(2)}) copy-start(bf16[1,10,1024]{2,1,0:T(8,128)(2,1)} %s0.1) | copy-start | bytes 61444
  0.0 5.2 %copy-start.3 = (bf16[1,16,3,3,3,3]{1,5,4,3,2,0:T(4,128)(2,1)S(1)}, bf16[1,16,3,3,3,3]{1,5,4,3,2,0:T(4,128)(2,1)}, u32[]{:S(2)}) copy-start(bf16[1,16,3,3,3,3]{1,5,4,3,2,0:T(4,128)(2,1)} %param.10) | copy-start | bytes 7780
  0.0 5.2 %copy-start.4 = (f32[16]{0:T(128)S(1)}, f32[16]{0:T(128)}, u32[]{:S(2)}) copy-start(f32[16]{0:T(128)} %param.9) | copy-start | bytes 196
  0.0 5.2 %copy-start.2 = (bf16[16,1,3,3,3,3]{0,5,4,3,2,1:T(4,128)(2,1)S(1)}, bf16[16,1,3,3,3,3]{0,5,4,3,2,1:T(4,128)(2,1)}, u32[]{:S(2)}) copy-start(bf16[16,1,3,3,3,3]{0,5,4,3,2,1:T(4,128)(2,1)} %param.8) | copy-start | bytes 7780
  0.0 8.4 %copy-start = (bf16[8,512,1024]{2,1,0:T(8,128)(2,1)S(1)}, bf16[8,512,1024]{2,1,0:T(8,128)(2,1)}, u32[]{:S(2)}) copy-start(bf16[8,512,1024]{2,1,0:T(8,128)(2,1)} %target_ref.3) | copy-start | bytes 25165828
  0.0 8.2 %collective-permute-start = (bf16[1,10,1024]{2,1,0:T(8,128)(2,1)}, bf16[1,10,1024]{2,1,0:T(8,128)(2,1)S(1)}, u32[]{:S(2)}, u32[]{:S(2)}) collective-permute-start(bf16[1,10,1024]{2,1,0:T(8,128)(2,1)} %s0.1), channel_id=1, source_target_pairs={{0,32},{32,0},{64,96},{96,64},{1,33},{33,1},{65,97},{97,65},{2,34}... | collective-permute-start | bytes 61448 | tf_op jit(solution)/shard_map/ppermute | solution.py:392
  1.5 5.6 %collective-permute-start.1 = (bf16[1,10,1024]{2,1,0:T(8,128)(2,1)}, bf16[1,10,1024]{2,1,0:T(8,128)(2,1)S(1)}, u32[]{:S(2)}, u32[]{:S(2)}) collective-permute-start(bf16[1,10,1024]{2,1,0:T(8,128)(2,1)} %s0.1), channel_id=1, source_target_pairs={{0,96},{32,64},{64,32},{96,0},{1,97},{33,65},{65,33},{97,1},{2,98}... | collective-permute-start | bytes 61448 | tf_op jit(solution)/shard_map/ppermute | solution.py:393
  7.1 1.3 %collective-permute-start.2 = (bf16[1,10,1024]{2,1,0:T(8,128)(2,1)S(1)}, bf16[1,10,1024]{2,1,0:T(8,128)(2,1)S(1)}, u32[]{:S(2)}, u32[]{:S(2)}) collective-permute-start(bf16[1,10,1024]{2,1,0:T(8,128)(2,1)S(1)} %collective-permute-done.1.s3), channel_id=1, source_target_pairs={{0,32},{32,0},{64,96},{96,64},{1,33},{33,1},{65,97},{97,65},{2,34}... | collective-permute-start | bytes 61448 | tf_op jit(solution)/shard_map/ppermute | solution.py:400
  9.2 4.8 %collective-permute-start.3 = (bf16[48,1024]{1,0:T(8,128)(2,1)S(1)}, bf16[48,1024]{1,0:T(8,128)(2,1)S(1)}, u32[]{:S(2)}, u32[]{:S(2)}) collective-permute-start(bf16[48,1024]{1,0:T(8,128)(2,1)S(1)} %get-tuple-element.23.edge_ref), channel_id=1, source_target_pairs={{0,64},{1,32},{2,33},{3,34},{4,35},{5,36},{6,37},{7,38},{8,39},{9,... | collective-permute-start | bytes 294920 | tf_op jit(solution)/shard_map/ppermute | solution.py:402
  15.3 15.0 %collective-permute-start.4 = (f32[4,24,512]{2,1,0:T(8,128)S(1)}, f32[4,24,512]{2,1,0:T(8,128)S(1)}, u32[]{:S(2)}, u32[]{:S(2)}) collective-permute-start(f32[4,24,512]{2,1,0:T(8,128)S(1)} %get-tuple-element.29.own_ref), channel_id=1, source_target_pairs={{0,32},{32,0},{64,96},{96,64},{1,33},{33,1},{65,97},{97,65},{2,34}... | collective-permute-start | bytes 589832 | tf_op jit(solution)/shard_map/ppermute | solution.py:413
